TPU v7x, 256 devices: a whole 4x4x8 slice. The times are simulated.
256 devices in a mesh: section: 16 (over x, y), expert: 16 (over z, core).
Axes of the slice: x: 4, y: 4, z: 8, core: 2. Of those that a mesh axis runs over, the one named last changes fastest.
Arguments:
- tokens: bfloat16 [16, 256, 7168], P('section', 'expert'), may hold values from -6 to 6
- norm_gain: float32 [16, 7168], P('section'), may hold values from 0.1 to 1.9
- gate_weight: bfloat16 [16, 7168, 4096], P('section', None, 'expert'), may hold values from -0.0625 to 0.0625
- up_weight: bfloat16 [16, 7168, 4096], P('section', None, 'expert'), may hold values from -0.0625 to 0.0625
- down_weight: bfloat16 [16, 4096, 7168], P('section', 'expert'), may hold values from -0.1875 to 0.1875
- block_scales: int32 [16, 3, 56, 32], P('section', None, None, 'expert'), may hold values from -1 to 1
- routes: int32 [16, 2, 256, 2], P('section', None, 'expert'), may hold values from 0 to 3, all different within a row; in each aligned block of 16 rows (0 to 15, 16 to 31, ..., all dimensions but the last counted through in order) at most 12 rows name the same one
- route_weights: bfloat16 [16, 2, 256, 2], P('section', None, 'expert'), may hold values from 0.19921875 to 1
Outputs:
- final: bfloat16 [16, 256, 7168], P('section', 'expert')
Inputs may be any that keep to these rules, and one draw needn't show every extreme that they name: `routes`: each token names 2 different experts. For each section and step, the 16 tokens of one device name no expert more than 12 times.
All inputs are finite; a program needn't handle non-finite values.
Results may differ from a plain program's by a relative error of at most 0.025.
Values may be sent and summed in bfloat16 or wider, within the bound.
No kernel may reach another device: no remote copies, remote signals or barrier semaphores. Data moves between devices by JAX's collectives and lax.ppermute only.
A program may use at most 128 MiB of HBM per device.

v0:
```python
import jax
import jax.numpy as jnp
from jax import lax
from jax.experimental import pallas as pl
from jax.experimental.pallas import tpu as pltpu
from jax.sharding import PartitionSpec as P

SPLIT = 4
TICKS = 2
LANES = 128
VMEM_LIMIT = 16 * 1024 * 1024
AHEAD = 4
F32 = jnp.float32
BF16 = jnp.bfloat16


def along_z(shard, by):
    length = lax.axis_size("expert")
    return lax.ppermute(
        shard, "expert", [(i, (i + 2 * by) % length) for i in range(length)]
    )


def other_core(shard):
    length = lax.axis_size("expert")
    return lax.ppermute(shard, "expert", [(i, i ^ 1) for i in range(length)])


def to_next_section(shard, by):
    sections, length = lax.axis_size("section"), lax.axis_size("expert")
    pairs = [
        (s * length + e, (s + 1) % sections * length + (e + 2 * by) % length)
        for s in range(sections)
        for e in range(length)
    ]
    return lax.ppermute(shard, ("section", "expert"), pairs)


def cut_of(width):
    return width // LANES // 2 * LANES


def gather_first(block):
    far_back, far_ahead = along_z(block, 2), along_z(block, -2)
    return [block, along_z(block, 1), along_z(block, -1), far_back, far_ahead]


def gather_second(first):
    far_back, far_ahead = first[3], first[4]
    cut = cut_of(far_back.shape[1])
    return first + [
        along_z(far_back, 1),
        along_z(far_ahead, -1),
        along_z(far_back[:, :cut], 2),
        along_z(far_ahead[:, cut:], -2),
    ]


def sum_to_next(state, outs):
    far = [
        along_z(outs[7], -2),
        along_z(outs[8], 2),
        along_z(outs[5], -1),
        along_z(outs[6], 1),
    ]
    far[0], last = lax.optimization_barrier((far[0], outs[2]))
    near = [along_z(outs[1], -1), along_z(last, 1)]
    back, ahead = join_far(outs[3], outs[4], *far)
    parts = [to_next_section(back, -2), to_next_section(ahead, 2)]
    parts.append(to_next_section(join_near(state, outs[0], *near), 0))
    return sum(part.astype(F32) for part in parts).astype(BF16)


def join_call(kernel, name, n_out, *operands):
    rows, width = operands[0].shape
    return pl.pallas_call(
        kernel,
        out_shape=[jax.ShapeDtypeStruct((rows, width), BF16)] * n_out,
        compiler_params=pltpu.CompilerParams(vmem_limit_bytes=VMEM_LIMIT),
        cost_estimate=pl.CostEstimate(
            flops=4 * rows * width, bytes_accessed=12 * rows * width, transcendentals=0
        ),
        name=name,
    )(*operands)


def join_far(back, ahead, left, right, back_3, ahead_3):
    width = back.shape[1]
    cut = cut_of(width)

    def kernel(back, ahead, left, right, b3, a3, back_out, ahead_out):
        lo, hi = slice(0, cut), slice(cut, width)
        f = lambda ref, cols: ref[:, cols].astype(F32)
        back_out[:, lo] = (f(back, lo) + f(b3, lo) + left[...].astype(F32)).astype(BF16)
        back_out[:, hi] = (f(back, hi) + f(b3, hi)).astype(BF16)
        ahead_out[:, lo] = (f(ahead, lo) + f(a3, lo)).astype(BF16)
        ahead_out[:, hi] = (f(ahead, hi) + f(a3, hi) + right[...].astype(F32)).astype(BF16)

    return join_call(kernel, "join_far", 2, back, ahead, left, right, back_3, ahead_3)


def join_near(state, own, back, ahead):
    def kernel(state, own, back, ahead, out):
        f = lambda ref: ref[...].astype(F32)
        out[...] = (f(state) + (f(own) + f(back) + f(ahead))).astype(BF16)

    return join_call(kernel, "join_near", 1, state, own, back, ahead)[0]


def load_rows(pieces, gain, rows_ref, squares_ref):
    height = pieces[0].shape[0]
    width = gain.shape[1]
    cut = cut_of(pieces[0].shape[1])

    def put(ref, at, lo, hi, base):
        held = None
        for c in range(lo, hi, LANES):
            x = ref[:, c - base : c - base + LANES].astype(F32)
            held = x * x if held is None else held + x * x
            rows_ref[at : at + height, c : c + LANES] = (
                x * gain[:, c : c + LANES]
            ).astype(BF16)
        return held

    for n in range(8):
        at = n * height
        if n < 7:
            held = put(pieces[n], at, 0, width, 0)
        else:
            held = put(pieces[7], at, 0, cut, 0) + put(pieces[8], at, cut, width, cut)
        squares_ref[at : at + height, :] = held


def load_table(pieces, width, table_ref):
    height = pieces[0].shape[0]
    cut = cut_of(pieces[0].shape[1])
    for n in range(8):
        ref, lo = (pieces[n], width) if n < 7 else (pieces[8], width - cut)
        table_ref[n * height : (n + 1) * height, :] = ref[:, lo : lo + LANES].astype(F32)


def scaled(block, factor):
    return block * jnp.full(block.shape, factor, F32).astype(BF16)


def scaled_weights(arrays, factors, first):
    side, width = min(arrays[0].shape), max(arrays[0].shape)
    per_block, blocks, strips = side // LANES, width // side, width // LANES
    group = max(n for n in (1, 2, 4) if blocks % n == 0)
    groups = [(n, at) for n in range(len(arrays)) for at in range(0, blocks, group)]

    def kernel(f_ref, *refs):
        ins, out_ref, sems = refs[: len(arrays)], refs[-2], refs[-1]

        def copies(n, at):
            if ins[n].shape[0] == width:
                src = ins[n].at[pl.ds(at * side, group * side), :]
                dst = out_ref.at[pl.ds(n * width + at * side, group * side), :]
                return [pltpu.make_async_copy(src, dst, sems.at[n, at])]
            return [
                pltpu.make_async_copy(
                    ins[n].at[:, pl.ds(j * side, side)],
                    out_ref.at[pl.ds(n * width + j * side, side), :],
                    sems.at[n, j],
                )
                for j in range(at, at + group)
            ]

        def scale(n, at):
            tall = ins[n].shape[0] == width
            for j in range(at, at + group):
                for a in range(per_block):
                    for b in range(per_block):
                        along, across = (a, b) if tall else (b, a)
                        strip = (first + n) * strips + j * per_block + along
                        row = n * width + j * side + a * LANES
                        place = (slice(row, row + LANES), slice(b * LANES, (b + 1) * LANES))
                        out_ref[place] = scaled(out_ref[place], f_ref[strip * per_block + across])

        for n in range(len(groups) + AHEAD):
            if n < len(groups):
                for copy in copies(*groups[n]):
                    copy.start()
            if n >= AHEAD:
                for copy in copies(*groups[n - AHEAD]):
                    copy.wait()
                scale(*groups[n - AHEAD])

    return pl.pallas_call(
        kernel,
        in_specs=[pl.BlockSpec(memory_space=pltpu.SMEM)]
        + [pl.BlockSpec(memory_space=pltpu.HBM)] * len(arrays),
        out_specs=pl.BlockSpec(memory_space=pltpu.VMEM),
        out_shape=jax.ShapeDtypeStruct((len(arrays) * width, side), BF16),
        scratch_shapes=[pltpu.SemaphoreType.DMA((len(arrays), blocks))],
        compiler_params=pltpu.CompilerParams(vmem_limit_bytes=VMEM_LIMIT),
        cost_estimate=pl.CostEstimate(
            flops=len(arrays) * width * side,
            bytes_accessed=4 * len(arrays) * width * side,
            transcendentals=0,
        ),
        name="scaled_weights",
    )(factors, *(pltpu.with_memory_space_constraint(w, pltpu.HBM) for w in arrays))


def experts_share(pieces, gain, weights, table, first_lane):
    width = gain.shape[1]
    side = weights[0].shape[1]
    height = pieces[0].shape[0]
    rows = 8 * height
    cut = cut_of(width)
    tile = side * max(n for n in (1, 2, 4) if width // side % n == 0)
    n_pieces = len(pieces)
    new_table = table is None

    def kernel(*refs):
        ins, gain_ref = refs[:n_pieces], refs[n_pieces]
        cores, rest = refs[n_pieces + 1 : n_pieces + 3], refs[n_pieces + 3 :]
        if not new_table:
            table_in, rest = rest[0], rest[1:]
        outs, table_ref = rest[:9], rest[9]
        rows_ref, squares_ref, hidden_ref = rest[10:]

        load_rows(ins, gain_ref, rows_ref, squares_ref)
        if new_table:
            load_table(ins, width, table_ref)
        else:
            table_ref[...] = table_in[...]
        mean = jnp.sum(squares_ref[...], axis=-1, keepdims=True) / width
        factor = lax.rsqrt(mean + 1e-06)
        lane = lax.broadcasted_iota(jnp.int32, (rows, LANES), 1)
        own_lane = first_lane + lax.div(lax.axis_index("expert"), SPLIT)
        picked = jnp.where(lane == own_lane, table_ref[...], 0.0)
        weight = jnp.sum(picked, axis=-1, keepdims=True)

        for core, ref in enumerate(cores):
            gate = jnp.dot(rows_ref[...], ref[:width, :], preferred_element_type=F32)
            up = jnp.dot(rows_ref[...], ref[width : 2 * width, :], preferred_element_type=F32)
            gate, up = gate * factor, up * factor
            hidden_ref[:, core * side : (core + 1) * side] = (
                gate / (1.0 + jnp.exp(-gate)) * up
            ).astype(BF16)

        for lo in range(0, width, side):
            product = sum(
                jnp.dot(
                    hidden_ref[:, core * side : (core + 1) * side],
                    ref[2 * width + lo : 2 * width + lo + side, :],
                    preferred_element_type=F32,
                )
                for core, ref in enumerate(cores)
            )
            product = (product * weight).astype(BF16)
            hi = lo + side
            for n in range(7):
                outs[n][:, lo:hi] = product[n * height : (n + 1) * height, :]
            last = product[7 * height :, :]
            if lo < cut:
                outs[7][:, lo : min(hi, cut)] = last[:, : min(hi, cut) - lo]
            if hi > cut:
                outs[8][:, max(lo, cut) - cut : hi - cut] = last[:, max(lo, cut) - lo :]

    vmem = pl.BlockSpec(memory_space=pltpu.VMEM)
    tables = [] if new_table else [table]
    held = [pltpu.with_memory_space_constraint(w, pltpu.VMEM) for w in weights]
    operands = [*pieces, gain, *held, *tables]
    out_sizes = [(height, width)] * 7 + [(height, cut), (height, width - cut)]
    results = pl.pallas_call(
        kernel,
        in_specs=[vmem] * len(operands),
        out_specs=[vmem] * 10,
        out_shape=[jax.ShapeDtypeStruct(s, BF16) for s in out_sizes]
        + [jax.ShapeDtypeStruct((rows, LANES), F32)],
        scratch_shapes=[
            pltpu.VMEM((rows, width), BF16),
            pltpu.VMEM((rows, LANES), F32),
            pltpu.VMEM((rows, 2 * side), BF16),
        ],
        compiler_params=pltpu.CompilerParams(vmem_limit_bytes=VMEM_LIMIT),
        cost_estimate=pl.CostEstimate(
            flops=12 * rows * width * side,
            bytes_accessed=12 * width * side,
            transcendentals=2 * rows * side,
        ),
        name="experts_share",
    )(*operands)
    return results[:9], results[9]


def weights_table(routes, route_weights, experts):
    ids = jnp.arange(experts, dtype=jnp.int32)
    matches = (routes[..., None] == ids).astype(F32)
    table = jnp.sum(matches * route_weights.astype(F32)[..., None], axis=2)
    table = table.transpose(1, 0, 2).reshape(table.shape[1], TICKS * experts)
    return jnp.pad(table, ((0, 0), (0, LANES - TICKS * experts))).astype(BF16)


def per_device(
    tokens, norm_gain, gate_weight, up_weight, down_weight, block_scales, routes, route_weights
):
    experts = lax.axis_size("expert") // SPLIT
    state = tokens[0]
    table = weights_table(routes[0], route_weights[0], experts)
    rows = jnp.concatenate([state, table], axis=1)

    factors = jnp.exp2(block_scales[0].astype(F32)).reshape(-1)
    rows, factors = lax.optimization_barrier((rows, factors))
    own = scaled_weights((gate_weight[0], up_weight[0], down_weight[0]), factors, 0)
    weights = (own, other_core(own))

    held_table = None
    for tick in range(TICKS):
        pieces = gather_second(gather_first(rows))
        outs, held_table = experts_share(
            pieces, norm_gain, weights, held_table, tick * experts
        )
        rows = state = sum_to_next(state, outs)
    return state[None]


def solution(mesh):
    in_specs = (
        P("section", "expert", None),
        P("section", None),
        P("section", None, "expert"),
        P("section", None, "expert"),
        P("section", "expert", None),
        P("section", None, None, "expert"),
        P("section", None, "expert", None),
        P("section", None, "expert", None),
    )
    out_specs = P("section", "expert", None)
    return jax.shard_map(
        per_device, mesh=mesh, in_specs=in_specs, out_specs=out_specs, check_vma=False
    )
```

profile of v0, /device:TPU:32, one launch (start us, length us, event | category | flops | bytes accessed | tf_op | source)
XLA Modules:
  0.0 165.6 jit_solution(7749009824572516920)
XLA Ops:
  3.4 7.5 %scaled_weights.1.refs_10_ = bf16[21504,256]{1,0:T(8,128)(2,1)S(1)} custom-call(f32[336]{0:T(512)S(1)} %exp2.18.f_ref, bf16[7168,256]{1,0:T(8,128)(2,1)} %bitcast.17, bf16[7168,256]{1,0:T(8,128)(2,1)} %bitcast.18, bf16[256,7168]{1,0:T(8,128)(2,1)} %bitcast.19), custom_call_target="tpu_custom_call" | custom-call | flops 5505024 | bytes 22020096 | tf_op jit(solution)/shard_map/scaled_weights/pallas_call | solution.py:189
  11.0 5.5 %collective-permute-start.3 = (bf16[16,7296]{1,0:T(8,128)(2,1)S(1)}, bf16[16,7296]{1,0:T(8,128)(2,1)S(1)}, u32[]{:S(2)}, u32[]{:S(2)}) collective-permute-start(bf16[16,7296]{1,0:T(8,128)(2,1)S(1)} %fusion.1.refs_0_), channel_id=1, source_target_pairs={{0,12},{1,13},{2,14},{3,15},{4,0},{5,1},{6,2},{7,3},{8,4},{9,5},{1... | collective-permute-start | bytes 700424 | tf_op jit(solution)/shard_map/ppermute | solution.py:19
  18.5 8.6 %collective-permute-done.3.refs_4_ = bf16[16,7296]{1,0:T(8,128)(2,1)S(1)} collective-permute-done((bf16[16,7296]{1,0:T(8,128)(2,1)S(1)}, bf16[16,7296]{1,0:T(8,128)(2,1)S(1)}, u32[]{:S(2)}, u32[]{:S(2)}) %collective-permute-start.3) | collective-permute-done | bytes 233504 | tf_op jit(solution)/shard_map/ppermute | solution.py:19
  27.2 4.5 %collective-permute-done.2.refs_3_ = bf16[16,7296]{1,0:T(8,128)(2,1)S(1)} collective-permute-done((bf16[16,7296]{1,0:T(8,128)(2,1)S(1)}, bf16[16,7296]{1,0:T(8,128)(2,1)S(1)}, u32[]{:S(2)}, u32[]{:S(2)}) %collective-permute-start.2) | collective-permute-done | bytes 233504 | tf_op jit(solution)/shard_map/ppermute | solution.py:19
  32.0 4.6 %collective-permute-start.7 = (bf16[16,3712]{1,0:T(8,128)(2,1)S(1)}, bf16[16,3712]{1,0:T(8,128)(2,1)S(1)}, u32[]{:S(2)}, u32[]{:S(2)}) collective-permute-start(bf16[16,3712]{1,0:T(8,128)(2,1)S(1)} %slice.17), channel_id=1, source_target_pairs={{0,12},{1,13},{2,14},{3,15},{4,0},{5,1},{6,2},{7,3},{8,4},{9,5},{1... | collective-permute-start | bytes 356360 | tf_op jit(solution)/shard_map/ppermute | solution.py:19
  36.9 9.1 %collective-permute-done.6.refs_7_ = bf16[16,3584]{1,0:T(8,128)(2,1)S(1)} collective-permute-done((bf16[16,3584]{1,0:T(8,128)(2,1)S(1)}, bf16[16,3584]{1,0:T(8,128)(2,1)S(1)}, u32[]{:S(2)}, u32[]{:S(2)}) %collective-permute-start.6) | collective-permute-done | bytes 114720 | tf_op jit(solution)/shard_map/ppermute | solution.py:19
  46.1 3.4 %experts_share.2 = (bf16[16,7168]{1,0:T(8,128)(2,1)S(1)}, bf16[16,7168]{1,0:T(8,128)(2,1)S(1)}, bf16[16,7168]{1,0:T(8,128)(2,1)S(1)}, bf16[16,7168]{1,0:T(8,128)...) custom-call(bf16[16,7296]{1,0:T(8,128)(2,1)S(1)} %fusion.1.refs_0_, ...), custom_call_target="tpu_custom_call" | custom-call | flops 2818572288 | bytes 22020096 | tf_op jit(solution)/shard_map/experts_share/pallas_call | solution.py:268
  50.4 1.6 collective-permute-start.12
  52.5 4.1 %collective-permute-done.9.left = bf16[16,3584]{1,0:T(8,128)(2,1)S(1)} collective-permute-done((bf16[16,3584]{1,0:T(8,128)(2,1)S(1)}, bf16[16,3584]{1,0:T(8,128)(2,1)S(1)}, u32[]{:S(2)}, u32[]{:S(2)}) %collective-permute-start.9) | collective-permute-done | bytes 114720 | tf_op jit(solution)/shard_map/ppermute | solution.py:19
  58.9 10.9 %collective-permute-done.10.right = bf16[16,3584]{1,0:T(8,128)(2,1)S(1)} collective-permute-done((bf16[16,3584]{1,0:T(8,128)(2,1)S(1)}, bf16[16,3584]{1,0:T(8,128)(2,1)S(1)}, u32[]{:S(2)}, u32[]{:S(2)}) %collective-permute-start.10) | collective-permute-done | bytes 114720 | tf_op jit(solution)/shard_map/ppermute | solution.py:19
  70.0 2.0 %collective-permute-start.13 = (bf16[16,7168]{1,0:T(8,128)(2,1)S(1)}, bf16[16,7168]{1,0:T(8,128)(2,1)S(1)}, u32[]{:S(2)}, u32[]{:S(2)}) collective-permute-start(bf16[16,7168]{1,0:T(8,128)(2,1)S(1)} %get-tuple-element.44), channel_id=1, source_target_pairs={{0,28},{1,29},{2,30},{3,31},{4,16},{5,17},{6,18},{7,19},{8,20},{9,... | collective-permute-start | bytes 688136 | tf_op jit(solution)/shard_map/ppermute | solution.py:36
  72.0 2.6 %collective-permute-start.14 = (bf16[16,7168]{1,0:T(8,128)(2,1)S(1)}, bf16[16,7168]{1,0:T(8,128)(2,1)S(1)}, u32[]{:S(2)}, u32[]{:S(2)}) collective-permute-start(bf16[16,7168]{1,0:T(8,128)(2,1)S(1)} %get-tuple-element.45), channel_id=1, source_target_pairs={{0,20},{1,21},{2,22},{3,23},{4,24},{5,25},{6,26},{7,27},{8,28},{9,... | collective-permute-start | bytes 688136 | tf_op jit(solution)/shard_map/ppermute | solution.py:36
  76.1 8.0 %collective-permute-done.13 = bf16[16,7168]{1,0:T(8,128)(2,1)S(1)} collective-permute-done((bf16[16,7168]{1,0:T(8,128)(2,1)S(1)}, bf16[16,7168]{1,0:T(8,128)(2,1)S(1)}, u32[]{:S(2)}, u32[]{:S(2)}) %collective-permute-start.13) | collective-permute-done | bytes 229408 | tf_op jit(solution)/shard_map/ppermute | solution.py:36
  84.1 2.2 %collective-permute-done.14 = bf16[16,7168]{1,0:T(8,128)(2,1)S(1)} collective-permute-done((bf16[16,7168]{1,0:T(8,128)(2,1)S(1)}, bf16[16,7168]{1,0:T(8,128)(2,1)S(1)}, u32[]{:S(2)}, u32[]{:S(2)}) %collective-permute-start.14) | collective-permute-done | bytes 229408 | tf_op jit(solution)/shard_map/ppermute | solution.py:36
  86.3 1.9 %collective-permute-done.17 = bf16[16,7168]{1,0:T(8,128)(2,1)S(1)} collective-permute-done((bf16[16,7168]{1,0:T(8,128)(2,1)S(1)}, bf16[16,7168]{1,0:T(8,128)(2,1)S(1)}, u32[]{:S(2)}, u32[]{:S(2)}) %collective-permute-start.17) | collective-permute-done | bytes 229408 | tf_op jit(solution)/shard_map/ppermute | solution.py:36
  88.3 2.2 %collective-permute-start.21 = (bf16[16,7168]{1,0:T(8,128)(2,1)S(1)}, bf16[16,7168]{1,0:T(8,128)(2,1)S(1)}, u32[]{:S(2)}, u32[]{:S(2)}) collective-permute-start(bf16[16,7168]{1,0:T(8,128)(2,1)S(1)} %add_convert_fusion.1.refs_0_.state), channel_id=1, source_target_pairs={{0,12},{1,13},{2,14},{3,15},{4,0},{5,1},{6,2},{7,3},{8,4},{9,5},{1... | collective-permute-start | bytes 688136 | tf_op jit(solution)/shard_map/ppermute | solution.py:19
  90.4 1.5 collective-permute-start.20
  91.9 1.8 %collective-permute-start.19 = (bf16[16,7168]{1,0:T(8,128)(2,1)S(1)}, bf16[16,7168]{1,0:T(8,128)(2,1)S(1)}, u32[]{:S(2)}, u32[]{:S(2)}) collective-permute-start(bf16[16,7168]{1,0:T(8,128)(2,1)S(1)} %add_convert_fusion.1.refs_0_.state), channel_id=1, source_target_pairs={{0,14},{1,15},{2,0},{3,1},{4,2},{5,3},{6,4},{7,5},{8,6},{9,7},{10,... | collective-permute-start | bytes 688136 | tf_op jit(solution)/shard_map/ppermute | solution.py:19
  94.1 8.9 %collective-permute-done.21.refs_4_ = bf16[16,7168]{1,0:T(8,128)(2,1)S(1)} collective-permute-done((bf16[16,7168]{1,0:T(8,128)(2,1)S(1)}, bf16[16,7168]{1,0:T(8,128)(2,1)S(1)}, u32[]{:S(2)}, u32[]{:S(2)}) %collective-permute-start.21) | collective-permute-done | bytes 229408 | tf_op jit(solution)/shard_map/ppermute | solution.py:19
  103.0 2.9 %collective-permute-done.20.refs_3_ = bf16[16,7168]{1,0:T(8,128)(2,1)S(1)} collective-permute-done((bf16[16,7168]{1,0:T(8,128)(2,1)S(1)}, bf16[16,7168]{1,0:T(8,128)(2,1)S(1)}, u32[]{:S(2)}, u32[]{:S(2)}) %collective-permute-start.20) | collective-permute-done | bytes 229408 | tf_op jit(solution)/shard_map/ppermute | solution.py:19
  106.2 5.1 %collective-permute-start.25 = (bf16[16,3584]{1,0:T(8,128)(2,1)S(1)}, bf16[16,3584]{1,0:T(8,128)(2,1)S(1)}, u32[]{:S(2)}, u32[]{:S(2)}) collective-permute-start(bf16[16,3584]{1,0:T(8,128)(2,1)S(1)} %slice.19), channel_id=1, source_target_pairs={{0,12},{1,13},{2,14},{3,15},{4,0},{5,1},{6,2},{7,3},{8,4},{9,5},{1... | collective-permute-start | bytes 344072 | tf_op jit(solution)/shard_map/ppermute | solution.py:19
  111.4 4.3 %collective-permute-done.25.refs_8_ = bf16[16,3584]{1,0:T(8,128)(2,1)S(1)} collective-permute-done((bf16[16,3584]{1,0:T(8,128)(2,1)S(1)}, bf16[16,3584]{1,0:T(8,128)(2,1)S(1)}, u32[]{:S(2)}, u32[]{:S(2)}) %collective-permute-start.25) | collective-permute-done | bytes 114720 | tf_op jit(solution)/shard_map/ppermute | solution.py:19
  115.7 3.0 %collective-permute-done.24.refs_7_ = bf16[16,3584]{1,0:T(8,128)(2,1)S(1)} collective-permute-done((bf16[16,3584]{1,0:T(8,128)(2,1)S(1)}, bf16[16,3584]{1,0:T(8,128)(2,1)S(1)}, u32[]{:S(2)}, u32[]{:S(2)}) %collective-permute-start.24) | collective-permute-done | bytes 114720 | tf_op jit(solution)/shard_map/ppermute | solution.py:19
  118.8 3.3 %experts_share.3 = (bf16[16,7168]{1,0:T(8,128)(2,1)S(1)}, bf16[16,7168]{1,0:T(8,128)(2,1)S(1)}, bf16[16,7168]{1,0:T(8,128)(2,1)S(1)}, bf16[16,7168]{1,0:T(8,128)...) custom-call(bf16[16,7168]{1,0:T(8,128)(2,1)S(1)} %add_convert_fusion, ...), custom_call_target="tpu_custom_call" | custom-call | flops 2818572288 | bytes 22020096 | tf_op jit(solution)/shard_map/experts_share/pallas_call | solution.py:268
  122.1 2.1 %collective-permute-start.26 = (bf16[16,3584]{1,0:T(8,128)(2,1)S(1)}, bf16[16,3584]{1,0:T(8,128)(2,1)S(1)}, u32[]{:S(2)}, u32[]{:S(2)}) collective-permute-start(bf16[16,3584]{1,0:T(8,128)(2,1)S(1)} %get-tuple-element.52), channel_id=1, source_target_pairs={{0,12},{1,13},{2,14},{3,15},{4,0},{5,1},{6,2},{7,3},{8,4},{9,5},{1... | collective-permute-start | bytes 344072 | tf_op jit(solution)/shard_map/ppermute | solution.py:19
  127.0 1.4 collective-permute-start.32
  128.3 1.5 collective-permute-done.26.left
  129.8 3.4 %collective-permute-start.33 = (bf16[16,7168]{1,0:T(8,128)(2,1)S(1)}, bf16[16,7168]{1,0:T(8,128)(2,1)S(1)}, u32[]{:S(2)}, u32[]{:S(2)}) collective-permute-start(bf16[16,7168]{1,0:T(8,128)(2,1)S(1)} %get-tuple-element.62), channel_id=1, source_target_pairs={{0,2},{1,3},{2,4},{3,5},{4,6},{5,7},{6,8},{7,9},{8,10},{9,11},{10,... | collective-permute-start | bytes 688136 | tf_op jit(solution)/shard_map/ppermute | solution.py:19
  134.2 13.3 %collective-permute-done.27.right = bf16[16,3584]{1,0:T(8,128)(2,1)S(1)} collective-permute-done((bf16[16,3584]{1,0:T(8,128)(2,1)S(1)}, bf16[16,3584]{1,0:T(8,128)(2,1)S(1)}, u32[]{:S(2)}, u32[]{:S(2)}) %collective-permute-start.27) | collective-permute-done | bytes 114720 | tf_op jit(solution)/shard_map/ppermute | solution.py:19
  148.1 13.3 %collective-permute-done.30 = bf16[16,7168]{1,0:T(8,128)(2,1)S(1)} collective-permute-done((bf16[16,7168]{1,0:T(8,128)(2,1)S(1)}, bf16[16,7168]{1,0:T(8,128)(2,1)S(1)}, u32[]{:S(2)}, u32[]{:S(2)}) %collective-permute-start.30) | collective-permute-done | bytes 229408 | tf_op jit(solution)/shard_map/ppermute | solution.py:36
  161.4 1.4 collective-permute-done.31
  162.8 2.0 %collective-permute-done.34 = bf16[16,7168]{1,0:T(8,128)(2,1)S(1)} collective-permute-done((bf16[16,7168]{1,0:T(8,128)(2,1)S(1)}, bf16[16,7168]{1,0:T(8,128)(2,1)S(1)}, u32[]{:S(2)}, u32[]{:S(2)}) %collective-permute-start.34) | collective-permute-done | bytes 229408 | tf_op jit(solution)/shard_map/ppermute | solution.py:36
  (62 shorter events, 17.5 us)
Async XLA Ops:
  10.9 35.2 %collective-permute-start.8 = (bf16[21504,256]{1,0:T(8,128)(2,1)S(1)}, bf16[21504,256]{1,0:T(8,128)(2,1)S(1)}, u32[]{:S(2)}, u32[]{:S(2)}) collective-permute-start(bf16[21504,256]{1,0:T(8,128)(2,1)S(1)} %scaled_weights.1.refs_10_), channel_id=1, source_target_pairs={{0,1},{1,0},{2,3},{3,2},{4,5},{5,4},{6,7},{7,6},{8,9},{9,8},{10,11... | collective-permute-start | bytes 33030152 | tf_op jit(solution)/shard_map/ppermute | solution.py:26
  11.0 16.1 %collective-permute-start.3 = (bf16[16,7296]{1,0:T(8,128)(2,1)S(1)}, bf16[16,7296]{1,0:T(8,128)(2,1)S(1)}, u32[]{:S(2)}, u32[]{:S(2)}) collective-permute-start(bf16[16,7296]{1,0:T(8,128)(2,1)S(1)} %fusion.1.refs_0_), channel_id=1, source_target_pairs={{0,12},{1,13},{2,14},{3,15},{4,0},{5,1},{6,2},{7,3},{8,4},{9,5},{1... | collective-permute-start | bytes 700424 | tf_op jit(solution)/shard_map/ppermute | solution.py:19
  16.4 15.3 %collective-permute-start.2 = (bf16[16,7296]{1,0:T(8,128)(2,1)S(1)}, bf16[16,7296]{1,0:T(8,128)(2,1)S(1)}, u32[]{:S(2)}, u32[]{:S(2)}) collective-permute-start(bf16[16,7296]{1,0:T(8,128)(2,1)S(1)} %fusion.1.refs_0_), channel_id=1, source_target_pairs={{0,4},{1,5},{2,6},{3,7},{4,8},{5,9},{6,10},{7,11},{8,12},{9,13},{1... | collective-permute-start | bytes 700424 | tf_op jit(solution)/shard_map/ppermute | solution.py:19
  16.4 15.6 %collective-permute-start.1 = (bf16[16,7296]{1,0:T(8,128)(2,1)S(1)}, bf16[16,7296]{1,0:T(8,128)(2,1)S(1)}, u32[]{:S(2)}, u32[]{:S(2)}) collective-permute-start(bf16[16,7296]{1,0:T(8,128)(2,1)S(1)} %fusion.1.refs_0_), channel_id=1, source_target_pairs={{0,14},{1,15},{2,0},{3,1},{4,2},{5,3},{6,4},{7,5},{8,6},{9,7},{10,... | collective-permute-start | bytes 700424 | tf_op jit(solution)/shard_map/ppermute | solution.py:19
  17.4 19.2 %collective-permute-start = (bf16[16,7296]{1,0:T(8,128)(2,1)S(1)}, bf16[16,7296]{1,0:T(8,128)(2,1)S(1)}, u32[]{:S(2)}, u32[]{:S(2)}) collective-permute-start(bf16[16,7296]{1,0:T(8,128)(2,1)S(1)} %fusion.1.refs_0_), channel_id=1, source_target_pairs={{0,2},{1,3},{2,4},{3,5},{4,6},{5,7},{6,8},{7,9},{8,10},{9,11},{10,... | collective-permute-start | bytes 700424 | tf_op jit(solution)/shard_map/ppermute | solution.py:19
  27.0 19.0 %collective-permute-start.5 = (bf16[16,7296]{1,0:T(8,128)(2,1)S(1)}, bf16[16,7296]{1,0:T(8,128)(2,1)S(1)}, u32[]{:S(2)}, u32[]{:S(2)}) collective-permute-start(bf16[16,7296]{1,0:T(8,128)(2,1)S(1)} %collective-permute-done.3.refs_4_), channel_id=1, source_target_pairs={{0,14},{1,15},{2,0},{3,1},{4,2},{5,3},{6,4},{7,5},{8,6},{9,7},{10,... | collective-permute-start | bytes 700424 | tf_op jit(solution)/shard_map/ppermute | solution.py:19
  31.7 14.3 %collective-permute-start.4 = (bf16[16,7296]{1,0:T(8,128)(2,1)S(1)}, bf16[16,7296]{1,0:T(8,128)(2,1)S(1)}, u32[]{:S(2)}, u32[]{:S(2)}) collective-permute-start(bf16[16,7296]{1,0:T(8,128)(2,1)S(1)} %collective-permute-done.2.refs_3_), channel_id=1, source_target_pairs={{0,2},{1,3},{2,4},{3,5},{4,6},{5,7},{6,8},{7,9},{8,10},{9,11},{10,... | collective-permute-start | bytes 700424 | tf_op jit(solution)/shard_map/ppermute | solution.py:19
  32.0 14.0 %collective-permute-start.7 = (bf16[16,3712]{1,0:T(8,128)(2,1)S(1)}, bf16[16,3712]{1,0:T(8,128)(2,1)S(1)}, u32[]{:S(2)}, u32[]{:S(2)}) collective-permute-start(bf16[16,3712]{1,0:T(8,128)(2,1)S(1)} %slice.17), channel_id=1, source_target_pairs={{0,12},{1,13},{2,14},{3,15},{4,0},{5,1},{6,2},{7,3},{8,4},{9,5},{1... | collective-permute-start | bytes 356360 | tf_op jit(solution)/shard_map/ppermute | solution.py:19
  36.6 9.4 %collective-permute-start.6 = (bf16[16,3584]{1,0:T(8,128)(2,1)S(1)}, bf16[16,3584]{1,0:T(8,128)(2,1)S(1)}, u32[]{:S(2)}, u32[]{:S(2)}) collective-permute-start(bf16[16,3584]{1,0:T(8,128)(2,1)S(1)} %slice.16), channel_id=1, source_target_pairs={{0,4},{1,5},{2,6},{3,7},{4,8},{5,9},{6,10},{7,11},{8,12},{9,13},{1... | collective-permute-start | bytes 344072 | tf_op jit(solution)/shard_map/ppermute | solution.py:19
  50.0 19.8 %collective-permute-start.11 = (bf16[16,7168]{1,0:T(8,128)(2,1)S(1)}, bf16[16,7168]{1,0:T(8,128)(2,1)S(1)}, u32[]{:S(2)}, u32[]{:S(2)}) collective-permute-start(bf16[16,7168]{1,0:T(8,128)(2,1)S(1)} %get-tuple-element.42), channel_id=1, source_target_pairs={{0,14},{1,15},{2,0},{3,1},{4,2},{5,3},{6,4},{7,5},{8,6},{9,7},{10,... | collective-permute-start | bytes 688136 | tf_op jit(solution)/shard_map/ppermute | solution.py:19
  50.4 19.4 %collective-permute-start.12 = (bf16[16,7168]{1,0:T(8,128)(2,1)S(1)}, bf16[16,7168]{1,0:T(8,128)(2,1)S(1)}, u32[]{:S(2)}, u32[]{:S(2)}) collective-permute-start(bf16[16,7168]{1,0:T(8,128)(2,1)S(1)} %get-tuple-element.43), channel_id=1, source_target_pairs={{0,2},{1,3},{2,4},{3,5},{4,6},{5,7},{6,8},{7,9},{8,10},{9,11},{10,... | collective-permute-start | bytes 688136 | tf_op jit(solution)/shard_map/ppermute | solution.py:19
  52.0 22.6 %collective-permute-start.15 = (bf16[16,7168]{1,0:T(8,128)(2,1)S(1)}, bf16[16,7168]{1,0:T(8,128)(2,1)S(1)}, u32[]{:S(2)}, u32[]{:S(2)}) collective-permute-start(bf16[16,7168]{1,0:T(8,128)(2,1)S(1)} %get-tuple-element.47), channel_id=1, source_target_pairs={{0,14},{1,15},{2,0},{3,1},{4,2},{5,3},{6,4},{7,5},{8,6},{9,7},{10,... | collective-permute-start | bytes 688136 | tf_op jit(solution)/shard_map/ppermute | solution.py:19
  56.6 18.1 %collective-permute-start.16 = (bf16[16,7168]{1,0:T(8,128)(2,1)S(1)}, bf16[16,7168]{1,0:T(8,128)(2,1)S(1)}, u32[]{:S(2)}, u32[]{:S(2)}) collective-permute-start(bf16[16,7168]{1,0:T(8,128)(2,1)S(1)} %get-tuple-element.48), channel_id=1, source_target_pairs={{0,2},{1,3},{2,4},{3,5},{4,6},{5,7},{6,8},{7,9},{8,10},{9,11},{10,... | collective-permute-start | bytes 688136 | tf_op jit(solution)/shard_map/ppermute | solution.py:19
  57.8 12.1 %collective-permute-start.10 = (bf16[16,3584]{1,0:T(8,128)(2,1)S(1)}, bf16[16,3584]{1,0:T(8,128)(2,1)S(1)}, u32[]{:S(2)}, u32[]{:S(2)}) collective-permute-start(bf16[16,3584]{1,0:T(8,128)(2,1)S(1)} %get-tuple-element.41), channel_id=1, source_target_pairs={{0,4},{1,5},{2,6},{3,7},{4,8},{5,9},{6,10},{7,11},{8,12},{9,13},{1... | collective-permute-start | bytes 344072 | tf_op jit(solution)/shard_map/ppermute | solution.py:19
  70.0 14.1 %collective-permute-start.13 = (bf16[16,7168]{1,0:T(8,128)(2,1)S(1)}, bf16[16,7168]{1,0:T(8,128)(2,1)S(1)}, u32[]{:S(2)}, u32[]{:S(2)}) collective-permute-start(bf16[16,7168]{1,0:T(8,128)(2,1)S(1)} %get-tuple-element.44), channel_id=1, source_target_pairs={{0,28},{1,29},{2,30},{3,31},{4,16},{5,17},{6,18},{7,19},{8,20},{9,... | collective-permute-start | bytes 688136 | tf_op jit(solution)/shard_map/ppermute | solution.py:36
  72.0 14.3 %collective-permute-start.14 = (bf16[16,7168]{1,0:T(8,128)(2,1)S(1)}, bf16[16,7168]{1,0:T(8,128)(2,1)S(1)}, u32[]{:S(2)}, u32[]{:S(2)}) collective-permute-start(bf16[16,7168]{1,0:T(8,128)(2,1)S(1)} %get-tuple-element.45), channel_id=1, source_target_pairs={{0,20},{1,21},{2,22},{3,23},{4,24},{5,25},{6,26},{7,27},{8,28},{9,... | collective-permute-start | bytes 688136 | tf_op jit(solution)/shard_map/ppermute | solution.py:36
  74.8 13.4 %collective-permute-start.17 = (bf16[16,7168]{1,0:T(8,128)(2,1)S(1)}, bf16[16,7168]{1,0:T(8,128)(2,1)S(1)}, u32[]{:S(2)}, u32[]{:S(2)}) collective-permute-start(bf16[16,7168]{1,0:T(8,128)(2,1)S(1)} %join_near.2), channel_id=1, source_target_pairs={{0,16},{1,17},{2,18},{3,19},{4,20},{5,21},{6,22},{7,23},{8,24},{9,... | collective-permute-start | bytes 688136 | tf_op jit(solution)/shard_map/ppermute | solution.py:36
  88.3 14.7 %collective-permute-start.21 = (bf16[16,7168]{1,0:T(8,128)(2,1)S(1)}, bf16[16,7168]{1,0:T(8,128)(2,1)S(1)}, u32[]{:S(2)}, u32[]{:S(2)}) collective-permute-start(bf16[16,7168]{1,0:T(8,128)(2,1)S(1)} %add_convert_fusion.1.refs_0_.state), channel_id=1, source_target_pairs={{0,12},{1,13},{2,14},{3,15},{4,0},{5,1},{6,2},{7,3},{8,4},{9,5},{1... | collective-permute-start | bytes 688136 | tf_op jit(solution)/shard_map/ppermute | solution.py:19
  90.4 15.4 %collective-permute-start.20 = (bf16[16,7168]{1,0:T(8,128)(2,1)S(1)}, bf16[16,7168]{1,0:T(8,128)(2,1)S(1)}, u32[]{:S(2)}, u32[]{:S(2)}) collective-permute-start(bf16[16,7168]{1,0:T(8,128)(2,1)S(1)} %add_convert_fusion.1.refs_0_.state), channel_id=1, source_target_pairs={{0,4},{1,5},{2,6},{3,7},{4,8},{5,9},{6,10},{7,11},{8,12},{9,13},{1... | collective-permute-start | bytes 688136 | tf_op jit(solution)/shard_map/ppermute | solution.py:19
  91.9 19.4 %collective-permute-start.19 = (bf16[16,7168]{1,0:T(8,128)(2,1)S(1)}, bf16[16,7168]{1,0:T(8,128)(2,1)S(1)}, u32[]{:S(2)}, u32[]{:S(2)}) collective-permute-start(bf16[16,7168]{1,0:T(8,128)(2,1)S(1)} %add_convert_fusion.1.refs_0_.state), channel_id=1, source_target_pairs={{0,14},{1,15},{2,0},{3,1},{4,2},{5,3},{6,4},{7,5},{8,6},{9,7},{10,... | collective-permute-start | bytes 688136 | tf_op jit(solution)/shard_map/ppermute | solution.py:19
  93.7 17.7 %collective-permute-start.18 = (bf16[16,7168]{1,0:T(8,128)(2,1)S(1)}, bf16[16,7168]{1,0:T(8,128)(2,1)S(1)}, u32[]{:S(2)}, u32[]{:S(2)}) collective-permute-start(bf16[16,7168]{1,0:T(8,128)(2,1)S(1)} %add_convert_fusion.1.refs_0_.state), channel_id=1, source_target_pairs={{0,2},{1,3},{2,4},{3,5},{4,6},{5,7},{6,8},{7,9},{8,10},{9,11},{10,... | collective-permute-start | bytes 688136 | tf_op jit(solution)/shard_map/ppermute | solution.py:19
  103.0 15.8 %collective-permute-start.23 = (bf16[16,7168]{1,0:T(8,128)(2,1)S(1)}, bf16[16,7168]{1,0:T(8,128)(2,1)S(1)}, u32[]{:S(2)}, u32[]{:S(2)}) collective-permute-start(bf16[16,7168]{1,0:T(8,128)(2,1)S(1)} %collective-permute-done.21.refs_4_), channel_id=1, source_target_pairs={{0,14},{1,15},{2,0},{3,1},{4,2},{5,3},{6,4},{7,5},{8,6},{9,7},{10,... | collective-permute-start | bytes 688136 | tf_op jit(solution)/shard_map/ppermute | solution.py:19
  105.9 12.9 %collective-permute-start.22 = (bf16[16,7168]{1,0:T(8,128)(2,1)S(1)}, bf16[16,7168]{1,0:T(8,128)(2,1)S(1)}, u32[]{:S(2)}, u32[]{:S(2)}) collective-permute-start(bf16[16,7168]{1,0:T(8,128)(2,1)S(1)} %collective-permute-done.20.refs_3_), channel_id=1, source_target_pairs={{0,2},{1,3},{2,4},{3,5},{4,6},{5,7},{6,8},{7,9},{8,10},{9,11},{10,... | collective-permute-start | bytes 688136 | tf_op jit(solution)/shard_map/ppermute | solution.py:19
  106.2 9.6 %collective-permute-start.25 = (bf16[16,3584]{1,0:T(8,128)(2,1)S(1)}, bf16[16,3584]{1,0:T(8,128)(2,1)S(1)}, u32[]{:S(2)}, u32[]{:S(2)}) collective-permute-start(bf16[16,3584]{1,0:T(8,128)(2,1)S(1)} %slice.19), channel_id=1, source_target_pairs={{0,12},{1,13},{2,14},{3,15},{4,0},{5,1},{6,2},{7,3},{8,4},{9,5},{1... | collective-permute-start | bytes 344072 | tf_op jit(solution)/shard_map/ppermute | solution.py:19
  124.2 23.3 %collective-permute-start.28 = (bf16[16,7168]{1,0:T(8,128)(2,1)S(1)}, bf16[16,7168]{1,0:T(8,128)(2,1)S(1)}, u32[]{:S(2)}, u32[]{:S(2)}) collective-permute-start(bf16[16,7168]{1,0:T(8,128)(2,1)S(1)} %get-tuple-element.56), channel_id=1, source_target_pairs={{0,14},{1,15},{2,0},{3,1},{4,2},{5,3},{6,4},{7,5},{8,6},{9,7},{10,... | collective-permute-start | bytes 688136 | tf_op jit(solution)/shard_map/ppermute | solution.py:19
  125.6 22.0 %collective-permute-start.29 = (bf16[16,7168]{1,0:T(8,128)(2,1)S(1)}, bf16[16,7168]{1,0:T(8,128)(2,1)S(1)}, u32[]{:S(2)}, u32[]{:S(2)}) collective-permute-start(bf16[16,7168]{1,0:T(8,128)(2,1)S(1)} %get-tuple-element.57), channel_id=1, source_target_pairs={{0,2},{1,3},{2,4},{3,5},{4,6},{5,7},{6,8},{7,9},{8,10},{9,11},{10,... | collective-permute-start | bytes 688136 | tf_op jit(solution)/shard_map/ppermute | solution.py:19
  127.0 20.9 %collective-permute-start.32 = (bf16[16,7168]{1,0:T(8,128)(2,1)S(1)}, bf16[16,7168]{1,0:T(8,128)(2,1)S(1)}, u32[]{:S(2)}, u32[]{:S(2)}) collective-permute-start(bf16[16,7168]{1,0:T(8,128)(2,1)S(1)} %get-tuple-element.61), channel_id=1, source_target_pairs={{0,14},{1,15},{2,0},{3,1},{4,2},{5,3},{6,4},{7,5},{8,6},{9,7},{10,... | collective-permute-start | bytes 688136 | tf_op jit(solution)/shard_map/ppermute | solution.py:19
  129.8 18.1 %collective-permute-start.33 = (bf16[16,7168]{1,0:T(8,128)(2,1)S(1)}, bf16[16,7168]{1,0:T(8,128)(2,1)S(1)}, u32[]{:S(2)}, u32[]{:S(2)}) collective-permute-start(bf16[16,7168]{1,0:T(8,128)(2,1)S(1)} %get-tuple-element.62), channel_id=1, source_target_pairs={{0,2},{1,3},{2,4},{3,5},{4,6},{5,7},{6,8},{7,9},{8,10},{9,11},{10,... | collective-permute-start | bytes 688136 | tf_op jit(solution)/shard_map/ppermute | solution.py:19
  133.3 14.3 %collective-permute-start.27 = (bf16[16,3584]{1,0:T(8,128)(2,1)S(1)}, bf16[16,3584]{1,0:T(8,128)(2,1)S(1)}, u32[]{:S(2)}, u32[]{:S(2)}) collective-permute-start(bf16[16,3584]{1,0:T(8,128)(2,1)S(1)} %get-tuple-element.55), channel_id=1, source_target_pairs={{0,4},{1,5},{2,6},{3,7},{4,8},{5,9},{6,10},{7,11},{8,12},{9,13},{1... | collective-permute-start | bytes 344072 | tf_op jit(solution)/shard_map/ppermute | solution.py:19
  147.7 13.7 %collective-permute-start.30 = (bf16[16,7168]{1,0:T(8,128)(2,1)S(1)}, bf16[16,7168]{1,0:T(8,128)(2,1)S(1)}, u32[]{:S(2)}, u32[]{:S(2)}) collective-permute-start(bf16[16,7168]{1,0:T(8,128)(2,1)S(1)} %get-tuple-element.58), channel_id=1, source_target_pairs={{0,28},{1,29},{2,30},{3,31},{4,16},{5,17},{6,18},{7,19},{8,20},{9,... | collective-permute-start | bytes 688136 | tf_op jit(solution)/shard_map/ppermute | solution.py:36
  147.8 15.0 %collective-permute-start.31 = (bf16[16,7168]{1,0:T(8,128)(2,1)S(1)}, bf16[16,7168]{1,0:T(8,128)(2,1)S(1)}, u32[]{:S(2)}, u32[]{:S(2)}) collective-permute-start(bf16[16,7168]{1,0:T(8,128)(2,1)S(1)} %get-tuple-element.59), channel_id=1, source_target_pairs={{0,20},{1,21},{2,22},{3,23},{4,24},{5,25},{6,26},{7,27},{8,28},{9,... | collective-permute-start | bytes 688136 | tf_op jit(solution)/shard_map/ppermute | solution.py:36
  148.0 16.8 %collective-permute-start.34 = (bf16[16,7168]{1,0:T(8,128)(2,1)S(1)}, bf16[16,7168]{1,0:T(8,128)(2,1)S(1)}, u32[]{:S(2)}, u32[]{:S(2)}) collective-permute-start(bf16[16,7168]{1,0:T(8,128)(2,1)S(1)} %join_near.3), channel_id=1, source_target_pairs={{0,16},{1,17},{2,18},{3,19},{4,20},{5,21},{6,22},{7,23},{8,24},{9,... | collective-permute-start | bytes 688136 | tf_op jit(solution)/shard_map/ppermute | solution.py:36
  (5 other events, 103.0 us)
where the time goes:
time: 166 us
  waiting for transfers between devices  100 us (60%)
  starting transfers between devices  46.1 us (28%)
  Pallas kernels  14.7 us (9%)
  other arithmetic  3.89 us (2%)
    ppermute x28, waiting for transfers between devices, along_z(): lax.ppermute(shard, 'expert', [(i, (i + 2 * by) % length) for i in range(...  71.5 us
    ppermute x28, starting transfers between devices, along_z(): lax.ppermute(shard, 'expert', [(i, (i + 2 * by) % length) for i in range(...  39.7 us
    ppermute x6, waiting for transfers between devices, to_next_section(): return lax.ppermute(shard, ('section', 'expert'), pairs)  28.8 us
    pallas_call x1, Pallas kernels, scaled_weights(): pl.pallas_call(kernel, in_specs=[pl.BlockSpec(memory_space=pltpu.SMEM)] +...  7.46 us
    pallas_call x2, Pallas kernels, experts_share(): pl.pallas_call(kernel, in_specs=[vmem] * len(operands), out_specs=[vmem]...  6.74 us
    ppermute x6, starting transfers between devices, to_next_section(): return lax.ppermute(shard, ('section', 'expert'), pairs)  6.26 us
  transfers between devices with their start and end apart: 35, of which 18 were waited for; matrix products, arithmetic and copies ran while one was open for 0% of the time, Pallas kernels for 0%

commit v1 on v0

--- a/solution.py
+++ b/solution.py
@@ -9,7 +9,7 @@
 TICKS = 2
 LANES = 128
 VMEM_LIMIT = 16 * 1024 * 1024
-AHEAD = 4
+AHEAD = 10
 F32 = jnp.float32
 BF16 = jnp.bfloat16
 
@@ -63,8 +63,9 @@
         along_z(outs[5], -1),
         along_z(outs[6], 1),
     ]
-    far[0], last = lax.optimization_barrier((far[0], outs[2]))
-    near = [along_z(outs[1], -1), along_z(last, 1)]
+    far[0], near_back = lax.optimization_barrier((far[0], outs[1]))
+    far[1], near_ahead = lax.optimization_barrier((far[1], outs[2]))
+    near = [along_z(near_back, -1), along_z(near_ahead, 1)]
     back, ahead = join_far(outs[3], outs[4], *far)
     parts = [to_next_section(back, -2), to_next_section(ahead, 2)]
     parts.append(to_next_section(join_near(state, outs[0], *near), 0))
@@ -143,14 +144,15 @@
     return block * jnp.full(block.shape, factor, F32).astype(BF16)
 
 
-def scaled_weights(arrays, factors, first):
+def prepare(tokens, routes, route_weights, exponents, arrays, experts):
+    height = tokens.shape[0]
     side, width = min(arrays[0].shape), max(arrays[0].shape)
     per_block, blocks, strips = side // LANES, width // side, width // LANES
     group = max(n for n in (1, 2, 4) if blocks % n == 0)
     groups = [(n, at) for n in range(len(arrays)) for at in range(0, blocks, group)]
 
-    def kernel(f_ref, *refs):
-        ins, out_ref, sems = refs[: len(arrays)], refs[-2], refs[-1]
+    def kernel(exp_ref, tokens_ref, routes_ref, route_weights_ref, *refs):
+        ins, rows_out, out_ref, sems = refs[: len(arrays)], *refs[len(arrays) :]
 
         def copies(n, at):
             if ins[n].shape[0] == width:
@@ -172,26 +174,43 @@
                 for a in range(per_block):
                     for b in range(per_block):
                         along, across = (a, b) if tall else (b, a)
-                        strip = (first + n) * strips + j * per_block + along
+                        strip = n * strips + j * per_block + along
+                        exponent = exp_ref[strip * per_block + across]
+                        factor = jnp.left_shift(1, exponent + 16).astype(F32) * 2.0**-16
                         row = n * width + j * side + a * LANES
                         place = (slice(row, row + LANES), slice(b * LANES, (b + 1) * LANES))
-                        out_ref[place] = scaled(out_ref[place], f_ref[strip * per_block + across])
+                        out_ref[place] = scaled(out_ref[place], factor)
 
         for n in range(len(groups) + AHEAD):
             if n < len(groups):
                 for copy in copies(*groups[n]):
                     copy.start()
+            if n == AHEAD:
+                lane = lax.broadcasted_iota(jnp.int32, (height, LANES), 1)
+                table = jnp.zeros((height, LANES), F32)
+                for step in range(TICKS):
+                    for k in range(routes.shape[-1]):
+                        named = routes_ref[step, :, k : k + 1] + step * experts
+                        weight = route_weights_ref[step, :, k : k + 1].astype(F32)
+                        table += jnp.where(lane == named, weight, 0.0)
+                rows_out[:, :width] = tokens_ref[...]
+                rows_out[:, width:] = table.astype(BF16)
             if n >= AHEAD:
                 for copy in copies(*groups[n - AHEAD]):
                     copy.wait()
                 scale(*groups[n - AHEAD])
 
+    vmem = pl.BlockSpec(memory_space=pltpu.VMEM)
     return pl.pallas_call(
         kernel,
         in_specs=[pl.BlockSpec(memory_space=pltpu.SMEM)]
+        + [vmem] * 3
         + [pl.BlockSpec(memory_space=pltpu.HBM)] * len(arrays),
-        out_specs=pl.BlockSpec(memory_space=pltpu.VMEM),
-        out_shape=jax.ShapeDtypeStruct((len(arrays) * width, side), BF16),
+        out_specs=[vmem] * 2,
+        out_shape=[
+            jax.ShapeDtypeStruct((height, width + LANES), BF16),
+            jax.ShapeDtypeStruct((len(arrays) * width, side), BF16),
+        ],
         scratch_shapes=[pltpu.SemaphoreType.DMA((len(arrays), blocks))],
         compiler_params=pltpu.CompilerParams(vmem_limit_bytes=VMEM_LIMIT),
         cost_estimate=pl.CostEstimate(
@@ -199,8 +218,14 @@
             bytes_accessed=4 * len(arrays) * width * side,
             transcendentals=0,
         ),
-        name="scaled_weights",
-    )(factors, *(pltpu.with_memory_space_constraint(w, pltpu.HBM) for w in arrays))
+        name="prepare",
+    )(
+        exponents,
+        tokens,
+        routes,
+        route_weights,
+        *(pltpu.with_memory_space_constraint(w, pltpu.HBM) for w in arrays),
+    )
 
 
 def experts_share(pieces, gain, weights, table, first_lane):
@@ -287,25 +312,19 @@
     return results[:9], results[9]
 
 
-def weights_table(routes, route_weights, experts):
-    ids = jnp.arange(experts, dtype=jnp.int32)
-    matches = (routes[..., None] == ids).astype(F32)
-    table = jnp.sum(matches * route_weights.astype(F32)[..., None], axis=2)
-    table = table.transpose(1, 0, 2).reshape(table.shape[1], TICKS * experts)
-    return jnp.pad(table, ((0, 0), (0, LANES - TICKS * experts))).astype(BF16)
-
-
 def per_device(
     tokens, norm_gain, gate_weight, up_weight, down_weight, block_scales, routes, route_weights
 ):
     experts = lax.axis_size("expert") // SPLIT
     state = tokens[0]
-    table = weights_table(routes[0], route_weights[0], experts)
-    rows = jnp.concatenate([state, table], axis=1)
-
-    factors = jnp.exp2(block_scales[0].astype(F32)).reshape(-1)
-    rows, factors = lax.optimization_barrier((rows, factors))
-    own = scaled_weights((gate_weight[0], up_weight[0], down_weight[0]), factors, 0)
+    rows, own = prepare(
+        state,
+        routes[0],
+        route_weights[0],
+        block_scales[0].reshape(-1),
+        (gate_weight[0], up_weight[0], down_weight[0]),
+        experts,
+    )
     weights = (own, other_core(own))
 
     held_table = None

time: 166 us -> 157 us (0.946)
  the two profiles are of different devices: /device:TPU:32 before, /device:TPU:0 now
where the time goes in v1:
time: 157 us; the launch traced here: 154 us
  waiting for transfers between devices  79.9 us (51%)
  starting transfers between devices  56.2 us (36%)
  Pallas kernels  13 us (8%)
  local copies, waits for them, and re-layouts  3.44 us (2%)
    ppermute x28, waiting for transfers between devices, along_z(): lax.ppermute(shard, 'expert', [(i, (i + 2 * by) % length) for i in range(...  56 us
    ppermute x28, starting transfers between devices, along_z(): lax.ppermute(shard, 'expert', [(i, (i + 2 * by) % length) for i in range(...  46.8 us
    ppermute x6, waiting for transfers between devices, to_next_section(): return lax.ppermute(shard, ('section', 'expert'), pairs)  23.9 us
    ppermute x6, starting transfers between devices, to_next_section(): return lax.ppermute(shard, ('section', 'expert'), pairs)  9.31 us
    pallas_call x2, Pallas kernels, experts_share(): pl.pallas_call(kernel, in_specs=[vmem] * len(operands), out_specs=[vmem]...  6.77 us
    pallas_call x1, Pallas kernels, prepare(): pl.pallas_call(kernel, in_specs=[pl.BlockSpec(memory_space=pltpu.SMEM)] +...  5.75 us
  transfers between devices with their start and end apart: 35, of which 23 were waited for; matrix products, arithmetic and copies ran while one was open for 0% of the time, Pallas kernels for 0%

profile of v1, /device:TPU:0, one launch (start us, length us, event | category | flops | bytes accessed | tf_op | source)
XLA Modules:
  0.0 153.7 jit_solution(1974708436329379363)
XLA Ops:
  3.4 5.7 %prepare.1 = (bf16[16,7296]{1,0:T(8,128)(2,1)S(1)}, bf16[21504,256]{1,0:T(8,128)(2,1)S(1)}) custom-call(s32[336]{0:T(512)S(1)} %reshape_squeeze.3.exp_ref, bf16[16,7168]{1,0:T(8,128)(2,1)S(1)} %bitcast.10, s32[2,16,2]{2,1,0:T(8,128)S(1)} %copy.12.routes_ref, bf16[2,16,2]{2,1,0:T(8,128)(2,1)S(1)} %copy.13.route_weights_ref, bf16[7168,256]{1,0:T(8,128)(2,1)} %bitcast.12, ...), custom_call_target="tpu_custom_call" | custom-call | flops 5505024 | bytes 22020096 | tf_op jit(solution)/shard_map/prepare/pallas_call | solution.py:204
  9.3 4.6 %collective-permute-start.3 = (bf16[16,7296]{1,0:T(8,128)(2,1)S(1)}, bf16[16,7296]{1,0:T(8,128)(2,1)S(1)}, u32[]{:S(2)}, u32[]{:S(2)}) collective-permute-start(bf16[16,7296]{1,0:T(8,128)(2,1)S(1)} %get-tuple-element.38.refs_0_), channel_id=1, source_target_pairs={{0,12},{1,13},{2,14},{3,15},{4,0},{5,1},{6,2},{7,3},{8,4},{9,5},{1... | collective-permute-start | bytes 700424 | tf_op jit(solution)/shard_map/ppermute | solution.py:19
  13.9 3.7 %collective-permute-start.1 = (bf16[16,7296]{1,0:T(8,128)(2,1)S(1)}, bf16[16,7296]{1,0:T(8,128)(2,1)S(1)}, u32[]{:S(2)}, u32[]{:S(2)}) collective-permute-start(bf16[16,7296]{1,0:T(8,128)(2,1)S(1)} %get-tuple-element.38.refs_0_), channel_id=1, source_target_pairs={{0,14},{1,15},{2,0},{3,1},{4,2},{5,3},{6,4},{7,5},{8,6},{9,7},{10,... | collective-permute-start | bytes 700424 | tf_op jit(solution)/shard_map/ppermute | solution.py:19
  17.6 6.0 %collective-permute-done.3.refs_4_ = bf16[16,7296]{1,0:T(8,128)(2,1)S(1)} collective-permute-done((bf16[16,7296]{1,0:T(8,128)(2,1)S(1)}, bf16[16,7296]{1,0:T(8,128)(2,1)S(1)}, u32[]{:S(2)}, u32[]{:S(2)}) %collective-permute-start.3) | collective-permute-done | bytes 233504 | tf_op jit(solution)/shard_map/ppermute | solution.py:19
  23.7 5.0 %collective-permute-start.5 = (bf16[16,7296]{1,0:T(8,128)(2,1)S(1)}, bf16[16,7296]{1,0:T(8,128)(2,1)S(1)}, u32[]{:S(2)}, u32[]{:S(2)}) collective-permute-start(bf16[16,7296]{1,0:T(8,128)(2,1)S(1)} %collective-permute-done.3.refs_4_), channel_id=1, source_target_pairs={{0,14},{1,15},{2,0},{3,1},{4,2},{5,3},{6,4},{7,5},{8,6},{9,7},{10,... | collective-permute-start | bytes 700424 | tf_op jit(solution)/shard_map/ppermute | solution.py:19
  31.0 2.0 %collective-permute-start.7 = (bf16[16,3712]{1,0:T(8,128)(2,1)S(1)}, bf16[16,3712]{1,0:T(8,128)(2,1)S(1)}, u32[]{:S(2)}, u32[]{:S(2)}) collective-permute-start(bf16[16,3712]{1,0:T(8,128)(2,1)S(1)} %slice.17), channel_id=1, source_target_pairs={{0,12},{1,13},{2,14},{3,15},{4,0},{5,1},{6,2},{7,3},{8,4},{9,5},{1... | collective-permute-start | bytes 356360 | tf_op jit(solution)/shard_map/ppermute | solution.py:19
  34.2 9.1 %collective-permute-done.6.refs_7_ = bf16[16,3584]{1,0:T(8,128)(2,1)S(1)} collective-permute-done((bf16[16,3584]{1,0:T(8,128)(2,1)S(1)}, bf16[16,3584]{1,0:T(8,128)(2,1)S(1)}, u32[]{:S(2)}, u32[]{:S(2)}) %collective-permute-start.6) | collective-permute-done | bytes 114720 | tf_op jit(solution)/shard_map/ppermute | solution.py:19
  43.3 3.4 %experts_share.2 = (bf16[16,7168]{1,0:T(8,128)(2,1)S(1)}, bf16[16,7168]{1,0:T(8,128)(2,1)S(1)}, bf16[16,7168]{1,0:T(8,128)(2,1)S(1)}, bf16[16,7168]{1,0:T(8,128)...) custom-call(bf16[16,7296]{1,0:T(8,128)(2,1)S(1)} %get-tuple-element., ...), custom_call_target="tpu_custom_call" | custom-call | flops 2818572288 | bytes 22020096 | tf_op jit(solution)/shard_map/experts_share/pallas_call | solution.py:293
  46.8 2.9 %collective-permute-start.10 = (bf16[16,3584]{1,0:T(8,128)(2,1)S(1)}, bf16[16,3584]{1,0:T(8,128)(2,1)S(1)}, u32[]{:S(2)}, u32[]{:S(2)}) collective-permute-start(bf16[16,3584]{1,0:T(8,128)(2,1)S(1)} %get-tuple-element.45), channel_id=1, source_target_pairs={{0,4},{1,5},{2,6},{3,7},{4,8},{5,9},{6,10},{7,11},{8,12},{9,13},{1... | collective-permute-start | bytes 344072 | tf_op jit(solution)/shard_map/ppermute | solution.py:19
  51.8 3.7 %collective-permute-done.9.left = bf16[16,3584]{1,0:T(8,128)(2,1)S(1)} collective-permute-done((bf16[16,3584]{1,0:T(8,128)(2,1)S(1)}, bf16[16,3584]{1,0:T(8,128)(2,1)S(1)}, u32[]{:S(2)}, u32[]{:S(2)}) %collective-permute-start.9) | collective-permute-done | bytes 114720 | tf_op jit(solution)/shard_map/ppermute | solution.py:19
  55.5 1.8 %collective-permute-done.10.right = bf16[16,3584]{1,0:T(8,128)(2,1)S(1)} collective-permute-done((bf16[16,3584]{1,0:T(8,128)(2,1)S(1)}, bf16[16,3584]{1,0:T(8,128)(2,1)S(1)}, u32[]{:S(2)}, u32[]{:S(2)}) %collective-permute-start.10) | collective-permute-done | bytes 114720 | tf_op jit(solution)/shard_map/ppermute | solution.py:19
  57.3 3.2 %collective-permute-start.15 = (bf16[16,7168]{1,0:T(8,128)(2,1)S(1)}, bf16[16,7168]{1,0:T(8,128)(2,1)S(1)}, u32[]{:S(2)}, u32[]{:S(2)}) collective-permute-start(bf16[16,7168]{1,0:T(8,128)(2,1)S(1)} %get-tuple-element.53), channel_id=1, source_target_pairs={{0,14},{1,15},{2,0},{3,1},{4,2},{5,3},{6,4},{7,5},{8,6},{9,7},{10,... | collective-permute-start | bytes 688136 | tf_op jit(solution)/shard_map/ppermute | solution.py:19
  61.8 1.7 %collective-permute-start.13 = (bf16[16,7168]{1,0:T(8,128)(2,1)S(1)}, bf16[16,7168]{1,0:T(8,128)(2,1)S(1)}, u32[]{:S(2)}, u32[]{:S(2)}) collective-permute-start(bf16[16,7168]{1,0:T(8,128)(2,1)S(1)} %get-tuple-element.50), channel_id=1, source_target_pairs={{0,28},{1,29},{2,30},{3,31},{4,16},{5,17},{6,18},{7,19},{8,20},{9,... | collective-permute-start | bytes 688136 | tf_op jit(solution)/shard_map/ppermute | solution.py:36
  63.5 3.5 %collective-permute-start.14 = (bf16[16,7168]{1,0:T(8,128)(2,1)S(1)}, bf16[16,7168]{1,0:T(8,128)(2,1)S(1)}, u32[]{:S(2)}, u32[]{:S(2)}) collective-permute-start(bf16[16,7168]{1,0:T(8,128)(2,1)S(1)} %get-tuple-element.51), channel_id=1, source_target_pairs={{0,20},{1,21},{2,22},{3,23},{4,24},{5,25},{6,26},{7,27},{8,28},{9,... | collective-permute-start | bytes 688136 | tf_op jit(solution)/shard_map/ppermute | solution.py:36
  67.0 4.0 %collective-permute-done.15.back = bf16[16,7168]{1,0:T(8,128)(2,1)S(1)} collective-permute-done((bf16[16,7168]{1,0:T(8,128)(2,1)S(1)}, bf16[16,7168]{1,0:T(8,128)(2,1)S(1)}, u32[]{:S(2)}, u32[]{:S(2)}) %collective-permute-start.15) | collective-permute-done | bytes 229408 | tf_op jit(solution)/shard_map/ppermute | solution.py:19
  71.2 2.4 %collective-permute-start.17 = (bf16[16,7168]{1,0:T(8,128)(2,1)S(1)}, bf16[16,7168]{1,0:T(8,128)(2,1)S(1)}, u32[]{:S(2)}, u32[]{:S(2)}) collective-permute-start(bf16[16,7168]{1,0:T(8,128)(2,1)S(1)} %join_near.2), channel_id=1, source_target_pairs={{0,16},{1,17},{2,18},{3,19},{4,20},{5,21},{6,22},{7,23},{8,24},{9,... | collective-permute-start | bytes 688136 | tf_op jit(solution)/shard_map/ppermute | solution.py:36
  73.6 6.7 %collective-permute-done.13 = bf16[16,7168]{1,0:T(8,128)(2,1)S(1)} collective-permute-done((bf16[16,7168]{1,0:T(8,128)(2,1)S(1)}, bf16[16,7168]{1,0:T(8,128)(2,1)S(1)}, u32[]{:S(2)}, u32[]{:S(2)}) %collective-permute-start.13) | collective-permute-done | bytes 229408 | tf_op jit(solution)/shard_map/ppermute | solution.py:36
  81.6 2.7 %collective-permute-done.17 = bf16[16,7168]{1,0:T(8,128)(2,1)S(1)} collective-permute-done((bf16[16,7168]{1,0:T(8,128)(2,1)S(1)}, bf16[16,7168]{1,0:T(8,128)(2,1)S(1)}, u32[]{:S(2)}, u32[]{:S(2)}) %collective-permute-start.17) | collective-permute-done | bytes 229408 | tf_op jit(solution)/shard_map/ppermute | solution.py:36
  89.4 6.6 %collective-permute-done.21.refs_4_ = bf16[16,7168]{1,0:T(8,128)(2,1)S(1)} collective-permute-done((bf16[16,7168]{1,0:T(8,128)(2,1)S(1)}, bf16[16,7168]{1,0:T(8,128)(2,1)S(1)}, u32[]{:S(2)}, u32[]{:S(2)}) %collective-permute-start.21) | collective-permute-done | bytes 229408 | tf_op jit(solution)/shard_map/ppermute | solution.py:19
  96.0 3.1 %collective-permute-start.23 = (bf16[16,7168]{1,0:T(8,128)(2,1)S(1)}, bf16[16,7168]{1,0:T(8,128)(2,1)S(1)}, u32[]{:S(2)}, u32[]{:S(2)}) collective-permute-start(bf16[16,7168]{1,0:T(8,128)(2,1)S(1)} %collective-permute-done.21.refs_4_), channel_id=1, source_target_pairs={{0,14},{1,15},{2,0},{3,1},{4,2},{5,3},{6,4},{7,5},{8,6},{9,7},{10,... | collective-permute-start | bytes 688136 | tf_op jit(solution)/shard_map/ppermute | solution.py:19
  99.4 2.2 %collective-permute-start.22 = (bf16[16,7168]{1,0:T(8,128)(2,1)S(1)}, bf16[16,7168]{1,0:T(8,128)(2,1)S(1)}, u32[]{:S(2)}, u32[]{:S(2)}) collective-permute-start(bf16[16,7168]{1,0:T(8,128)(2,1)S(1)} %collective-permute-done.20.refs_3_), channel_id=1, source_target_pairs={{0,2},{1,3},{2,4},{3,5},{4,6},{5,7},{6,8},{7,9},{8,10},{9,11},{10,... | collective-permute-start | bytes 688136 | tf_op jit(solution)/shard_map/ppermute | solution.py:19
  102.1 2.6 %collective-permute-start.24 = (bf16[16,3584]{1,0:T(8,128)(2,1)S(1)}, bf16[16,3584]{1,0:T(8,128)(2,1)S(1)}, u32[]{:S(2)}, u32[]{:S(2)}) collective-permute-start(bf16[16,3584]{1,0:T(8,128)(2,1)S(1)} %slice.18), channel_id=1, source_target_pairs={{0,4},{1,5},{2,6},{3,7},{4,8},{5,9},{6,10},{7,11},{8,12},{9,13},{1... | collective-permute-start | bytes 344072 | tf_op jit(solution)/shard_map/ppermute | solution.py:19
  104.7 4.5 %collective-permute-done.25.refs_8_ = bf16[16,3584]{1,0:T(8,128)(2,1)S(1)} collective-permute-done((bf16[16,3584]{1,0:T(8,128)(2,1)S(1)}, bf16[16,3584]{1,0:T(8,128)(2,1)S(1)}, u32[]{:S(2)}, u32[]{:S(2)}) %collective-permute-start.25) | collective-permute-done | bytes 114720 | tf_op jit(solution)/shard_map/ppermute | solution.py:19
  109.3 4.0 %collective-permute-done.24.refs_7_ = bf16[16,3584]{1,0:T(8,128)(2,1)S(1)} collective-permute-done((bf16[16,3584]{1,0:T(8,128)(2,1)S(1)}, bf16[16,3584]{1,0:T(8,128)(2,1)S(1)}, u32[]{:S(2)}, u32[]{:S(2)}) %collective-permute-start.24) | collective-permute-done | bytes 114720 | tf_op jit(solution)/shard_map/ppermute | solution.py:19
  113.2 3.3 %experts_share.3 = (bf16[16,7168]{1,0:T(8,128)(2,1)S(1)}, bf16[16,7168]{1,0:T(8,128)(2,1)S(1)}, bf16[16,7168]{1,0:T(8,128)(2,1)S(1)}, bf16[16,7168]{1,0:T(8,128)...) custom-call(bf16[16,7168]{1,0:T(8,128)(2,1)S(1)} %add_convert_fusion, ...), custom_call_target="tpu_custom_call" | custom-call | flops 2818572288 | bytes 22020096 | tf_op jit(solution)/shard_map/experts_share/pallas_call | solution.py:293
  116.6 2.0 %collective-permute-start.26 = (bf16[16,3584]{1,0:T(8,128)(2,1)S(1)}, bf16[16,3584]{1,0:T(8,128)(2,1)S(1)}, u32[]{:S(2)}, u32[]{:S(2)}) collective-permute-start(bf16[16,3584]{1,0:T(8,128)(2,1)S(1)} %get-tuple-element.58), channel_id=1, source_target_pairs={{0,12},{1,13},{2,14},{3,15},{4,0},{5,1},{6,2},{7,3},{8,4},{9,5},{1... | collective-permute-start | bytes 344072 | tf_op jit(solution)/shard_map/ppermute | solution.py:19
  121.6 2.1 %collective-permute-done.26.left = bf16[16,3584]{1,0:T(8,128)(2,1)S(1)} collective-permute-done((bf16[16,3584]{1,0:T(8,128)(2,1)S(1)}, bf16[16,3584]{1,0:T(8,128)(2,1)S(1)}, u32[]{:S(2)}, u32[]{:S(2)}) %collective-permute-start.26) | collective-permute-done | bytes 114720 | tf_op jit(solution)/shard_map/ppermute | solution.py:19
  123.7 3.9 %collective-permute-done.27.right = bf16[16,3584]{1,0:T(8,128)(2,1)S(1)} collective-permute-done((bf16[16,3584]{1,0:T(8,128)(2,1)S(1)}, bf16[16,3584]{1,0:T(8,128)(2,1)S(1)}, u32[]{:S(2)}, u32[]{:S(2)}) %collective-permute-start.27) | collective-permute-done | bytes 114720 | tf_op jit(solution)/shard_map/ppermute | solution.py:19
  127.6 3.2 %collective-permute-start.32 = (bf16[16,7168]{1,0:T(8,128)(2,1)S(1)}, bf16[16,7168]{1,0:T(8,128)(2,1)S(1)}, u32[]{:S(2)}, u32[]{:S(2)}) collective-permute-start(bf16[16,7168]{1,0:T(8,128)(2,1)S(1)} %get-tuple-element.69), channel_id=1, source_target_pairs={{0,14},{1,15},{2,0},{3,1},{4,2},{5,3},{6,4},{7,5},{8,6},{9,7},{10,... | collective-permute-start | bytes 688136 | tf_op jit(solution)/shard_map/ppermute | solution.py:19
  132.8 6.6 %collective-permute-done.33.ahead = bf16[16,7168]{1,0:T(8,128)(2,1)S(1)} collective-permute-done((bf16[16,7168]{1,0:T(8,128)(2,1)S(1)}, bf16[16,7168]{1,0:T(8,128)(2,1)S(1)}, u32[]{:S(2)}, u32[]{:S(2)}) %collective-permute-start.33) | collective-permute-done | bytes 229408 | tf_op jit(solution)/shard_map/ppermute | solution.py:19
  139.7 7.9 %collective-permute-done.30 = bf16[16,7168]{1,0:T(8,128)(2,1)S(1)} collective-permute-done((bf16[16,7168]{1,0:T(8,128)(2,1)S(1)}, bf16[16,7168]{1,0:T(8,128)(2,1)S(1)}, u32[]{:S(2)}, u32[]{:S(2)}) %collective-permute-start.30) | collective-permute-done | bytes 229408 | tf_op jit(solution)/shard_map/ppermute | solution.py:36
  148.1 4.8 %collective-permute-done.34 = bf16[16,7168]{1,0:T(8,128)(2,1)S(1)} collective-permute-done((bf16[16,7168]{1,0:T(8,128)(2,1)S(1)}, bf16[16,7168]{1,0:T(8,128)(2,1)S(1)}, u32[]{:S(2)}, u32[]{:S(2)}) %collective-permute-start.34) | collective-permute-done | bytes 229408 | tf_op jit(solution)/shard_map/ppermute | solution.py:36
  (61 shorter events, 24.1 us)
Async XLA Ops:
  9.2 34.1 %collective-permute-start.8 = (bf16[21504,256]{1,0:T(8,128)(2,1)S(1)}, bf16[21504,256]{1,0:T(8,128)(2,1)S(1)}, u32[]{:S(2)}, u32[]{:S(2)}) collective-permute-start(bf16[21504,256]{1,0:T(8,128)(2,1)S(1)} %get-tuple-element.39.refs_10_), channel_id=1, source_target_pairs={{0,1},{1,0},{2,3},{3,2},{4,5},{5,4},{6,7},{7,6},{8,9},{9,8},{10,11... | collective-permute-start | bytes 33030152 | tf_op jit(solution)/shard_map/ppermute | solution.py:26
  9.3 14.4 %collective-permute-start.3 = (bf16[16,7296]{1,0:T(8,128)(2,1)S(1)}, bf16[16,7296]{1,0:T(8,128)(2,1)S(1)}, u32[]{:S(2)}, u32[]{:S(2)}) collective-permute-start(bf16[16,7296]{1,0:T(8,128)(2,1)S(1)} %get-tuple-element.38.refs_0_), channel_id=1, source_target_pairs={{0,12},{1,13},{2,14},{3,15},{4,0},{5,1},{6,2},{7,3},{8,4},{9,5},{1... | collective-permute-start | bytes 700424 | tf_op jit(solution)/shard_map/ppermute | solution.py:19
  13.9 15.0 %collective-permute-start.2 = (bf16[16,7296]{1,0:T(8,128)(2,1)S(1)}, bf16[16,7296]{1,0:T(8,128)(2,1)S(1)}, u32[]{:S(2)}, u32[]{:S(2)}) collective-permute-start(bf16[16,7296]{1,0:T(8,128)(2,1)S(1)} %get-tuple-element.38.refs_0_), channel_id=1, source_target_pairs={{0,4},{1,5},{2,6},{3,7},{4,8},{5,9},{6,10},{7,11},{8,12},{9,13},{1... | collective-permute-start | bytes 700424 | tf_op jit(solution)/shard_map/ppermute | solution.py:19
  13.9 17.1 %collective-permute-start.1 = (bf16[16,7296]{1,0:T(8,128)(2,1)S(1)}, bf16[16,7296]{1,0:T(8,128)(2,1)S(1)}, u32[]{:S(2)}, u32[]{:S(2)}) collective-permute-start(bf16[16,7296]{1,0:T(8,128)(2,1)S(1)} %get-tuple-element.38.refs_0_), channel_id=1, source_target_pairs={{0,14},{1,15},{2,0},{3,1},{4,2},{5,3},{6,4},{7,5},{8,6},{9,7},{10,... | collective-permute-start | bytes 700424 | tf_op jit(solution)/shard_map/ppermute | solution.py:19
  17.6 16.2 %collective-permute-start = (bf16[16,7296]{1,0:T(8,128)(2,1)S(1)}, bf16[16,7296]{1,0:T(8,128)(2,1)S(1)}, u32[]{:S(2)}, u32[]{:S(2)}) collective-permute-start(bf16[16,7296]{1,0:T(8,128)(2,1)S(1)} %get-tuple-element.38.refs_0_), channel_id=1, source_target_pairs={{0,2},{1,3},{2,4},{3,5},{4,6},{5,7},{6,8},{7,9},{8,10},{9,11},{10,... | collective-permute-start | bytes 700424 | tf_op jit(solution)/shard_map/ppermute | solution.py:19
  23.7 19.6 %collective-permute-start.5 = (bf16[16,7296]{1,0:T(8,128)(2,1)S(1)}, bf16[16,7296]{1,0:T(8,128)(2,1)S(1)}, u32[]{:S(2)}, u32[]{:S(2)}) collective-permute-start(bf16[16,7296]{1,0:T(8,128)(2,1)S(1)} %collective-permute-done.3.refs_4_), channel_id=1, source_target_pairs={{0,14},{1,15},{2,0},{3,1},{4,2},{5,3},{6,4},{7,5},{8,6},{9,7},{10,... | collective-permute-start | bytes 700424 | tf_op jit(solution)/shard_map/ppermute | solution.py:19
  28.9 14.3 %collective-permute-start.4 = (bf16[16,7296]{1,0:T(8,128)(2,1)S(1)}, bf16[16,7296]{1,0:T(8,128)(2,1)S(1)}, u32[]{:S(2)}, u32[]{:S(2)}) collective-permute-start(bf16[16,7296]{1,0:T(8,128)(2,1)S(1)} %collective-permute-done.2.refs_3_), channel_id=1, source_target_pairs={{0,2},{1,3},{2,4},{3,5},{4,6},{5,7},{6,8},{7,9},{8,10},{9,11},{10,... | collective-permute-start | bytes 700424 | tf_op jit(solution)/shard_map/ppermute | solution.py:19
  31.0 12.3 %collective-permute-start.7 = (bf16[16,3712]{1,0:T(8,128)(2,1)S(1)}, bf16[16,3712]{1,0:T(8,128)(2,1)S(1)}, u32[]{:S(2)}, u32[]{:S(2)}) collective-permute-start(bf16[16,3712]{1,0:T(8,128)(2,1)S(1)} %slice.17), channel_id=1, source_target_pairs={{0,12},{1,13},{2,14},{3,15},{4,0},{5,1},{6,2},{7,3},{8,4},{9,5},{1... | collective-permute-start | bytes 356360 | tf_op jit(solution)/shard_map/ppermute | solution.py:19
  33.9 9.4 %collective-permute-start.6 = (bf16[16,3584]{1,0:T(8,128)(2,1)S(1)}, bf16[16,3584]{1,0:T(8,128)(2,1)S(1)}, u32[]{:S(2)}, u32[]{:S(2)}) collective-permute-start(bf16[16,3584]{1,0:T(8,128)(2,1)S(1)} %slice.16), channel_id=1, source_target_pairs={{0,4},{1,5},{2,6},{3,7},{4,8},{5,9},{6,10},{7,11},{8,12},{9,13},{1... | collective-permute-start | bytes 344072 | tf_op jit(solution)/shard_map/ppermute | solution.py:19
  46.8 10.5 %collective-permute-start.10 = (bf16[16,3584]{1,0:T(8,128)(2,1)S(1)}, bf16[16,3584]{1,0:T(8,128)(2,1)S(1)}, u32[]{:S(2)}, u32[]{:S(2)}) collective-permute-start(bf16[16,3584]{1,0:T(8,128)(2,1)S(1)} %get-tuple-element.45), channel_id=1, source_target_pairs={{0,4},{1,5},{2,6},{3,7},{4,8},{5,9},{6,10},{7,11},{8,12},{9,13},{1... | collective-permute-start | bytes 344072 | tf_op jit(solution)/shard_map/ppermute | solution.py:19
  49.7 10.8 %collective-permute-start.11 = (bf16[16,7168]{1,0:T(8,128)(2,1)S(1)}, bf16[16,7168]{1,0:T(8,128)(2,1)S(1)}, u32[]{:S(2)}, u32[]{:S(2)}) collective-permute-start(bf16[16,7168]{1,0:T(8,128)(2,1)S(1)} %get-tuple-element.48), channel_id=1, source_target_pairs={{0,14},{1,15},{2,0},{3,1},{4,2},{5,3},{6,4},{7,5},{8,6},{9,7},{10,... | collective-permute-start | bytes 688136 | tf_op jit(solution)/shard_map/ppermute | solution.py:19
  51.2 10.4 %collective-permute-start.12 = (bf16[16,7168]{1,0:T(8,128)(2,1)S(1)}, bf16[16,7168]{1,0:T(8,128)(2,1)S(1)}, u32[]{:S(2)}, u32[]{:S(2)}) collective-permute-start(bf16[16,7168]{1,0:T(8,128)(2,1)S(1)} %get-tuple-element.49), channel_id=1, source_target_pairs={{0,2},{1,3},{2,4},{3,5},{4,6},{5,7},{6,8},{7,9},{8,10},{9,11},{10,... | collective-permute-start | bytes 688136 | tf_op jit(solution)/shard_map/ppermute | solution.py:19
  57.3 9.7 %collective-permute-start.16 = (bf16[16,7168]{1,0:T(8,128)(2,1)S(1)}, bf16[16,7168]{1,0:T(8,128)(2,1)S(1)}, u32[]{:S(2)}, u32[]{:S(2)}) collective-permute-start(bf16[16,7168]{1,0:T(8,128)(2,1)S(1)} %get-tuple-element.54), channel_id=1, source_target_pairs={{0,2},{1,3},{2,4},{3,5},{4,6},{5,7},{6,8},{7,9},{8,10},{9,11},{10,... | collective-permute-start | bytes 688136 | tf_op jit(solution)/shard_map/ppermute | solution.py:19
  57.3 13.7 %collective-permute-start.15 = (bf16[16,7168]{1,0:T(8,128)(2,1)S(1)}, bf16[16,7168]{1,0:T(8,128)(2,1)S(1)}, u32[]{:S(2)}, u32[]{:S(2)}) collective-permute-start(bf16[16,7168]{1,0:T(8,128)(2,1)S(1)} %get-tuple-element.53), channel_id=1, source_target_pairs={{0,14},{1,15},{2,0},{3,1},{4,2},{5,3},{6,4},{7,5},{8,6},{9,7},{10,... | collective-permute-start | bytes 688136 | tf_op jit(solution)/shard_map/ppermute | solution.py:19
  61.8 18.5 %collective-permute-start.13 = (bf16[16,7168]{1,0:T(8,128)(2,1)S(1)}, bf16[16,7168]{1,0:T(8,128)(2,1)S(1)}, u32[]{:S(2)}, u32[]{:S(2)}) collective-permute-start(bf16[16,7168]{1,0:T(8,128)(2,1)S(1)} %get-tuple-element.50), channel_id=1, source_target_pairs={{0,28},{1,29},{2,30},{3,31},{4,16},{5,17},{6,18},{7,19},{8,20},{9,... | collective-permute-start | bytes 688136 | tf_op jit(solution)/shard_map/ppermute | solution.py:36
  63.5 18.1 %collective-permute-start.14 = (bf16[16,7168]{1,0:T(8,128)(2,1)S(1)}, bf16[16,7168]{1,0:T(8,128)(2,1)S(1)}, u32[]{:S(2)}, u32[]{:S(2)}) collective-permute-start(bf16[16,7168]{1,0:T(8,128)(2,1)S(1)} %get-tuple-element.51), channel_id=1, source_target_pairs={{0,20},{1,21},{2,22},{3,23},{4,24},{5,25},{6,26},{7,27},{8,28},{9,... | collective-permute-start | bytes 688136 | tf_op jit(solution)/shard_map/ppermute | solution.py:36
  71.2 13.1 %collective-permute-start.17 = (bf16[16,7168]{1,0:T(8,128)(2,1)S(1)}, bf16[16,7168]{1,0:T(8,128)(2,1)S(1)}, u32[]{:S(2)}, u32[]{:S(2)}) collective-permute-start(bf16[16,7168]{1,0:T(8,128)(2,1)S(1)} %join_near.2), channel_id=1, source_target_pairs={{0,16},{1,17},{2,18},{3,19},{4,20},{5,21},{6,22},{7,23},{8,24},{9,... | collective-permute-start | bytes 688136 | tf_op jit(solution)/shard_map/ppermute | solution.py:36
  84.4 11.6 %collective-permute-start.21 = (bf16[16,7168]{1,0:T(8,128)(2,1)S(1)}, bf16[16,7168]{1,0:T(8,128)(2,1)S(1)}, u32[]{:S(2)}, u32[]{:S(2)}) collective-permute-start(bf16[16,7168]{1,0:T(8,128)(2,1)S(1)} %add_convert_fusion.1.refs_0_.state), channel_id=1, source_target_pairs={{0,12},{1,13},{2,14},{3,15},{4,0},{5,1},{6,2},{7,3},{8,4},{9,5},{1... | collective-permute-start | bytes 688136 | tf_op jit(solution)/shard_map/ppermute | solution.py:19
  85.8 13.7 %collective-permute-start.20 = (bf16[16,7168]{1,0:T(8,128)(2,1)S(1)}, bf16[16,7168]{1,0:T(8,128)(2,1)S(1)}, u32[]{:S(2)}, u32[]{:S(2)}) collective-permute-start(bf16[16,7168]{1,0:T(8,128)(2,1)S(1)} %add_convert_fusion.1.refs_0_.state), channel_id=1, source_target_pairs={{0,4},{1,5},{2,6},{3,7},{4,8},{5,9},{6,10},{7,11},{8,12},{9,13},{1... | collective-permute-start | bytes 688136 | tf_op jit(solution)/shard_map/ppermute | solution.py:19
  87.4 14.7 %collective-permute-start.19 = (bf16[16,7168]{1,0:T(8,128)(2,1)S(1)}, bf16[16,7168]{1,0:T(8,128)(2,1)S(1)}, u32[]{:S(2)}, u32[]{:S(2)}) collective-permute-start(bf16[16,7168]{1,0:T(8,128)(2,1)S(1)} %add_convert_fusion.1.refs_0_.state), channel_id=1, source_target_pairs={{0,14},{1,15},{2,0},{3,1},{4,2},{5,3},{6,4},{7,5},{8,6},{9,7},{10,... | collective-permute-start | bytes 688136 | tf_op jit(solution)/shard_map/ppermute | solution.py:19
  89.1 15.7 %collective-permute-start.18 = (bf16[16,7168]{1,0:T(8,128)(2,1)S(1)}, bf16[16,7168]{1,0:T(8,128)(2,1)S(1)}, u32[]{:S(2)}, u32[]{:S(2)}) collective-permute-start(bf16[16,7168]{1,0:T(8,128)(2,1)S(1)} %add_convert_fusion.1.refs_0_.state), channel_id=1, source_target_pairs={{0,2},{1,3},{2,4},{3,5},{4,6},{5,7},{6,8},{7,9},{8,10},{9,11},{10,... | collective-permute-start | bytes 688136 | tf_op jit(solution)/shard_map/ppermute | solution.py:19
  96.0 17.2 %collective-permute-start.23 = (bf16[16,7168]{1,0:T(8,128)(2,1)S(1)}, bf16[16,7168]{1,0:T(8,128)(2,1)S(1)}, u32[]{:S(2)}, u32[]{:S(2)}) collective-permute-start(bf16[16,7168]{1,0:T(8,128)(2,1)S(1)} %collective-permute-done.21.refs_4_), channel_id=1, source_target_pairs={{0,14},{1,15},{2,0},{3,1},{4,2},{5,3},{6,4},{7,5},{8,6},{9,7},{10,... | collective-permute-start | bytes 688136 | tf_op jit(solution)/shard_map/ppermute | solution.py:19
  99.4 13.8 %collective-permute-start.22 = (bf16[16,7168]{1,0:T(8,128)(2,1)S(1)}, bf16[16,7168]{1,0:T(8,128)(2,1)S(1)}, u32[]{:S(2)}, u32[]{:S(2)}) collective-permute-start(bf16[16,7168]{1,0:T(8,128)(2,1)S(1)} %collective-permute-done.20.refs_3_), channel_id=1, source_target_pairs={{0,2},{1,3},{2,4},{3,5},{4,6},{5,7},{6,8},{7,9},{8,10},{9,11},{10,... | collective-permute-start | bytes 688136 | tf_op jit(solution)/shard_map/ppermute | solution.py:19
  102.1 11.2 %collective-permute-start.24 = (bf16[16,3584]{1,0:T(8,128)(2,1)S(1)}, bf16[16,3584]{1,0:T(8,128)(2,1)S(1)}, u32[]{:S(2)}, u32[]{:S(2)}) collective-permute-start(bf16[16,3584]{1,0:T(8,128)(2,1)S(1)} %slice.18), channel_id=1, source_target_pairs={{0,4},{1,5},{2,6},{3,7},{4,8},{5,9},{6,10},{7,11},{8,12},{9,13},{1... | collective-permute-start | bytes 344072 | tf_op jit(solution)/shard_map/ppermute | solution.py:19
  118.6 9.0 %collective-permute-start.27 = (bf16[16,3584]{1,0:T(8,128)(2,1)S(1)}, bf16[16,3584]{1,0:T(8,128)(2,1)S(1)}, u32[]{:S(2)}, u32[]{:S(2)}) collective-permute-start(bf16[16,3584]{1,0:T(8,128)(2,1)S(1)} %get-tuple-element.61), channel_id=1, source_target_pairs={{0,4},{1,5},{2,6},{3,7},{4,8},{5,9},{6,10},{7,11},{8,12},{9,13},{1... | collective-permute-start | bytes 344072 | tf_op jit(solution)/shard_map/ppermute | solution.py:19
  119.6 11.3 %collective-permute-start.28 = (bf16[16,7168]{1,0:T(8,128)(2,1)S(1)}, bf16[16,7168]{1,0:T(8,128)(2,1)S(1)}, u32[]{:S(2)}, u32[]{:S(2)}) collective-permute-start(bf16[16,7168]{1,0:T(8,128)(2,1)S(1)} %get-tuple-element.64), channel_id=1, source_target_pairs={{0,14},{1,15},{2,0},{3,1},{4,2},{5,3},{6,4},{7,5},{8,6},{9,7},{10,... | collective-permute-start | bytes 688136 | tf_op jit(solution)/shard_map/ppermute | solution.py:19
  120.0 11.1 %collective-permute-start.29 = (bf16[16,7168]{1,0:T(8,128)(2,1)S(1)}, bf16[16,7168]{1,0:T(8,128)(2,1)S(1)}, u32[]{:S(2)}, u32[]{:S(2)}) collective-permute-start(bf16[16,7168]{1,0:T(8,128)(2,1)S(1)} %get-tuple-element.65), channel_id=1, source_target_pairs={{0,2},{1,3},{2,4},{3,5},{4,6},{5,7},{6,8},{7,9},{8,10},{9,11},{10,... | collective-permute-start | bytes 688136 | tf_op jit(solution)/shard_map/ppermute | solution.py:19
  127.6 11.8 %collective-permute-start.33 = (bf16[16,7168]{1,0:T(8,128)(2,1)S(1)}, bf16[16,7168]{1,0:T(8,128)(2,1)S(1)}, u32[]{:S(2)}, u32[]{:S(2)}) collective-permute-start(bf16[16,7168]{1,0:T(8,128)(2,1)S(1)} %get-tuple-element.70), channel_id=1, source_target_pairs={{0,2},{1,3},{2,4},{3,5},{4,6},{5,7},{6,8},{7,9},{8,10},{9,11},{10,... | collective-permute-start | bytes 688136 | tf_op jit(solution)/shard_map/ppermute | solution.py:19
  127.6 11.8 %collective-permute-start.32 = (bf16[16,7168]{1,0:T(8,128)(2,1)S(1)}, bf16[16,7168]{1,0:T(8,128)(2,1)S(1)}, u32[]{:S(2)}, u32[]{:S(2)}) collective-permute-start(bf16[16,7168]{1,0:T(8,128)(2,1)S(1)} %get-tuple-element.69), channel_id=1, source_target_pairs={{0,14},{1,15},{2,0},{3,1},{4,2},{5,3},{6,4},{7,5},{8,6},{9,7},{10,... | collective-permute-start | bytes 688136 | tf_op jit(solution)/shard_map/ppermute | solution.py:19
  131.3 16.4 %collective-permute-start.30 = (bf16[16,7168]{1,0:T(8,128)(2,1)S(1)}, bf16[16,7168]{1,0:T(8,128)(2,1)S(1)}, u32[]{:S(2)}, u32[]{:S(2)}) collective-permute-start(bf16[16,7168]{1,0:T(8,128)(2,1)S(1)} %get-tuple-element.66), channel_id=1, source_target_pairs={{0,28},{1,29},{2,30},{3,31},{4,16},{5,17},{6,18},{7,19},{8,20},{9,... | collective-permute-start | bytes 688136 | tf_op jit(solution)/shard_map/ppermute | solution.py:36
  131.5 16.6 %collective-permute-start.31 = (bf16[16,7168]{1,0:T(8,128)(2,1)S(1)}, bf16[16,7168]{1,0:T(8,128)(2,1)S(1)}, u32[]{:S(2)}, u32[]{:S(2)}) collective-permute-start(bf16[16,7168]{1,0:T(8,128)(2,1)S(1)} %get-tuple-element.67), channel_id=1, source_target_pairs={{0,20},{1,21},{2,22},{3,23},{4,24},{5,25},{6,26},{7,27},{8,28},{9,... | collective-permute-start | bytes 688136 | tf_op jit(solution)/shard_map/ppermute | solution.py:36
  139.6 13.3 %collective-permute-start.34 = (bf16[16,7168]{1,0:T(8,128)(2,1)S(1)}, bf16[16,7168]{1,0:T(8,128)(2,1)S(1)}, u32[]{:S(2)}, u32[]{:S(2)}) collective-permute-start(bf16[16,7168]{1,0:T(8,128)(2,1)S(1)} %join_near.3), channel_id=1, source_target_pairs={{0,16},{1,17},{2,18},{3,19},{4,20},{5,21},{6,22},{7,23},{8,24},{9,... | collective-permute-start | bytes 688136 | tf_op jit(solution)/shard_map/ppermute | solution.py:36
  (6 other events, 102.4 us)

commit v2 on v1

--- a/solution.py
+++ b/solution.py
@@ -56,7 +56,7 @@
     ]
 
 
-def sum_to_next(state, outs):
+def sum_to_next(outs):
     far = [
         along_z(outs[7], -2),
         along_z(outs[8], 2),
@@ -65,24 +65,14 @@
     ]
     far[0], near_back = lax.optimization_barrier((far[0], outs[1]))
     far[1], near_ahead = lax.optimization_barrier((far[1], outs[2]))
-    near = [along_z(near_back, -1), along_z(near_ahead, 1)]
+    parts = [
+        to_next_section(outs[0], 0),
+        to_next_section(near_back, -1),
+        to_next_section(near_ahead, 1),
+    ]
     back, ahead = join_far(outs[3], outs[4], *far)
-    parts = [to_next_section(back, -2), to_next_section(ahead, 2)]
-    parts.append(to_next_section(join_near(state, outs[0], *near), 0))
+    parts += [to_next_section(back, -2), to_next_section(ahead, 2)]
     return sum(part.astype(F32) for part in parts).astype(BF16)
-
-
-def join_call(kernel, name, n_out, *operands):
-    rows, width = operands[0].shape
-    return pl.pallas_call(
-        kernel,
-        out_shape=[jax.ShapeDtypeStruct((rows, width), BF16)] * n_out,
-        compiler_params=pltpu.CompilerParams(vmem_limit_bytes=VMEM_LIMIT),
-        cost_estimate=pl.CostEstimate(
-            flops=4 * rows * width, bytes_accessed=12 * rows * width, transcendentals=0
-        ),
-        name=name,
-    )(*operands)
 
 
 def join_far(back, ahead, left, right, back_3, ahead_3):
@@ -97,15 +87,16 @@
         ahead_out[:, lo] = (f(ahead, lo) + f(a3, lo)).astype(BF16)
         ahead_out[:, hi] = (f(ahead, hi) + f(a3, hi) + right[...].astype(F32)).astype(BF16)
 
-    return join_call(kernel, "join_far", 2, back, ahead, left, right, back_3, ahead_3)
-
-
-def join_near(state, own, back, ahead):
-    def kernel(state, own, back, ahead, out):
-        f = lambda ref: ref[...].astype(F32)
-        out[...] = (f(state) + (f(own) + f(back) + f(ahead))).astype(BF16)
-
-    return join_call(kernel, "join_near", 1, state, own, back, ahead)[0]
+    rows = back.shape[0]
+    return pl.pallas_call(
+        kernel,
+        out_shape=[jax.ShapeDtypeStruct((rows, width), BF16)] * 2,
+        compiler_params=pltpu.CompilerParams(vmem_limit_bytes=VMEM_LIMIT),
+        cost_estimate=pl.CostEstimate(
+            flops=6 * rows * width, bytes_accessed=14 * rows * width, transcendentals=0
+        ),
+        name="join_far",
+    )(back, ahead, left, right, back_3, ahead_3)
 
 
 def load_rows(pieces, gain, rows_ref, squares_ref):
@@ -147,12 +138,12 @@
 def prepare(tokens, routes, route_weights, exponents, arrays, experts):
     height = tokens.shape[0]
     side, width = min(arrays[0].shape), max(arrays[0].shape)
-    per_block, blocks, strips = side // LANES, width // side, width // LANES
+    per_block, blocks = side // LANES, width // side
     group = max(n for n in (1, 2, 4) if blocks % n == 0)
     groups = [(n, at) for n in range(len(arrays)) for at in range(0, blocks, group)]
 
     def kernel(exp_ref, tokens_ref, routes_ref, route_weights_ref, *refs):
-        ins, rows_out, out_ref, sems = refs[: len(arrays)], *refs[len(arrays) :]
+        ins, rows_out, out_ref, sems, rows_sem = refs[: len(arrays)], *refs[len(arrays) :]
 
         def copies(n, at):
             if ins[n].shape[0] == width:
@@ -174,44 +165,44 @@
                 for a in range(per_block):
                     for b in range(per_block):
                         along, across = (a, b) if tall else (b, a)
-                        strip = n * strips + j * per_block + along
-                        exponent = exp_ref[strip * per_block + across]
+                        strip = j * per_block + along
+                        exponent = exp_ref[n, across, strip]
                         factor = jnp.left_shift(1, exponent + 16).astype(F32) * 2.0**-16
                         row = n * width + j * side + a * LANES
                         place = (slice(row, row + LANES), slice(b * LANES, (b + 1) * LANES))
                         out_ref[place] = scaled(out_ref[place], factor)
 
+        rows_copy = pltpu.make_async_copy(tokens_ref, rows_out.at[:, pl.ds(0, width)], rows_sem)
+        rows_copy.start()
         for n in range(len(groups) + AHEAD):
             if n < len(groups):
                 for copy in copies(*groups[n]):
                     copy.start()
             if n == AHEAD:
-                lane = lax.broadcasted_iota(jnp.int32, (height, LANES), 1)
-                table = jnp.zeros((height, LANES), F32)
+                lane = lax.broadcasted_iota(jnp.int32, (LANES, height), 0)
+                table = jnp.zeros((LANES, height), F32)
                 for step in range(TICKS):
-                    for k in range(routes.shape[-1]):
-                        named = routes_ref[step, :, k : k + 1] + step * experts
-                        weight = route_weights_ref[step, :, k : k + 1].astype(F32)
+                    for k in range(routes.shape[1]):
+                        named = routes_ref[step, k : k + 1, :] + step * experts
+                        weight = route_weights_ref[step].astype(F32)[k : k + 1, :]
                         table += jnp.where(lane == named, weight, 0.0)
-                rows_out[:, :width] = tokens_ref[...]
-                rows_out[:, width:] = table.astype(BF16)
+                rows_out[:, width:] = table.T.astype(BF16)
             if n >= AHEAD:
                 for copy in copies(*groups[n - AHEAD]):
                     copy.wait()
                 scale(*groups[n - AHEAD])
-
-    vmem = pl.BlockSpec(memory_space=pltpu.VMEM)
+        rows_copy.wait()
+
+    vmem, hbm = (pl.BlockSpec(memory_space=space) for space in (pltpu.VMEM, pltpu.HBM))
     return pl.pallas_call(
         kernel,
-        in_specs=[pl.BlockSpec(memory_space=pltpu.SMEM)]
-        + [vmem] * 3
-        + [pl.BlockSpec(memory_space=pltpu.HBM)] * len(arrays),
+        in_specs=[pl.BlockSpec(memory_space=pltpu.SMEM), hbm, vmem, vmem] + [hbm] * len(arrays),
         out_specs=[vmem] * 2,
         out_shape=[
             jax.ShapeDtypeStruct((height, width + LANES), BF16),
             jax.ShapeDtypeStruct((len(arrays) * width, side), BF16),
         ],
-        scratch_shapes=[pltpu.SemaphoreType.DMA((len(arrays), blocks))],
+        scratch_shapes=[pltpu.SemaphoreType.DMA((len(arrays), blocks)), pltpu.SemaphoreType.DMA],
         compiler_params=pltpu.CompilerParams(vmem_limit_bytes=VMEM_LIMIT),
         cost_estimate=pl.CostEstimate(
             flops=len(arrays) * width * side,
@@ -221,7 +212,7 @@
         name="prepare",
     )(
         exponents,
-        tokens,
+        pltpu.with_memory_space_constraint(tokens, pltpu.HBM),
         routes,
         route_weights,
         *(pltpu.with_memory_space_constraint(w, pltpu.HBM) for w in arrays),
@@ -275,9 +266,12 @@
                 )
                 for core, ref in enumerate(cores)
             )
-            product = (product * weight).astype(BF16)
+            product = product * weight
             hi = lo + side
-            for n in range(7):
+            kept = ins[0][:, lo:hi].astype(F32) + product[:height, :]
+            outs[0][:, lo:hi] = kept.astype(BF16)
+            product = product.astype(BF16)
+            for n in range(1, 7):
                 outs[n][:, lo:hi] = product[n * height : (n + 1) * height, :]
             last = product[7 * height :, :]
             if lo < cut:
@@ -316,12 +310,11 @@
     tokens, norm_gain, gate_weight, up_weight, down_weight, block_scales, routes, route_weights
 ):
     experts = lax.axis_size("expert") // SPLIT
-    state = tokens[0]
     rows, own = prepare(
-        state,
-        routes[0],
-        route_weights[0],
-        block_scales[0].reshape(-1),
+        tokens[0],
+        routes[0].transpose(0, 2, 1),
+        route_weights[0].transpose(0, 2, 1),
+        block_scales[0].transpose(0, 2, 1),
         (gate_weight[0], up_weight[0], down_weight[0]),
         experts,
     )
@@ -333,8 +326,8 @@
         outs, held_table = experts_share(
             pieces, norm_gain, weights, held_table, tick * experts
         )
-        rows = state = sum_to_next(state, outs)
-    return state[None]
+        rows = sum_to_next(outs)
+    return rows[None]
 
 
 def solution(mesh):

time: 157 us -> 161 us (1.025); the launches traced: 154 us -> 161 us
  starting transfers between devices: 56.2 us -> 65 us
    ppermute x28 -> x24, waiting for transfers between devices: 56 us -> 40.8 us  [along_z(): lax.ppermute(shard, 'expert', [(i, (i + 2 * by) % length) for i in range(...]
    ppermute x6 -> x10, waiting for transfers between devices: 23.9 us -> 38.7 us  [to_next_section(): return lax.ppermute(shard, ('section', 'expert'), pairs)]
    ppermute x6 -> x10, starting transfers between devices: 9.31 us -> 17.8 us  [to_next_section(): return lax.ppermute(shard, ('section', 'expert'), pairs)]
    ppermute x28 -> x24, starting transfers between devices: 46.8 us -> 47.1 us  [along_z(): lax.ppermute(shard, 'expert', [(i, (i + 2 * by) % length) for i in range(...]
    pallas_call x5 -> x3, Pallas kernels: 6.27 us -> 6.14 us  [the longest x1 5.85 us: prepare(): pl.pallas_call(kernel, in_specs=[pl.BlockSpec(memory_space=pltpu.SMEM), h...]
  transfers between devices with their start and end apart: 35 -> 35, of which waited for: 23 -> 16; matrix products, arithmetic and copies ran while one was open for 0% -> 0% of each run, Pallas kernels for 0% -> 0%
where the time goes in v2:
time: 161 us
  waiting for transfers between devices  79.5 us (49%)
  starting transfers between devices  65 us (40%)
  Pallas kernels  12.9 us (8%)
  local copies, waits for them, and re-layouts  2.08 us (1%)
    ppermute x24, starting transfers between devices, along_z(): lax.ppermute(shard, 'expert', [(i, (i + 2 * by) % length) for i in range(...  47.1 us
    ppermute x24, waiting for transfers between devices, along_z(): lax.ppermute(shard, 'expert', [(i, (i + 2 * by) % length) for i in range(...  40.8 us
    ppermute x10, waiting for transfers between devices, to_next_section(): return lax.ppermute(shard, ('section', 'expert'), pairs)  38.7 us
    ppermute x10, starting transfers between devices, to_next_section(): return lax.ppermute(shard, ('section', 'expert'), pairs)  17.8 us
    pallas_call x2, Pallas kernels, experts_share(): pl.pallas_call(kernel, in_specs=[vmem] * len(operands), out_specs=[vmem]...  6.76 us
    pallas_call x1, Pallas kernels, prepare(): pl.pallas_call(kernel, in_specs=[pl.BlockSpec(memory_space=pltpu.SMEM), h...  5.85 us
  transfers between devices with their start and end apart: 35, of which 16 were waited for; matrix products, arithmetic and copies ran while one was open for 0% of the time, Pallas kernels for 0%

profile of v2, /device:TPU:0, one launch (start us, length us, event | category | flops | bytes accessed | tf_op | source)
XLA Modules:
  0.0 160.6 jit_solution(1519849282370484960)
XLA Ops:
  2.0 5.8 %prepare.1 = (bf16[16,7296]{1,0:T(8,128)(2,1)S(1)}, bf16[21504,256]{1,0:T(8,128)(2,1)S(1)}) custom-call(s32[3,2,56]{2,1,0:T(2,128)S(1)} %bitcast.15, bf16[16,7168]{1,0:T(8,128)(2,1)} %bitcast.21, s32[2,2,16]{2,1,0:T(2,128)S(1)} %bitcast.16, bf16[2,2,16]{2,1,0:T(2,128)(2,1)S(1)} %bitcast.17, bf16[7168,256]{1,0:T(8,128)(2,1)} %bitcast.18, ...), custom_call_target="tpu_custom_call" | custom-call | flops 5505024 | bytes 22020096 | tf_op jit(solution)/shard_map/prepare/pallas_call | solution.py:197
  8.0 4.6 %collective-permute-start.3 = (bf16[16,7296]{1,0:T(8,128)(2,1)S(1)}, bf16[16,7296]{1,0:T(8,128)(2,1)S(1)}, u32[]{:S(2)}, u32[]{:S(2)}) collective-permute-start(bf16[16,7296]{1,0:T(8,128)(2,1)S(1)} %get-tuple-element.38.refs_0_), channel_id=1, source_target_pairs={{0,12},{1,13},{2,14},{3,15},{4,0},{5,1},{6,2},{7,3},{8,4},{9,5},{1... | collective-permute-start | bytes 700424 | tf_op jit(solution)/shard_map/ppermute | solution.py:19
  12.7 3.7 %collective-permute-start.1 = (bf16[16,7296]{1,0:T(8,128)(2,1)S(1)}, bf16[16,7296]{1,0:T(8,128)(2,1)S(1)}, u32[]{:S(2)}, u32[]{:S(2)}) collective-permute-start(bf16[16,7296]{1,0:T(8,128)(2,1)S(1)} %get-tuple-element.38.refs_0_), channel_id=1, source_target_pairs={{0,14},{1,15},{2,0},{3,1},{4,2},{5,3},{6,4},{7,5},{8,6},{9,7},{10,... | collective-permute-start | bytes 700424 | tf_op jit(solution)/shard_map/ppermute | solution.py:19
  16.3 6.0 %collective-permute-done.3.refs_4_ = bf16[16,7296]{1,0:T(8,128)(2,1)S(1)} collective-permute-done((bf16[16,7296]{1,0:T(8,128)(2,1)S(1)}, bf16[16,7296]{1,0:T(8,128)(2,1)S(1)}, u32[]{:S(2)}, u32[]{:S(2)}) %collective-permute-start.3) | collective-permute-done | bytes 233504 | tf_op jit(solution)/shard_map/ppermute | solution.py:19
  22.4 5.0 %collective-permute-start.5 = (bf16[16,7296]{1,0:T(8,128)(2,1)S(1)}, bf16[16,7296]{1,0:T(8,128)(2,1)S(1)}, u32[]{:S(2)}, u32[]{:S(2)}) collective-permute-start(bf16[16,7296]{1,0:T(8,128)(2,1)S(1)} %collective-permute-done.3.refs_4_), channel_id=1, source_target_pairs={{0,14},{1,15},{2,0},{3,1},{4,2},{5,3},{6,4},{7,5},{8,6},{9,7},{10,... | collective-permute-start | bytes 700424 | tf_op jit(solution)/shard_map/ppermute | solution.py:19
  29.7 2.0 %collective-permute-start.7 = (bf16[16,3712]{1,0:T(8,128)(2,1)S(1)}, bf16[16,3712]{1,0:T(8,128)(2,1)S(1)}, u32[]{:S(2)}, u32[]{:S(2)}) collective-permute-start(bf16[16,3712]{1,0:T(8,128)(2,1)S(1)} %slice.17), channel_id=1, source_target_pairs={{0,12},{1,13},{2,14},{3,15},{4,0},{5,1},{6,2},{7,3},{8,4},{9,5},{1... | collective-permute-start | bytes 356360 | tf_op jit(solution)/shard_map/ppermute | solution.py:19
  32.9 9.1 %collective-permute-done.6.refs_7_ = bf16[16,3584]{1,0:T(8,128)(2,1)S(1)} collective-permute-done((bf16[16,3584]{1,0:T(8,128)(2,1)S(1)}, bf16[16,3584]{1,0:T(8,128)(2,1)S(1)}, u32[]{:S(2)}, u32[]{:S(2)}) %collective-permute-start.6) | collective-permute-done | bytes 114720 | tf_op jit(solution)/shard_map/ppermute | solution.py:19
  42.0 3.4 %experts_share.2 = (bf16[16,7168]{1,0:T(8,128)(2,1)S(1)}, bf16[16,7168]{1,0:T(8,128)(2,1)S(1)}, bf16[16,7168]{1,0:T(8,128)(2,1)S(1)}, bf16[16,7168]{1,0:T(8,128)...) custom-call(bf16[16,7296]{1,0:T(8,128)(2,1)S(1)} %get-tuple-element., ...), custom_call_target="tpu_custom_call" | custom-call | flops 2818572288 | bytes 22020096 | tf_op jit(solution)/shard_map/experts_share/pallas_call | solution.py:287
  45.8 1.8 %collective-permute-start.15 = (bf16[16,7168]{1,0:T(8,128)(2,1)S(1)}, bf16[16,7168]{1,0:T(8,128)(2,1)S(1)}, u32[]{:S(2)}, u32[]{:S(2)}) collective-permute-start(bf16[16,7168]{1,0:T(8,128)(2,1)S(1)} %get-tuple-element.52), channel_id=1, source_target_pairs={{0,2},{1,3},{2,4},{3,5},{4,6},{5,7},{6,8},{7,9},{8,10},{9,11},{10,... | collective-permute-start | bytes 688136 | tf_op jit(solution)/shard_map/ppermute | solution.py:19
  47.6 2.9 %collective-permute-start.12 = (bf16[16,3584]{1,0:T(8,128)(2,1)S(1)}, bf16[16,3584]{1,0:T(8,128)(2,1)S(1)}, u32[]{:S(2)}, u32[]{:S(2)}) collective-permute-start(bf16[16,3584]{1,0:T(8,128)(2,1)S(1)} %get-tuple-element.44), channel_id=1, source_target_pairs={{0,4},{1,5},{2,6},{3,7},{4,8},{5,9},{6,10},{7,11},{8,12},{9,13},{1... | collective-permute-start | bytes 344072 | tf_op jit(solution)/shard_map/ppermute | solution.py:19
  50.5 1.6 collective-permute-start.9
  52.1 6.1 %collective-permute-done.10.left = bf16[16,3584]{1,0:T(8,128)(2,1)S(1)} collective-permute-done((bf16[16,3584]{1,0:T(8,128)(2,1)S(1)}, bf16[16,3584]{1,0:T(8,128)(2,1)S(1)}, u32[]{:S(2)}, u32[]{:S(2)}) %collective-permute-start.10) | collective-permute-done | bytes 114720 | tf_op jit(solution)/shard_map/ppermute | solution.py:19
  58.2 3.1 %collective-permute-start.13 = (bf16[16,7168]{1,0:T(8,128)(2,1)S(1)}, bf16[16,7168]{1,0:T(8,128)(2,1)S(1)}, u32[]{:S(2)}, u32[]{:S(2)}) collective-permute-start(bf16[16,7168]{1,0:T(8,128)(2,1)S(1)} %get-tuple-element.46), channel_id=1, source_target_pairs={{0,18},{1,19},{2,20},{3,21},{4,22},{5,23},{6,24},{7,25},{8,26},{9,... | collective-permute-start | bytes 688136 | tf_op jit(solution)/shard_map/ppermute | solution.py:36
  61.2 2.2 %collective-permute-start.11 = (bf16[16,7168]{1,0:T(8,128)(2,1)S(1)}, bf16[16,7168]{1,0:T(8,128)(2,1)S(1)}, u32[]{:S(2)}, u32[]{:S(2)}) collective-permute-start(bf16[16,7168]{1,0:T(8,128)(2,1)S(1)} %get-tuple-element.43), channel_id=1, source_target_pairs={{0,30},{1,31},{2,16},{3,17},{4,18},{5,19},{6,20},{7,21},{8,22},{9,... | collective-permute-start | bytes 688136 | tf_op jit(solution)/shard_map/ppermute | solution.py:36
  64.9 3.0 %collective-permute-start.17 = (bf16[16,7168]{1,0:T(8,128)(2,1)S(1)}, bf16[16,7168]{1,0:T(8,128)(2,1)S(1)}, u32[]{:S(2)}, u32[]{:S(2)}) collective-permute-start(bf16[16,7168]{1,0:T(8,128)(2,1)S(1)} %get-tuple-element.54), channel_id=1, source_target_pairs={{0,20},{1,21},{2,22},{3,23},{4,24},{5,25},{6,26},{7,27},{8,28},{9,... | collective-permute-start | bytes 688136 | tf_op jit(solution)/shard_map/ppermute | solution.py:36
  67.9 9.0 %collective-permute-done.13 = bf16[16,7168]{1,0:T(8,128)(2,1)S(1)} collective-permute-done((bf16[16,7168]{1,0:T(8,128)(2,1)S(1)}, bf16[16,7168]{1,0:T(8,128)(2,1)S(1)}, u32[]{:S(2)}, u32[]{:S(2)}) %collective-permute-start.13) | collective-permute-done | bytes 229408 | tf_op jit(solution)/shard_map/ppermute | solution.py:36
  76.9 8.9 %collective-permute-done.11 = bf16[16,7168]{1,0:T(8,128)(2,1)S(1)} collective-permute-done((bf16[16,7168]{1,0:T(8,128)(2,1)S(1)}, bf16[16,7168]{1,0:T(8,128)(2,1)S(1)}, u32[]{:S(2)}, u32[]{:S(2)}) %collective-permute-start.11) | collective-permute-done | bytes 229408 | tf_op jit(solution)/shard_map/ppermute | solution.py:36
  86.0 2.9 %collective-permute-start.20 = (bf16[16,7168]{1,0:T(8,128)(2,1)S(1)}, bf16[16,7168]{1,0:T(8,128)(2,1)S(1)}, u32[]{:S(2)}, u32[]{:S(2)}) collective-permute-start(bf16[16,7168]{1,0:T(8,128)(2,1)S(1)} %add_convert_fusion.1.refs_0_), channel_id=1, source_target_pairs={{0,4},{1,5},{2,6},{3,7},{4,8},{5,9},{6,10},{7,11},{8,12},{9,13},{1... | collective-permute-start | bytes 688136 | tf_op jit(solution)/shard_map/ppermute | solution.py:19
  88.9 9.0 %collective-permute-start.19 = (bf16[16,7168]{1,0:T(8,128)(2,1)S(1)}, bf16[16,7168]{1,0:T(8,128)(2,1)S(1)}, u32[]{:S(2)}, u32[]{:S(2)}) collective-permute-start(bf16[16,7168]{1,0:T(8,128)(2,1)S(1)} %add_convert_fusion.1.refs_0_), channel_id=1, source_target_pairs={{0,14},{1,15},{2,0},{3,1},{4,2},{5,3},{6,4},{7,5},{8,6},{9,7},{10,... | collective-permute-start | bytes 688136 | tf_op jit(solution)/shard_map/ppermute | solution.py:19
  98.0 6.6 %collective-permute-start.23 = (bf16[16,7168]{1,0:T(8,128)(2,1)S(1)}, bf16[16,7168]{1,0:T(8,128)(2,1)S(1)}, u32[]{:S(2)}, u32[]{:S(2)}) collective-permute-start(bf16[16,7168]{1,0:T(8,128)(2,1)S(1)} %collective-permute-done.21.refs_4_), channel_id=1, source_target_pairs={{0,14},{1,15},{2,0},{3,1},{4,2},{5,3},{6,4},{7,5},{8,6},{9,7},{10,... | collective-permute-start | bytes 688136 | tf_op jit(solution)/shard_map/ppermute | solution.py:19
  106.1 1.8 %collective-permute-done.19.refs_2_ = bf16[16,7168]{1,0:T(8,128)(2,1)S(1)} collective-permute-done((bf16[16,7168]{1,0:T(8,128)(2,1)S(1)}, bf16[16,7168]{1,0:T(8,128)(2,1)S(1)}, u32[]{:S(2)}, u32[]{:S(2)}) %collective-permute-start.19) | collective-permute-done | bytes 229408 | tf_op jit(solution)/shard_map/ppermute | solution.py:19
  107.9 3.7 %collective-permute-done.25.refs_8_ = bf16[16,3584]{1,0:T(8,128)(2,1)S(1)} collective-permute-done((bf16[16,3584]{1,0:T(8,128)(2,1)S(1)}, bf16[16,3584]{1,0:T(8,128)(2,1)S(1)}, u32[]{:S(2)}, u32[]{:S(2)}) %collective-permute-start.25) | collective-permute-done | bytes 114720 | tf_op jit(solution)/shard_map/ppermute | solution.py:19
  111.6 4.4 %collective-permute-done.24.refs_7_ = bf16[16,3584]{1,0:T(8,128)(2,1)S(1)} collective-permute-done((bf16[16,3584]{1,0:T(8,128)(2,1)S(1)}, bf16[16,3584]{1,0:T(8,128)(2,1)S(1)}, u32[]{:S(2)}, u32[]{:S(2)}) %collective-permute-start.24) | collective-permute-done | bytes 114720 | tf_op jit(solution)/shard_map/ppermute | solution.py:19
  116.1 3.3 %experts_share.3 = (bf16[16,7168]{1,0:T(8,128)(2,1)S(1)}, bf16[16,7168]{1,0:T(8,128)(2,1)S(1)}, bf16[16,7168]{1,0:T(8,128)(2,1)S(1)}, bf16[16,7168]{1,0:T(8,128)...) custom-call(bf16[16,7168]{1,0:T(8,128)(2,1)S(1)} %add_convert_fusion, ...), custom_call_target="tpu_custom_call" | custom-call | flops 2818572288 | bytes 22020096 | tf_op jit(solution)/shard_map/experts_share/pallas_call | solution.py:287
  119.4 1.7 %collective-permute-start.31 = (bf16[16,7168]{1,0:T(8,128)(2,1)S(1)}, bf16[16,7168]{1,0:T(8,128)(2,1)S(1)}, u32[]{:S(2)}, u32[]{:S(2)}) collective-permute-start(bf16[16,7168]{1,0:T(8,128)(2,1)S(1)} %get-tuple-element.67), channel_id=1, source_target_pairs={{0,14},{1,15},{2,0},{3,1},{4,2},{5,3},{6,4},{7,5},{8,6},{9,7},{10,... | collective-permute-start | bytes 688136 | tf_op jit(solution)/shard_map/ppermute | solution.py:19
  122.7 1.7 %collective-permute-start.29 = (bf16[16,3584]{1,0:T(8,128)(2,1)S(1)}, bf16[16,3584]{1,0:T(8,128)(2,1)S(1)}, u32[]{:S(2)}, u32[]{:S(2)}) collective-permute-start(bf16[16,3584]{1,0:T(8,128)(2,1)S(1)} %get-tuple-element.60), channel_id=1, source_target_pairs={{0,4},{1,5},{2,6},{3,7},{4,8},{5,9},{6,10},{7,11},{8,12},{9,13},{1... | collective-permute-start | bytes 344072 | tf_op jit(solution)/shard_map/ppermute | solution.py:19
  124.4 4.6 %collective-permute-done.27.left = bf16[16,3584]{1,0:T(8,128)(2,1)S(1)} collective-permute-done((bf16[16,3584]{1,0:T(8,128)(2,1)S(1)}, bf16[16,3584]{1,0:T(8,128)(2,1)S(1)}, u32[]{:S(2)}, u32[]{:S(2)}) %collective-permute-start.27) | collective-permute-done | bytes 114720 | tf_op jit(solution)/shard_map/ppermute | solution.py:19
  129.1 3.0 %collective-permute-done.29.right = bf16[16,3584]{1,0:T(8,128)(2,1)S(1)} collective-permute-done((bf16[16,3584]{1,0:T(8,128)(2,1)S(1)}, bf16[16,3584]{1,0:T(8,128)(2,1)S(1)}, u32[]{:S(2)}, u32[]{:S(2)}) %collective-permute-start.29) | collective-permute-done | bytes 114720 | tf_op jit(solution)/shard_map/ppermute | solution.py:19
  132.1 1.7 %collective-permute-start.30 = (bf16[16,7168]{1,0:T(8,128)(2,1)S(1)}, bf16[16,7168]{1,0:T(8,128)(2,1)S(1)}, u32[]{:S(2)}, u32[]{:S(2)}) collective-permute-start(bf16[16,7168]{1,0:T(8,128)(2,1)S(1)} %get-tuple-element.62), channel_id=1, source_target_pairs={{0,18},{1,19},{2,20},{3,21},{4,22},{5,23},{6,24},{7,25},{8,26},{9,... | collective-permute-start | bytes 688136 | tf_op jit(solution)/shard_map/ppermute | solution.py:36
  134.0 4.8 %collective-permute-start.34 = (bf16[16,7168]{1,0:T(8,128)(2,1)S(1)}, bf16[16,7168]{1,0:T(8,128)(2,1)S(1)}, u32[]{:S(2)}, u32[]{:S(2)}) collective-permute-start(bf16[16,7168]{1,0:T(8,128)(2,1)S(1)} %get-tuple-element.70), channel_id=1, source_target_pairs={{0,20},{1,21},{2,22},{3,23},{4,24},{5,25},{6,26},{7,27},{8,28},{9,... | collective-permute-start | bytes 688136 | tf_op jit(solution)/shard_map/ppermute | solution.py:36
  138.9 10.5 %collective-permute-done.30 = bf16[16,7168]{1,0:T(8,128)(2,1)S(1)} collective-permute-done((bf16[16,7168]{1,0:T(8,128)(2,1)S(1)}, bf16[16,7168]{1,0:T(8,128)(2,1)S(1)}, u32[]{:S(2)}, u32[]{:S(2)}) %collective-permute-start.30) | collective-permute-done | bytes 229408 | tf_op jit(solution)/shard_map/ppermute | solution.py:36
  149.6 10.2 %collective-permute-done.33 = bf16[16,7168]{1,0:T(8,128)(2,1)S(1)} collective-permute-done((bf16[16,7168]{1,0:T(8,128)(2,1)S(1)}, bf16[16,7168]{1,0:T(8,128)(2,1)S(1)}, u32[]{:S(2)}, u32[]{:S(2)}) %collective-permute-start.33) | collective-permute-done | bytes 229408 | tf_op jit(solution)/shard_map/ppermute | solution.py:36
  (57 shorter events, 12.2 us)
Async XLA Ops:
  7.9 34.1 %collective-permute-start.8 = (bf16[21504,256]{1,0:T(8,128)(2,1)S(1)}, bf16[21504,256]{1,0:T(8,128)(2,1)S(1)}, u32[]{:S(2)}, u32[]{:S(2)}) collective-permute-start(bf16[21504,256]{1,0:T(8,128)(2,1)S(1)} %get-tuple-element.39.refs_10_), channel_id=1, source_target_pairs={{0,1},{1,0},{2,3},{3,2},{4,5},{5,4},{6,7},{7,6},{8,9},{9,8},{10,11... | collective-permute-start | bytes 33030152 | tf_op jit(solution)/shard_map/ppermute | solution.py:26
  8.0 14.4 %collective-permute-start.3 = (bf16[16,7296]{1,0:T(8,128)(2,1)S(1)}, bf16[16,7296]{1,0:T(8,128)(2,1)S(1)}, u32[]{:S(2)}, u32[]{:S(2)}) collective-permute-start(bf16[16,7296]{1,0:T(8,128)(2,1)S(1)} %get-tuple-element.38.refs_0_), channel_id=1, source_target_pairs={{0,12},{1,13},{2,14},{3,15},{4,0},{5,1},{6,2},{7,3},{8,4},{9,5},{1... | collective-permute-start | bytes 700424 | tf_op jit(solution)/shard_map/ppermute | solution.py:19
  12.6 15.0 %collective-permute-start.2 = (bf16[16,7296]{1,0:T(8,128)(2,1)S(1)}, bf16[16,7296]{1,0:T(8,128)(2,1)S(1)}, u32[]{:S(2)}, u32[]{:S(2)}) collective-permute-start(bf16[16,7296]{1,0:T(8,128)(2,1)S(1)} %get-tuple-element.38.refs_0_), channel_id=1, source_target_pairs={{0,4},{1,5},{2,6},{3,7},{4,8},{5,9},{6,10},{7,11},{8,12},{9,13},{1... | collective-permute-start | bytes 700424 | tf_op jit(solution)/shard_map/ppermute | solution.py:19
  12.7 17.1 %collective-permute-start.1 = (bf16[16,7296]{1,0:T(8,128)(2,1)S(1)}, bf16[16,7296]{1,0:T(8,128)(2,1)S(1)}, u32[]{:S(2)}, u32[]{:S(2)}) collective-permute-start(bf16[16,7296]{1,0:T(8,128)(2,1)S(1)} %get-tuple-element.38.refs_0_), channel_id=1, source_target_pairs={{0,14},{1,15},{2,0},{3,1},{4,2},{5,3},{6,4},{7,5},{8,6},{9,7},{10,... | collective-permute-start | bytes 700424 | tf_op jit(solution)/shard_map/ppermute | solution.py:19
  16.3 16.2 %collective-permute-start = (bf16[16,7296]{1,0:T(8,128)(2,1)S(1)}, bf16[16,7296]{1,0:T(8,128)(2,1)S(1)}, u32[]{:S(2)}, u32[]{:S(2)}) collective-permute-start(bf16[16,7296]{1,0:T(8,128)(2,1)S(1)} %get-tuple-element.38.refs_0_), channel_id=1, source_target_pairs={{0,2},{1,3},{2,4},{3,5},{4,6},{5,7},{6,8},{7,9},{8,10},{9,11},{10,... | collective-permute-start | bytes 700424 | tf_op jit(solution)/shard_map/ppermute | solution.py:19
  22.4 19.6 %collective-permute-start.5 = (bf16[16,7296]{1,0:T(8,128)(2,1)S(1)}, bf16[16,7296]{1,0:T(8,128)(2,1)S(1)}, u32[]{:S(2)}, u32[]{:S(2)}) collective-permute-start(bf16[16,7296]{1,0:T(8,128)(2,1)S(1)} %collective-permute-done.3.refs_4_), channel_id=1, source_target_pairs={{0,14},{1,15},{2,0},{3,1},{4,2},{5,3},{6,4},{7,5},{8,6},{9,7},{10,... | collective-permute-start | bytes 700424 | tf_op jit(solution)/shard_map/ppermute | solution.py:19
  27.7 14.3 %collective-permute-start.4 = (bf16[16,7296]{1,0:T(8,128)(2,1)S(1)}, bf16[16,7296]{1,0:T(8,128)(2,1)S(1)}, u32[]{:S(2)}, u32[]{:S(2)}) collective-permute-start(bf16[16,7296]{1,0:T(8,128)(2,1)S(1)} %collective-permute-done.2.refs_3_), channel_id=1, source_target_pairs={{0,2},{1,3},{2,4},{3,5},{4,6},{5,7},{6,8},{7,9},{8,10},{9,11},{10,... | collective-permute-start | bytes 700424 | tf_op jit(solution)/shard_map/ppermute | solution.py:19
  29.7 12.3 %collective-permute-start.7 = (bf16[16,3712]{1,0:T(8,128)(2,1)S(1)}, bf16[16,3712]{1,0:T(8,128)(2,1)S(1)}, u32[]{:S(2)}, u32[]{:S(2)}) collective-permute-start(bf16[16,3712]{1,0:T(8,128)(2,1)S(1)} %slice.17), channel_id=1, source_target_pairs={{0,12},{1,13},{2,14},{3,15},{4,0},{5,1},{6,2},{7,3},{8,4},{9,5},{1... | collective-permute-start | bytes 356360 | tf_op jit(solution)/shard_map/ppermute | solution.py:19
  32.6 9.4 %collective-permute-start.6 = (bf16[16,3584]{1,0:T(8,128)(2,1)S(1)}, bf16[16,3584]{1,0:T(8,128)(2,1)S(1)}, u32[]{:S(2)}, u32[]{:S(2)}) collective-permute-start(bf16[16,3584]{1,0:T(8,128)(2,1)S(1)} %slice.16), channel_id=1, source_target_pairs={{0,4},{1,5},{2,6},{3,7},{4,8},{5,9},{6,10},{7,11},{8,12},{9,13},{1... | collective-permute-start | bytes 344072 | tf_op jit(solution)/shard_map/ppermute | solution.py:19
  45.5 18.0 %collective-permute-start.14 = (bf16[16,7168]{1,0:T(8,128)(2,1)S(1)}, bf16[16,7168]{1,0:T(8,128)(2,1)S(1)}, u32[]{:S(2)}, u32[]{:S(2)}) collective-permute-start(bf16[16,7168]{1,0:T(8,128)(2,1)S(1)} %get-tuple-element.51), channel_id=1, source_target_pairs={{0,14},{1,15},{2,0},{3,1},{4,2},{5,3},{6,4},{7,5},{8,6},{9,7},{10,... | collective-permute-start | bytes 688136 | tf_op jit(solution)/shard_map/ppermute | solution.py:19
  45.8 17.7 %collective-permute-start.15 = (bf16[16,7168]{1,0:T(8,128)(2,1)S(1)}, bf16[16,7168]{1,0:T(8,128)(2,1)S(1)}, u32[]{:S(2)}, u32[]{:S(2)}) collective-permute-start(bf16[16,7168]{1,0:T(8,128)(2,1)S(1)} %get-tuple-element.52), channel_id=1, source_target_pairs={{0,2},{1,3},{2,4},{3,5},{4,6},{5,7},{6,8},{7,9},{8,10},{9,11},{10,... | collective-permute-start | bytes 688136 | tf_op jit(solution)/shard_map/ppermute | solution.py:19
  47.6 10.6 %collective-permute-start.10 = (bf16[16,3584]{1,0:T(8,128)(2,1)S(1)}, bf16[16,3584]{1,0:T(8,128)(2,1)S(1)}, u32[]{:S(2)}, u32[]{:S(2)}) collective-permute-start(bf16[16,3584]{1,0:T(8,128)(2,1)S(1)} %get-tuple-element.41), channel_id=1, source_target_pairs={{0,12},{1,13},{2,14},{3,15},{4,0},{5,1},{6,2},{7,3},{8,4},{9,5},{1... | collective-permute-start | bytes 344072 | tf_op jit(solution)/shard_map/ppermute | solution.py:19
  47.6 10.6 %collective-permute-start.12 = (bf16[16,3584]{1,0:T(8,128)(2,1)S(1)}, bf16[16,3584]{1,0:T(8,128)(2,1)S(1)}, u32[]{:S(2)}, u32[]{:S(2)}) collective-permute-start(bf16[16,3584]{1,0:T(8,128)(2,1)S(1)} %get-tuple-element.44), channel_id=1, source_target_pairs={{0,4},{1,5},{2,6},{3,7},{4,8},{5,9},{6,10},{7,11},{8,12},{9,13},{1... | collective-permute-start | bytes 344072 | tf_op jit(solution)/shard_map/ppermute | solution.py:19
  50.5 17.4 %collective-permute-start.9 = (bf16[16,7168]{1,0:T(8,128)(2,1)S(1)}, bf16[16,7168]{1,0:T(8,128)(2,1)S(1)}, u32[]{:S(2)}, u32[]{:S(2)}) collective-permute-start(bf16[16,7168]{1,0:T(8,128)(2,1)S(1)} %get-tuple-element.40), channel_id=1, source_target_pairs={{0,16},{1,17},{2,18},{3,19},{4,20},{5,21},{6,22},{7,23},{8,24},{9,... | collective-permute-start | bytes 688136 | tf_op jit(solution)/shard_map/ppermute | solution.py:36
  58.2 18.7 %collective-permute-start.13 = (bf16[16,7168]{1,0:T(8,128)(2,1)S(1)}, bf16[16,7168]{1,0:T(8,128)(2,1)S(1)}, u32[]{:S(2)}, u32[]{:S(2)}) collective-permute-start(bf16[16,7168]{1,0:T(8,128)(2,1)S(1)} %get-tuple-element.46), channel_id=1, source_target_pairs={{0,18},{1,19},{2,20},{3,21},{4,22},{5,23},{6,24},{7,25},{8,26},{9,... | collective-permute-start | bytes 688136 | tf_op jit(solution)/shard_map/ppermute | solution.py:36
  61.2 24.6 %collective-permute-start.11 = (bf16[16,7168]{1,0:T(8,128)(2,1)S(1)}, bf16[16,7168]{1,0:T(8,128)(2,1)S(1)}, u32[]{:S(2)}, u32[]{:S(2)}) collective-permute-start(bf16[16,7168]{1,0:T(8,128)(2,1)S(1)} %get-tuple-element.43), channel_id=1, source_target_pairs={{0,30},{1,31},{2,16},{3,17},{4,18},{5,19},{6,20},{7,21},{8,22},{9,... | collective-permute-start | bytes 688136 | tf_op jit(solution)/shard_map/ppermute | solution.py:36
  63.6 22.2 %collective-permute-start.16 = (bf16[16,7168]{1,0:T(8,128)(2,1)S(1)}, bf16[16,7168]{1,0:T(8,128)(2,1)S(1)}, u32[]{:S(2)}, u32[]{:S(2)}) collective-permute-start(bf16[16,7168]{1,0:T(8,128)(2,1)S(1)} %get-tuple-element.53), channel_id=1, source_target_pairs={{0,28},{1,29},{2,30},{3,31},{4,16},{5,17},{6,18},{7,19},{8,20},{9,... | collective-permute-start | bytes 688136 | tf_op jit(solution)/shard_map/ppermute | solution.py:36
  64.9 20.9 %collective-permute-start.17 = (bf16[16,7168]{1,0:T(8,128)(2,1)S(1)}, bf16[16,7168]{1,0:T(8,128)(2,1)S(1)}, u32[]{:S(2)}, u32[]{:S(2)}) collective-permute-start(bf16[16,7168]{1,0:T(8,128)(2,1)S(1)} %get-tuple-element.54), channel_id=1, source_target_pairs={{0,20},{1,21},{2,22},{3,23},{4,24},{5,25},{6,26},{7,27},{8,28},{9,... | collective-permute-start | bytes 688136 | tf_op jit(solution)/shard_map/ppermute | solution.py:36
  85.9 12.0 %collective-permute-start.21 = (bf16[16,7168]{1,0:T(8,128)(2,1)S(1)}, bf16[16,7168]{1,0:T(8,128)(2,1)S(1)}, u32[]{:S(2)}, u32[]{:S(2)}) collective-permute-start(bf16[16,7168]{1,0:T(8,128)(2,1)S(1)} %add_convert_fusion.1.refs_0_), channel_id=1, source_target_pairs={{0,12},{1,13},{2,14},{3,15},{4,0},{5,1},{6,2},{7,3},{8,4},{9,5},{1... | collective-permute-start | bytes 688136 | tf_op jit(solution)/shard_map/ppermute | solution.py:19
  86.0 18.5 %collective-permute-start.20 = (bf16[16,7168]{1,0:T(8,128)(2,1)S(1)}, bf16[16,7168]{1,0:T(8,128)(2,1)S(1)}, u32[]{:S(2)}, u32[]{:S(2)}) collective-permute-start(bf16[16,7168]{1,0:T(8,128)(2,1)S(1)} %add_convert_fusion.1.refs_0_), channel_id=1, source_target_pairs={{0,4},{1,5},{2,6},{3,7},{4,8},{5,9},{6,10},{7,11},{8,12},{9,13},{1... | collective-permute-start | bytes 688136 | tf_op jit(solution)/shard_map/ppermute | solution.py:19
  88.9 19.0 %collective-permute-start.19 = (bf16[16,7168]{1,0:T(8,128)(2,1)S(1)}, bf16[16,7168]{1,0:T(8,128)(2,1)S(1)}, u32[]{:S(2)}, u32[]{:S(2)}) collective-permute-start(bf16[16,7168]{1,0:T(8,128)(2,1)S(1)} %add_convert_fusion.1.refs_0_), channel_id=1, source_target_pairs={{0,14},{1,15},{2,0},{3,1},{4,2},{5,3},{6,4},{7,5},{8,6},{9,7},{10,... | collective-permute-start | bytes 688136 | tf_op jit(solution)/shard_map/ppermute | solution.py:19
  98.0 9.9 %collective-permute-start.18 = (bf16[16,7168]{1,0:T(8,128)(2,1)S(1)}, bf16[16,7168]{1,0:T(8,128)(2,1)S(1)}, u32[]{:S(2)}, u32[]{:S(2)}) collective-permute-start(bf16[16,7168]{1,0:T(8,128)(2,1)S(1)} %add_convert_fusion.1.refs_0_), channel_id=1, source_target_pairs={{0,2},{1,3},{2,4},{3,5},{4,6},{5,7},{6,8},{7,9},{8,10},{9,11},{10,... | collective-permute-start | bytes 688136 | tf_op jit(solution)/shard_map/ppermute | solution.py:19
  98.0 18.1 %collective-permute-start.23 = (bf16[16,7168]{1,0:T(8,128)(2,1)S(1)}, bf16[16,7168]{1,0:T(8,128)(2,1)S(1)}, u32[]{:S(2)}, u32[]{:S(2)}) collective-permute-start(bf16[16,7168]{1,0:T(8,128)(2,1)S(1)} %collective-permute-done.21.refs_4_), channel_id=1, source_target_pairs={{0,14},{1,15},{2,0},{3,1},{4,2},{5,3},{6,4},{7,5},{8,6},{9,7},{10,... | collective-permute-start | bytes 688136 | tf_op jit(solution)/shard_map/ppermute | solution.py:19
  104.5 11.5 %collective-permute-start.22 = (bf16[16,7168]{1,0:T(8,128)(2,1)S(1)}, bf16[16,7168]{1,0:T(8,128)(2,1)S(1)}, u32[]{:S(2)}, u32[]{:S(2)}) collective-permute-start(bf16[16,7168]{1,0:T(8,128)(2,1)S(1)} %collective-permute-done.20.refs_3_), channel_id=1, source_target_pairs={{0,2},{1,3},{2,4},{3,5},{4,6},{5,7},{6,8},{7,9},{8,10},{9,11},{10,... | collective-permute-start | bytes 688136 | tf_op jit(solution)/shard_map/ppermute | solution.py:19
  119.4 14.3 %collective-permute-start.31 = (bf16[16,7168]{1,0:T(8,128)(2,1)S(1)}, bf16[16,7168]{1,0:T(8,128)(2,1)S(1)}, u32[]{:S(2)}, u32[]{:S(2)}) collective-permute-start(bf16[16,7168]{1,0:T(8,128)(2,1)S(1)} %get-tuple-element.67), channel_id=1, source_target_pairs={{0,14},{1,15},{2,0},{3,1},{4,2},{5,3},{6,4},{7,5},{8,6},{9,7},{10,... | collective-permute-start | bytes 688136 | tf_op jit(solution)/shard_map/ppermute | solution.py:19
  121.2 12.6 %collective-permute-start.32 = (bf16[16,7168]{1,0:T(8,128)(2,1)S(1)}, bf16[16,7168]{1,0:T(8,128)(2,1)S(1)}, u32[]{:S(2)}, u32[]{:S(2)}) collective-permute-start(bf16[16,7168]{1,0:T(8,128)(2,1)S(1)} %get-tuple-element.68), channel_id=1, source_target_pairs={{0,2},{1,3},{2,4},{3,5},{4,6},{5,7},{6,8},{7,9},{8,10},{9,11},{10,... | collective-permute-start | bytes 688136 | tf_op jit(solution)/shard_map/ppermute | solution.py:19
  122.7 9.4 %collective-permute-start.29 = (bf16[16,3584]{1,0:T(8,128)(2,1)S(1)}, bf16[16,3584]{1,0:T(8,128)(2,1)S(1)}, u32[]{:S(2)}, u32[]{:S(2)}) collective-permute-start(bf16[16,3584]{1,0:T(8,128)(2,1)S(1)} %get-tuple-element.60), channel_id=1, source_target_pairs={{0,4},{1,5},{2,6},{3,7},{4,8},{5,9},{6,10},{7,11},{8,12},{9,13},{1... | collective-permute-start | bytes 344072 | tf_op jit(solution)/shard_map/ppermute | solution.py:19
  124.4 14.4 %collective-permute-start.26 = (bf16[16,7168]{1,0:T(8,128)(2,1)S(1)}, bf16[16,7168]{1,0:T(8,128)(2,1)S(1)}, u32[]{:S(2)}, u32[]{:S(2)}) collective-permute-start(bf16[16,7168]{1,0:T(8,128)(2,1)S(1)} %get-tuple-element.56), channel_id=1, source_target_pairs={{0,16},{1,17},{2,18},{3,19},{4,20},{5,21},{6,22},{7,23},{8,24},{9,... | collective-permute-start | bytes 688136 | tf_op jit(solution)/shard_map/ppermute | solution.py:36
  132.1 17.3 %collective-permute-start.30 = (bf16[16,7168]{1,0:T(8,128)(2,1)S(1)}, bf16[16,7168]{1,0:T(8,128)(2,1)S(1)}, u32[]{:S(2)}, u32[]{:S(2)}) collective-permute-start(bf16[16,7168]{1,0:T(8,128)(2,1)S(1)} %get-tuple-element.62), channel_id=1, source_target_pairs={{0,18},{1,19},{2,20},{3,21},{4,22},{5,23},{6,24},{7,25},{8,26},{9,... | collective-permute-start | bytes 688136 | tf_op jit(solution)/shard_map/ppermute | solution.py:36
  133.7 15.8 %collective-permute-start.28 = (bf16[16,7168]{1,0:T(8,128)(2,1)S(1)}, bf16[16,7168]{1,0:T(8,128)(2,1)S(1)}, u32[]{:S(2)}, u32[]{:S(2)}) collective-permute-start(bf16[16,7168]{1,0:T(8,128)(2,1)S(1)} %get-tuple-element.59), channel_id=1, source_target_pairs={{0,30},{1,31},{2,16},{3,17},{4,18},{5,19},{6,20},{7,21},{8,22},{9,... | collective-permute-start | bytes 688136 | tf_op jit(solution)/shard_map/ppermute | solution.py:36
  133.9 25.8 %collective-permute-start.33 = (bf16[16,7168]{1,0:T(8,128)(2,1)S(1)}, bf16[16,7168]{1,0:T(8,128)(2,1)S(1)}, u32[]{:S(2)}, u32[]{:S(2)}) collective-permute-start(bf16[16,7168]{1,0:T(8,128)(2,1)S(1)} %get-tuple-element.69), channel_id=1, source_target_pairs={{0,28},{1,29},{2,30},{3,31},{4,16},{5,17},{6,18},{7,19},{8,20},{9,... | collective-permute-start | bytes 688136 | tf_op jit(solution)/shard_map/ppermute | solution.py:36
  134.0 25.7 %collective-permute-start.34 = (bf16[16,7168]{1,0:T(8,128)(2,1)S(1)}, bf16[16,7168]{1,0:T(8,128)(2,1)S(1)}, u32[]{:S(2)}, u32[]{:S(2)}) collective-permute-start(bf16[16,7168]{1,0:T(8,128)(2,1)S(1)} %get-tuple-element.70), channel_id=1, source_target_pairs={{0,20},{1,21},{2,22},{3,23},{4,24},{5,25},{6,26},{7,27},{8,28},{9,... | collective-permute-start | bytes 688136 | tf_op jit(solution)/shard_map/ppermute | solution.py:36
  (7 other events, 64.8 us)

commit v3 on v2

--- a/solution.py
+++ b/solution.py
@@ -65,14 +65,27 @@
     ]
     far[0], near_back = lax.optimization_barrier((far[0], outs[1]))
     far[1], near_ahead = lax.optimization_barrier((far[1], outs[2]))
-    parts = [
-        to_next_section(outs[0], 0),
-        to_next_section(near_back, -1),
-        to_next_section(near_ahead, 1),
-    ]
+    near = [along_z(near_back, -1), along_z(near_ahead, 1)]
     back, ahead = join_far(outs[3], outs[4], *far)
-    parts += [to_next_section(back, -2), to_next_section(ahead, 2)]
+    parts = [to_next_section(back, -2), to_next_section(ahead, 2)]
+    parts.append(to_next_section(join_near(outs[0], *near), 0))
     return sum(part.astype(F32) for part in parts).astype(BF16)
+
+
+def join_near(own, back, ahead):
+    def kernel(own, back, ahead, out):
+        f = lambda ref: ref[...].astype(F32)
+        out[...] = (f(own) + (f(back) + f(ahead))).astype(BF16)
+
+    return pl.pallas_call(
+        kernel,
+        out_shape=jax.ShapeDtypeStruct(own.shape, BF16),
+        compiler_params=pltpu.CompilerParams(vmem_limit_bytes=VMEM_LIMIT),
+        cost_estimate=pl.CostEstimate(
+            flops=2 * own.size, bytes_accessed=8 * own.size, transcendentals=0
+        ),
+        name="join_near",
+    )(own, back, ahead)
 
 
 def join_far(back, ahead, left, right, back_3, ahead_3):
@@ -142,8 +155,9 @@
     group = max(n for n in (1, 2, 4) if blocks % n == 0)
     groups = [(n, at) for n in range(len(arrays)) for at in range(0, blocks, group)]
 
-    def kernel(exp_ref, tokens_ref, routes_ref, route_weights_ref, *refs):
-        ins, rows_out, out_ref, sems, rows_sem = refs[: len(arrays)], *refs[len(arrays) :]
+    def kernel(exp_in, tokens_ref, routes_in, route_weights_ref, *refs):
+        ins, refs = refs[: len(arrays)], refs[len(arrays) :]
+        rows_out, out_ref, exp_ref, routes_ref, sems, small_sems = refs
 
         def copies(n, at):
             if ins[n].shape[0] == width:
@@ -172,13 +186,20 @@
                         place = (slice(row, row + LANES), slice(b * LANES, (b + 1) * LANES))
                         out_ref[place] = scaled(out_ref[place], factor)
 
-        rows_copy = pltpu.make_async_copy(tokens_ref, rows_out.at[:, pl.ds(0, width)], rows_sem)
-        rows_copy.start()
+        small = [
+            pltpu.make_async_copy(exp_in, exp_ref, small_sems.at[0]),
+            pltpu.make_async_copy(routes_in, routes_ref, small_sems.at[1]),
+            pltpu.make_async_copy(tokens_ref, rows_out.at[:, pl.ds(0, width)], small_sems.at[2]),
+        ]
+        for copy in small:
+            copy.start()
         for n in range(len(groups) + AHEAD):
             if n < len(groups):
                 for copy in copies(*groups[n]):
                     copy.start()
             if n == AHEAD:
+                for copy in small:
+                    copy.wait()
                 lane = lax.broadcasted_iota(jnp.int32, (LANES, height), 0)
                 table = jnp.zeros((LANES, height), F32)
                 for step in range(TICKS):
@@ -191,18 +212,22 @@
                 for copy in copies(*groups[n - AHEAD]):
                     copy.wait()
                 scale(*groups[n - AHEAD])
-        rows_copy.wait()
 
     vmem, hbm = (pl.BlockSpec(memory_space=space) for space in (pltpu.VMEM, pltpu.HBM))
     return pl.pallas_call(
         kernel,
-        in_specs=[pl.BlockSpec(memory_space=pltpu.SMEM), hbm, vmem, vmem] + [hbm] * len(arrays),
+        in_specs=[hbm, hbm, hbm, vmem] + [hbm] * len(arrays),
         out_specs=[vmem] * 2,
         out_shape=[
             jax.ShapeDtypeStruct((height, width + LANES), BF16),
             jax.ShapeDtypeStruct((len(arrays) * width, side), BF16),
         ],
-        scratch_shapes=[pltpu.SemaphoreType.DMA((len(arrays), blocks)), pltpu.SemaphoreType.DMA],
+        scratch_shapes=[
+            pltpu.SMEM(exponents.shape, jnp.int32),
+            pltpu.VMEM(routes.shape, jnp.int32),
+            pltpu.SemaphoreType.DMA((len(arrays), blocks)),
+            pltpu.SemaphoreType.DMA((3,)),
+        ],
         compiler_params=pltpu.CompilerParams(vmem_limit_bytes=VMEM_LIMIT),
         cost_estimate=pl.CostEstimate(
             flops=len(arrays) * width * side,
@@ -211,9 +236,7 @@
         ),
         name="prepare",
     )(
-        exponents,
-        pltpu.with_memory_space_constraint(tokens, pltpu.HBM),
-        routes,
+        *(pltpu.with_memory_space_constraint(a, pltpu.HBM) for a in (exponents, tokens, routes)),
         route_weights,
         *(pltpu.with_memory_space_constraint(w, pltpu.HBM) for w in arrays),
     )

time: 161 us -> 154 us (0.957); the launches traced: 161 us -> 151 us
  starting transfers between devices: 65 us -> 56.2 us
    ppermute x24 -> x28, waiting for transfers between devices: 40.8 us -> 54.9 us  [along_z(): lax.ppermute(shard, 'expert', [(i, (i + 2 * by) % length) for i in range(...]
    ppermute x10 -> x6, waiting for transfers between devices: 38.7 us -> 25 us  [to_next_section(): return lax.ppermute(shard, ('section', 'expert'), pairs)]
    ppermute x10 -> x6, starting transfers between devices: 17.8 us -> 8.75 us  [to_next_section(): return lax.ppermute(shard, ('section', 'expert'), pairs)]
    pallas_call x1 -> x3, Pallas kernels: 5.85 us -> 6.42 us  [the longest x1 6.24 us: prepare(): pl.pallas_call(kernel, in_specs=[hbm, hbm, hbm, vmem] + [hbm] * len(array...]
    ppermute x24 -> x28, starting transfers between devices: 47.1 us -> 47.3 us  [along_z(): lax.ppermute(shard, 'expert', [(i, (i + 2 * by) % length) for i in range(...]
  transfers between devices with their start and end apart: 35 -> 35, of which waited for: 16 -> 23; matrix products, arithmetic and copies ran while one was open for 0% -> 0% of each run, Pallas kernels for 0% -> 0%
where the time goes in v3:
time: 154 us; the launch traced here: 151 us
  waiting for transfers between devices  79.9 us (52%)
  starting transfers between devices  56.2 us (36%)
  Pallas kernels  13.5 us (9%)
    ppermute x28, waiting for transfers between devices, along_z(): lax.ppermute(shard, 'expert', [(i, (i + 2 * by) % length) for i in range(...  54.9 us
    ppermute x28, starting transfers between devices, along_z(): lax.ppermute(shard, 'expert', [(i, (i + 2 * by) % length) for i in range(...  47.3 us
    ppermute x6, waiting for transfers between devices, to_next_section(): return lax.ppermute(shard, ('section', 'expert'), pairs)  25 us
    ppermute x6, starting transfers between devices, to_next_section(): return lax.ppermute(shard, ('section', 'expert'), pairs)  8.75 us
    pallas_call x2, Pallas kernels, experts_share(): pl.pallas_call(kernel, in_specs=[vmem] * len(operands), out_specs=[vmem]...  6.75 us
    pallas_call x1, Pallas kernels, prepare(): pl.pallas_call(kernel, in_specs=[hbm, hbm, hbm, vmem] + [hbm] * len(array...  6.24 us
  transfers between devices with their start and end apart: 35, of which 23 were waited for; matrix products, arithmetic and copies ran while one was open for 0% of the time, Pallas kernels for 0%

profile of v3, /device:TPU:0, one launch (start us, length us, event | category | flops | bytes accessed | tf_op | source)
XLA Modules:
  0.0 151.3 jit_solution(16124626390328739968)
XLA Ops:
  0.7 6.2 %prepare.1 = (bf16[16,7296]{1,0:T(8,128)(2,1)S(1)}, bf16[21504,256]{1,0:T(8,128)(2,1)S(1)}) custom-call(s32[3,2,56]{2,1,0:T(2,128)} %bitcast.20, bf16[16,7168]{1,0:T(8,128)(2,1)} %bitcast.19, s32[2,2,16]{2,1,0:T(2,128)} %bitcast.21, bf16[2,2,16]{2,1,0:T(2,128)(2,1)S(1)} %bitcast.15, bf16[7168,256]{1,0:T(8,128)(2,1)} %bitcast.16, bf16[7168,256]{1,0:T(8,128)(2,1)} %bitcast.17, ...), custom_call_target="tpu_custom_call" | custom-call | flops 5505024 | bytes 22020096 | tf_op jit(solution)/shard_map/prepare/pallas_call | solution.py:217
  7.0 4.6 %collective-permute-start.3 = (bf16[16,7296]{1,0:T(8,128)(2,1)S(1)}, bf16[16,7296]{1,0:T(8,128)(2,1)S(1)}, u32[]{:S(2)}, u32[]{:S(2)}) collective-permute-start(bf16[16,7296]{1,0:T(8,128)(2,1)S(1)} %get-tuple-element.38.refs_0_), channel_id=1, source_target_pairs={{0,12},{1,13},{2,14},{3,15},{4,0},{5,1},{6,2},{7,3},{8,4},{9,5},{1... | collective-permute-start | bytes 700424 | tf_op jit(solution)/shard_map/ppermute | solution.py:19
  11.7 3.7 %collective-permute-start.1 = (bf16[16,7296]{1,0:T(8,128)(2,1)S(1)}, bf16[16,7296]{1,0:T(8,128)(2,1)S(1)}, u32[]{:S(2)}, u32[]{:S(2)}) collective-permute-start(bf16[16,7296]{1,0:T(8,128)(2,1)S(1)} %get-tuple-element.38.refs_0_), channel_id=1, source_target_pairs={{0,14},{1,15},{2,0},{3,1},{4,2},{5,3},{6,4},{7,5},{8,6},{9,7},{10,... | collective-permute-start | bytes 700424 | tf_op jit(solution)/shard_map/ppermute | solution.py:19
  15.4 6.0 %collective-permute-done.3.refs_4_ = bf16[16,7296]{1,0:T(8,128)(2,1)S(1)} collective-permute-done((bf16[16,7296]{1,0:T(8,128)(2,1)S(1)}, bf16[16,7296]{1,0:T(8,128)(2,1)S(1)}, u32[]{:S(2)}, u32[]{:S(2)}) %collective-permute-start.3) | collective-permute-done | bytes 233504 | tf_op jit(solution)/shard_map/ppermute | solution.py:19
  21.4 5.0 %collective-permute-start.5 = (bf16[16,7296]{1,0:T(8,128)(2,1)S(1)}, bf16[16,7296]{1,0:T(8,128)(2,1)S(1)}, u32[]{:S(2)}, u32[]{:S(2)}) collective-permute-start(bf16[16,7296]{1,0:T(8,128)(2,1)S(1)} %collective-permute-done.3.refs_4_), channel_id=1, source_target_pairs={{0,14},{1,15},{2,0},{3,1},{4,2},{5,3},{6,4},{7,5},{8,6},{9,7},{10,... | collective-permute-start | bytes 700424 | tf_op jit(solution)/shard_map/ppermute | solution.py:19
  28.7 2.0 %collective-permute-start.7 = (bf16[16,3712]{1,0:T(8,128)(2,1)S(1)}, bf16[16,3712]{1,0:T(8,128)(2,1)S(1)}, u32[]{:S(2)}, u32[]{:S(2)}) collective-permute-start(bf16[16,3712]{1,0:T(8,128)(2,1)S(1)} %slice.17), channel_id=1, source_target_pairs={{0,12},{1,13},{2,14},{3,15},{4,0},{5,1},{6,2},{7,3},{8,4},{9,5},{1... | collective-permute-start | bytes 356360 | tf_op jit(solution)/shard_map/ppermute | solution.py:19
  31.9 9.1 %collective-permute-done.6.refs_7_ = bf16[16,3584]{1,0:T(8,128)(2,1)S(1)} collective-permute-done((bf16[16,3584]{1,0:T(8,128)(2,1)S(1)}, bf16[16,3584]{1,0:T(8,128)(2,1)S(1)}, u32[]{:S(2)}, u32[]{:S(2)}) %collective-permute-start.6) | collective-permute-done | bytes 114720 | tf_op jit(solution)/shard_map/ppermute | solution.py:19
  41.0 3.4 %experts_share.2 = (bf16[16,7168]{1,0:T(8,128)(2,1)S(1)}, bf16[16,7168]{1,0:T(8,128)(2,1)S(1)}, bf16[16,7168]{1,0:T(8,128)(2,1)S(1)}, bf16[16,7168]{1,0:T(8,128)...) custom-call(bf16[16,7296]{1,0:T(8,128)(2,1)S(1)} %get-tuple-element., ...), custom_call_target="tpu_custom_call" | custom-call | flops 2818572288 | bytes 22020096 | tf_op jit(solution)/shard_map/experts_share/pallas_call | solution.py:310
  44.6 2.9 %collective-permute-start.10 = (bf16[16,3584]{1,0:T(8,128)(2,1)S(1)}, bf16[16,3584]{1,0:T(8,128)(2,1)S(1)}, u32[]{:S(2)}, u32[]{:S(2)}) collective-permute-start(bf16[16,3584]{1,0:T(8,128)(2,1)S(1)} %get-tuple-element.45), channel_id=1, source_target_pairs={{0,4},{1,5},{2,6},{3,7},{4,8},{5,9},{6,10},{7,11},{8,12},{9,13},{1... | collective-permute-start | bytes 344072 | tf_op jit(solution)/shard_map/ppermute | solution.py:19
  49.5 3.7 %collective-permute-done.9.left = bf16[16,3584]{1,0:T(8,128)(2,1)S(1)} collective-permute-done((bf16[16,3584]{1,0:T(8,128)(2,1)S(1)}, bf16[16,3584]{1,0:T(8,128)(2,1)S(1)}, u32[]{:S(2)}, u32[]{:S(2)}) %collective-permute-start.9) | collective-permute-done | bytes 114720 | tf_op jit(solution)/shard_map/ppermute | solution.py:19
  53.3 1.8 %collective-permute-done.10.right = bf16[16,3584]{1,0:T(8,128)(2,1)S(1)} collective-permute-done((bf16[16,3584]{1,0:T(8,128)(2,1)S(1)}, bf16[16,3584]{1,0:T(8,128)(2,1)S(1)}, u32[]{:S(2)}, u32[]{:S(2)}) %collective-permute-start.10) | collective-permute-done | bytes 114720 | tf_op jit(solution)/shard_map/ppermute | solution.py:19
  55.1 3.2 %collective-permute-start.15 = (bf16[16,7168]{1,0:T(8,128)(2,1)S(1)}, bf16[16,7168]{1,0:T(8,128)(2,1)S(1)}, u32[]{:S(2)}, u32[]{:S(2)}) collective-permute-start(bf16[16,7168]{1,0:T(8,128)(2,1)S(1)} %get-tuple-element.53), channel_id=1, source_target_pairs={{0,14},{1,15},{2,0},{3,1},{4,2},{5,3},{6,4},{7,5},{8,6},{9,7},{10,... | collective-permute-start | bytes 688136 | tf_op jit(solution)/shard_map/ppermute | solution.py:19
  61.2 3.5 %collective-permute-start.14 = (bf16[16,7168]{1,0:T(8,128)(2,1)S(1)}, bf16[16,7168]{1,0:T(8,128)(2,1)S(1)}, u32[]{:S(2)}, u32[]{:S(2)}) collective-permute-start(bf16[16,7168]{1,0:T(8,128)(2,1)S(1)} %get-tuple-element.51), channel_id=1, source_target_pairs={{0,20},{1,21},{2,22},{3,23},{4,24},{5,25},{6,26},{7,27},{8,28},{9,... | collective-permute-start | bytes 688136 | tf_op jit(solution)/shard_map/ppermute | solution.py:36
  64.8 4.0 %collective-permute-done.15.back = bf16[16,7168]{1,0:T(8,128)(2,1)S(1)} collective-permute-done((bf16[16,7168]{1,0:T(8,128)(2,1)S(1)}, bf16[16,7168]{1,0:T(8,128)(2,1)S(1)}, u32[]{:S(2)}, u32[]{:S(2)}) %collective-permute-start.15) | collective-permute-done | bytes 229408 | tf_op jit(solution)/shard_map/ppermute | solution.py:19
  68.8 2.5 %collective-permute-start.17 = (bf16[16,7168]{1,0:T(8,128)(2,1)S(1)}, bf16[16,7168]{1,0:T(8,128)(2,1)S(1)}, u32[]{:S(2)}, u32[]{:S(2)}) collective-permute-start(bf16[16,7168]{1,0:T(8,128)(2,1)S(1)} %join_near.2), channel_id=1, source_target_pairs={{0,16},{1,17},{2,18},{3,19},{4,20},{5,21},{6,22},{7,23},{8,24},{9,... | collective-permute-start | bytes 688136 | tf_op jit(solution)/shard_map/ppermute | solution.py:36
  71.3 6.7 %collective-permute-done.13 = bf16[16,7168]{1,0:T(8,128)(2,1)S(1)} collective-permute-done((bf16[16,7168]{1,0:T(8,128)(2,1)S(1)}, bf16[16,7168]{1,0:T(8,128)(2,1)S(1)}, u32[]{:S(2)}, u32[]{:S(2)}) %collective-permute-start.13) | collective-permute-done | bytes 229408 | tf_op jit(solution)/shard_map/ppermute | solution.py:36
  79.4 2.7 %collective-permute-done.17 = bf16[16,7168]{1,0:T(8,128)(2,1)S(1)} collective-permute-done((bf16[16,7168]{1,0:T(8,128)(2,1)S(1)}, bf16[16,7168]{1,0:T(8,128)(2,1)S(1)}, u32[]{:S(2)}, u32[]{:S(2)}) %collective-permute-start.17) | collective-permute-done | bytes 229408 | tf_op jit(solution)/shard_map/ppermute | solution.py:36
  87.2 6.5 %collective-permute-done.21.refs_4_ = bf16[16,7168]{1,0:T(8,128)(2,1)S(1)} collective-permute-done((bf16[16,7168]{1,0:T(8,128)(2,1)S(1)}, bf16[16,7168]{1,0:T(8,128)(2,1)S(1)}, u32[]{:S(2)}, u32[]{:S(2)}) %collective-permute-start.21) | collective-permute-done | bytes 229408 | tf_op jit(solution)/shard_map/ppermute | solution.py:19
  93.7 3.3 %collective-permute-start.23 = (bf16[16,7168]{1,0:T(8,128)(2,1)S(1)}, bf16[16,7168]{1,0:T(8,128)(2,1)S(1)}, u32[]{:S(2)}, u32[]{:S(2)}) collective-permute-start(bf16[16,7168]{1,0:T(8,128)(2,1)S(1)} %collective-permute-done.21.refs_4_), channel_id=1, source_target_pairs={{0,14},{1,15},{2,0},{3,1},{4,2},{5,3},{6,4},{7,5},{8,6},{9,7},{10,... | collective-permute-start | bytes 688136 | tf_op jit(solution)/shard_map/ppermute | solution.py:19
  97.4 1.8 %collective-permute-start.22 = (bf16[16,7168]{1,0:T(8,128)(2,1)S(1)}, bf16[16,7168]{1,0:T(8,128)(2,1)S(1)}, u32[]{:S(2)}, u32[]{:S(2)}) collective-permute-start(bf16[16,7168]{1,0:T(8,128)(2,1)S(1)} %collective-permute-done.20.refs_3_), channel_id=1, source_target_pairs={{0,2},{1,3},{2,4},{3,5},{4,6},{5,7},{6,8},{7,9},{8,10},{9,11},{10,... | collective-permute-start | bytes 688136 | tf_op jit(solution)/shard_map/ppermute | solution.py:19
  99.4 3.0 %collective-permute-start.24 = (bf16[16,3584]{1,0:T(8,128)(2,1)S(1)}, bf16[16,3584]{1,0:T(8,128)(2,1)S(1)}, u32[]{:S(2)}, u32[]{:S(2)}) collective-permute-start(bf16[16,3584]{1,0:T(8,128)(2,1)S(1)} %slice.18), channel_id=1, source_target_pairs={{0,4},{1,5},{2,6},{3,7},{4,8},{5,9},{6,10},{7,11},{8,12},{9,13},{1... | collective-permute-start | bytes 344072 | tf_op jit(solution)/shard_map/ppermute | solution.py:19
  102.3 4.6 %collective-permute-done.25.refs_8_ = bf16[16,3584]{1,0:T(8,128)(2,1)S(1)} collective-permute-done((bf16[16,3584]{1,0:T(8,128)(2,1)S(1)}, bf16[16,3584]{1,0:T(8,128)(2,1)S(1)}, u32[]{:S(2)}, u32[]{:S(2)}) %collective-permute-start.25) | collective-permute-done | bytes 114720 | tf_op jit(solution)/shard_map/ppermute | solution.py:19
  107.0 4.2 %collective-permute-done.24.refs_7_ = bf16[16,3584]{1,0:T(8,128)(2,1)S(1)} collective-permute-done((bf16[16,3584]{1,0:T(8,128)(2,1)S(1)}, bf16[16,3584]{1,0:T(8,128)(2,1)S(1)}, u32[]{:S(2)}, u32[]{:S(2)}) %collective-permute-start.24) | collective-permute-done | bytes 114720 | tf_op jit(solution)/shard_map/ppermute | solution.py:19
  111.2 3.3 %experts_share.3 = (bf16[16,7168]{1,0:T(8,128)(2,1)S(1)}, bf16[16,7168]{1,0:T(8,128)(2,1)S(1)}, bf16[16,7168]{1,0:T(8,128)(2,1)S(1)}, bf16[16,7168]{1,0:T(8,128)...) custom-call(bf16[16,7168]{1,0:T(8,128)(2,1)S(1)} %add_convert_fusion, ...), custom_call_target="tpu_custom_call" | custom-call | flops 2818572288 | bytes 22020096 | tf_op jit(solution)/shard_map/experts_share/pallas_call | solution.py:310
  115.7 1.8 %collective-permute-start.27 = (bf16[16,3584]{1,0:T(8,128)(2,1)S(1)}, bf16[16,3584]{1,0:T(8,128)(2,1)S(1)}, u32[]{:S(2)}, u32[]{:S(2)}) collective-permute-start(bf16[16,3584]{1,0:T(8,128)(2,1)S(1)} %get-tuple-element.61), channel_id=1, source_target_pairs={{0,4},{1,5},{2,6},{3,7},{4,8},{5,9},{6,10},{7,11},{8,12},{9,13},{1... | collective-permute-start | bytes 344072 | tf_op jit(solution)/shard_map/ppermute | solution.py:19
  119.5 2.1 %collective-permute-done.26.left = bf16[16,3584]{1,0:T(8,128)(2,1)S(1)} collective-permute-done((bf16[16,3584]{1,0:T(8,128)(2,1)S(1)}, bf16[16,3584]{1,0:T(8,128)(2,1)S(1)}, u32[]{:S(2)}, u32[]{:S(2)}) %collective-permute-start.26) | collective-permute-done | bytes 114720 | tf_op jit(solution)/shard_map/ppermute | solution.py:19
  121.6 2.3 %collective-permute-done.27.right = bf16[16,3584]{1,0:T(8,128)(2,1)S(1)} collective-permute-done((bf16[16,3584]{1,0:T(8,128)(2,1)S(1)}, bf16[16,3584]{1,0:T(8,128)(2,1)S(1)}, u32[]{:S(2)}, u32[]{:S(2)}) %collective-permute-start.27) | collective-permute-done | bytes 114720 | tf_op jit(solution)/shard_map/ppermute | solution.py:19
  123.9 2.2 %collective-permute-start.33 = (bf16[16,7168]{1,0:T(8,128)(2,1)S(1)}, bf16[16,7168]{1,0:T(8,128)(2,1)S(1)}, u32[]{:S(2)}, u32[]{:S(2)}) collective-permute-start(bf16[16,7168]{1,0:T(8,128)(2,1)S(1)} %get-tuple-element.70), channel_id=1, source_target_pairs={{0,2},{1,3},{2,4},{3,5},{4,6},{5,7},{6,8},{7,9},{8,10},{9,11},{10,... | collective-permute-start | bytes 688136 | tf_op jit(solution)/shard_map/ppermute | solution.py:19
  130.6 5.4 %collective-permute-done.33.ahead = bf16[16,7168]{1,0:T(8,128)(2,1)S(1)} collective-permute-done((bf16[16,7168]{1,0:T(8,128)(2,1)S(1)}, bf16[16,7168]{1,0:T(8,128)(2,1)S(1)}, u32[]{:S(2)}, u32[]{:S(2)}) %collective-permute-start.33) | collective-permute-done | bytes 229408 | tf_op jit(solution)/shard_map/ppermute | solution.py:19
  136.2 7.9 %collective-permute-done.30 = bf16[16,7168]{1,0:T(8,128)(2,1)S(1)} collective-permute-done((bf16[16,7168]{1,0:T(8,128)(2,1)S(1)}, bf16[16,7168]{1,0:T(8,128)(2,1)S(1)}, u32[]{:S(2)}, u32[]{:S(2)}) %collective-permute-start.30) | collective-permute-done | bytes 229408 | tf_op jit(solution)/shard_map/ppermute | solution.py:36
  144.1 1.7 %collective-permute-done.31 = bf16[16,7168]{1,0:T(8,128)(2,1)S(1)} collective-permute-done((bf16[16,7168]{1,0:T(8,128)(2,1)S(1)}, bf16[16,7168]{1,0:T(8,128)(2,1)S(1)}, u32[]{:S(2)}, u32[]{:S(2)}) %collective-permute-start.31) | collective-permute-done | bytes 229408 | tf_op jit(solution)/shard_map/ppermute | solution.py:36
  145.9 4.6 %collective-permute-done.34 = bf16[16,7168]{1,0:T(8,128)(2,1)S(1)} collective-permute-done((bf16[16,7168]{1,0:T(8,128)(2,1)S(1)}, bf16[16,7168]{1,0:T(8,128)(2,1)S(1)}, u32[]{:S(2)}, u32[]{:S(2)}) %collective-permute-start.34) | collective-permute-done | bytes 229408 | tf_op jit(solution)/shard_map/ppermute | solution.py:36
  (55 shorter events, 25.1 us)
Async XLA Ops:
  6.9 34.1 %collective-permute-start.8 = (bf16[21504,256]{1,0:T(8,128)(2,1)S(1)}, bf16[21504,256]{1,0:T(8,128)(2,1)S(1)}, u32[]{:S(2)}, u32[]{:S(2)}) collective-permute-start(bf16[21504,256]{1,0:T(8,128)(2,1)S(1)} %get-tuple-element.39.refs_10_), channel_id=1, source_target_pairs={{0,1},{1,0},{2,3},{3,2},{4,5},{5,4},{6,7},{7,6},{8,9},{9,8},{10,11... | collective-permute-start | bytes 33030152 | tf_op jit(solution)/shard_map/ppermute | solution.py:26
  7.0 14.4 %collective-permute-start.3 = (bf16[16,7296]{1,0:T(8,128)(2,1)S(1)}, bf16[16,7296]{1,0:T(8,128)(2,1)S(1)}, u32[]{:S(2)}, u32[]{:S(2)}) collective-permute-start(bf16[16,7296]{1,0:T(8,128)(2,1)S(1)} %get-tuple-element.38.refs_0_), channel_id=1, source_target_pairs={{0,12},{1,13},{2,14},{3,15},{4,0},{5,1},{6,2},{7,3},{8,4},{9,5},{1... | collective-permute-start | bytes 700424 | tf_op jit(solution)/shard_map/ppermute | solution.py:19
  11.7 15.0 %collective-permute-start.2 = (bf16[16,7296]{1,0:T(8,128)(2,1)S(1)}, bf16[16,7296]{1,0:T(8,128)(2,1)S(1)}, u32[]{:S(2)}, u32[]{:S(2)}) collective-permute-start(bf16[16,7296]{1,0:T(8,128)(2,1)S(1)} %get-tuple-element.38.refs_0_), channel_id=1, source_target_pairs={{0,4},{1,5},{2,6},{3,7},{4,8},{5,9},{6,10},{7,11},{8,12},{9,13},{1... | collective-permute-start | bytes 700424 | tf_op jit(solution)/shard_map/ppermute | solution.py:19
  11.7 17.1 %collective-permute-start.1 = (bf16[16,7296]{1,0:T(8,128)(2,1)S(1)}, bf16[16,7296]{1,0:T(8,128)(2,1)S(1)}, u32[]{:S(2)}, u32[]{:S(2)}) collective-permute-start(bf16[16,7296]{1,0:T(8,128)(2,1)S(1)} %get-tuple-element.38.refs_0_), channel_id=1, source_target_pairs={{0,14},{1,15},{2,0},{3,1},{4,2},{5,3},{6,4},{7,5},{8,6},{9,7},{10,... | collective-permute-start | bytes 700424 | tf_op jit(solution)/shard_map/ppermute | solution.py:19
  15.4 16.2 %collective-permute-start = (bf16[16,7296]{1,0:T(8,128)(2,1)S(1)}, bf16[16,7296]{1,0:T(8,128)(2,1)S(1)}, u32[]{:S(2)}, u32[]{:S(2)}) collective-permute-start(bf16[16,7296]{1,0:T(8,128)(2,1)S(1)} %get-tuple-element.38.refs_0_), channel_id=1, source_target_pairs={{0,2},{1,3},{2,4},{3,5},{4,6},{5,7},{6,8},{7,9},{8,10},{9,11},{10,... | collective-permute-start | bytes 700424 | tf_op jit(solution)/shard_map/ppermute | solution.py:19
  21.4 19.6 %collective-permute-start.5 = (bf16[16,7296]{1,0:T(8,128)(2,1)S(1)}, bf16[16,7296]{1,0:T(8,128)(2,1)S(1)}, u32[]{:S(2)}, u32[]{:S(2)}) collective-permute-start(bf16[16,7296]{1,0:T(8,128)(2,1)S(1)} %collective-permute-done.3.refs_4_), channel_id=1, source_target_pairs={{0,14},{1,15},{2,0},{3,1},{4,2},{5,3},{6,4},{7,5},{8,6},{9,7},{10,... | collective-permute-start | bytes 700424 | tf_op jit(solution)/shard_map/ppermute | solution.py:19
  26.7 14.3 %collective-permute-start.4 = (bf16[16,7296]{1,0:T(8,128)(2,1)S(1)}, bf16[16,7296]{1,0:T(8,128)(2,1)S(1)}, u32[]{:S(2)}, u32[]{:S(2)}) collective-permute-start(bf16[16,7296]{1,0:T(8,128)(2,1)S(1)} %collective-permute-done.2.refs_3_), channel_id=1, source_target_pairs={{0,2},{1,3},{2,4},{3,5},{4,6},{5,7},{6,8},{7,9},{8,10},{9,11},{10,... | collective-permute-start | bytes 700424 | tf_op jit(solution)/shard_map/ppermute | solution.py:19
  28.7 12.3 %collective-permute-start.7 = (bf16[16,3712]{1,0:T(8,128)(2,1)S(1)}, bf16[16,3712]{1,0:T(8,128)(2,1)S(1)}, u32[]{:S(2)}, u32[]{:S(2)}) collective-permute-start(bf16[16,3712]{1,0:T(8,128)(2,1)S(1)} %slice.17), channel_id=1, source_target_pairs={{0,12},{1,13},{2,14},{3,15},{4,0},{5,1},{6,2},{7,3},{8,4},{9,5},{1... | collective-permute-start | bytes 356360 | tf_op jit(solution)/shard_map/ppermute | solution.py:19
  31.6 9.4 %collective-permute-start.6 = (bf16[16,3584]{1,0:T(8,128)(2,1)S(1)}, bf16[16,3584]{1,0:T(8,128)(2,1)S(1)}, u32[]{:S(2)}, u32[]{:S(2)}) collective-permute-start(bf16[16,3584]{1,0:T(8,128)(2,1)S(1)} %slice.16), channel_id=1, source_target_pairs={{0,4},{1,5},{2,6},{3,7},{4,8},{5,9},{6,10},{7,11},{8,12},{9,13},{1... | collective-permute-start | bytes 344072 | tf_op jit(solution)/shard_map/ppermute | solution.py:19
  44.5 8.8 %collective-permute-start.9 = (bf16[16,3584]{1,0:T(8,128)(2,1)S(1)}, bf16[16,3584]{1,0:T(8,128)(2,1)S(1)}, u32[]{:S(2)}, u32[]{:S(2)}) collective-permute-start(bf16[16,3584]{1,0:T(8,128)(2,1)S(1)} %get-tuple-element.42), channel_id=1, source_target_pairs={{0,12},{1,13},{2,14},{3,15},{4,0},{5,1},{6,2},{7,3},{8,4},{9,5},{1... | collective-permute-start | bytes 344072 | tf_op jit(solution)/shard_map/ppermute | solution.py:19
  44.6 10.5 %collective-permute-start.10 = (bf16[16,3584]{1,0:T(8,128)(2,1)S(1)}, bf16[16,3584]{1,0:T(8,128)(2,1)S(1)}, u32[]{:S(2)}, u32[]{:S(2)}) collective-permute-start(bf16[16,3584]{1,0:T(8,128)(2,1)S(1)} %get-tuple-element.45), channel_id=1, source_target_pairs={{0,4},{1,5},{2,6},{3,7},{4,8},{5,9},{6,10},{7,11},{8,12},{9,13},{1... | collective-permute-start | bytes 344072 | tf_op jit(solution)/shard_map/ppermute | solution.py:19
  47.5 10.8 %collective-permute-start.11 = (bf16[16,7168]{1,0:T(8,128)(2,1)S(1)}, bf16[16,7168]{1,0:T(8,128)(2,1)S(1)}, u32[]{:S(2)}, u32[]{:S(2)}) collective-permute-start(bf16[16,7168]{1,0:T(8,128)(2,1)S(1)} %get-tuple-element.48), channel_id=1, source_target_pairs={{0,14},{1,15},{2,0},{3,1},{4,2},{5,3},{6,4},{7,5},{8,6},{9,7},{10,... | collective-permute-start | bytes 688136 | tf_op jit(solution)/shard_map/ppermute | solution.py:19
  48.9 10.4 %collective-permute-start.12 = (bf16[16,7168]{1,0:T(8,128)(2,1)S(1)}, bf16[16,7168]{1,0:T(8,128)(2,1)S(1)}, u32[]{:S(2)}, u32[]{:S(2)}) collective-permute-start(bf16[16,7168]{1,0:T(8,128)(2,1)S(1)} %get-tuple-element.49), channel_id=1, source_target_pairs={{0,2},{1,3},{2,4},{3,5},{4,6},{5,7},{6,8},{7,9},{8,10},{9,11},{10,... | collective-permute-start | bytes 688136 | tf_op jit(solution)/shard_map/ppermute | solution.py:19
  55.1 9.7 %collective-permute-start.16 = (bf16[16,7168]{1,0:T(8,128)(2,1)S(1)}, bf16[16,7168]{1,0:T(8,128)(2,1)S(1)}, u32[]{:S(2)}, u32[]{:S(2)}) collective-permute-start(bf16[16,7168]{1,0:T(8,128)(2,1)S(1)} %get-tuple-element.54), channel_id=1, source_target_pairs={{0,2},{1,3},{2,4},{3,5},{4,6},{5,7},{6,8},{7,9},{8,10},{9,11},{10,... | collective-permute-start | bytes 688136 | tf_op jit(solution)/shard_map/ppermute | solution.py:19
  55.1 13.7 %collective-permute-start.15 = (bf16[16,7168]{1,0:T(8,128)(2,1)S(1)}, bf16[16,7168]{1,0:T(8,128)(2,1)S(1)}, u32[]{:S(2)}, u32[]{:S(2)}) collective-permute-start(bf16[16,7168]{1,0:T(8,128)(2,1)S(1)} %get-tuple-element.53), channel_id=1, source_target_pairs={{0,14},{1,15},{2,0},{3,1},{4,2},{5,3},{6,4},{7,5},{8,6},{9,7},{10,... | collective-permute-start | bytes 688136 | tf_op jit(solution)/shard_map/ppermute | solution.py:19
  59.5 18.5 %collective-permute-start.13 = (bf16[16,7168]{1,0:T(8,128)(2,1)S(1)}, bf16[16,7168]{1,0:T(8,128)(2,1)S(1)}, u32[]{:S(2)}, u32[]{:S(2)}) collective-permute-start(bf16[16,7168]{1,0:T(8,128)(2,1)S(1)} %get-tuple-element.50), channel_id=1, source_target_pairs={{0,28},{1,29},{2,30},{3,31},{4,16},{5,17},{6,18},{7,19},{8,20},{9,... | collective-permute-start | bytes 688136 | tf_op jit(solution)/shard_map/ppermute | solution.py:36
  61.2 18.1 %collective-permute-start.14 = (bf16[16,7168]{1,0:T(8,128)(2,1)S(1)}, bf16[16,7168]{1,0:T(8,128)(2,1)S(1)}, u32[]{:S(2)}, u32[]{:S(2)}) collective-permute-start(bf16[16,7168]{1,0:T(8,128)(2,1)S(1)} %get-tuple-element.51), channel_id=1, source_target_pairs={{0,20},{1,21},{2,22},{3,23},{4,24},{5,25},{6,26},{7,27},{8,28},{9,... | collective-permute-start | bytes 688136 | tf_op jit(solution)/shard_map/ppermute | solution.py:36
  68.8 13.2 %collective-permute-start.17 = (bf16[16,7168]{1,0:T(8,128)(2,1)S(1)}, bf16[16,7168]{1,0:T(8,128)(2,1)S(1)}, u32[]{:S(2)}, u32[]{:S(2)}) collective-permute-start(bf16[16,7168]{1,0:T(8,128)(2,1)S(1)} %join_near.2), channel_id=1, source_target_pairs={{0,16},{1,17},{2,18},{3,19},{4,20},{5,21},{6,22},{7,23},{8,24},{9,... | collective-permute-start | bytes 688136 | tf_op jit(solution)/shard_map/ppermute | solution.py:36
  82.2 11.5 %collective-permute-start.21 = (bf16[16,7168]{1,0:T(8,128)(2,1)S(1)}, bf16[16,7168]{1,0:T(8,128)(2,1)S(1)}, u32[]{:S(2)}, u32[]{:S(2)}) collective-permute-start(bf16[16,7168]{1,0:T(8,128)(2,1)S(1)} %add_convert_fusion.1.refs_0_), channel_id=1, source_target_pairs={{0,12},{1,13},{2,14},{3,15},{4,0},{5,1},{6,2},{7,3},{8,4},{9,5},{1... | collective-permute-start | bytes 688136 | tf_op jit(solution)/shard_map/ppermute | solution.py:19
  83.5 13.9 %collective-permute-start.20 = (bf16[16,7168]{1,0:T(8,128)(2,1)S(1)}, bf16[16,7168]{1,0:T(8,128)(2,1)S(1)}, u32[]{:S(2)}, u32[]{:S(2)}) collective-permute-start(bf16[16,7168]{1,0:T(8,128)(2,1)S(1)} %add_convert_fusion.1.refs_0_), channel_id=1, source_target_pairs={{0,4},{1,5},{2,6},{3,7},{4,8},{5,9},{6,10},{7,11},{8,12},{9,13},{1... | collective-permute-start | bytes 688136 | tf_op jit(solution)/shard_map/ppermute | solution.py:19
  85.2 14.2 %collective-permute-start.19 = (bf16[16,7168]{1,0:T(8,128)(2,1)S(1)}, bf16[16,7168]{1,0:T(8,128)(2,1)S(1)}, u32[]{:S(2)}, u32[]{:S(2)}) collective-permute-start(bf16[16,7168]{1,0:T(8,128)(2,1)S(1)} %add_convert_fusion.1.refs_0_), channel_id=1, source_target_pairs={{0,14},{1,15},{2,0},{3,1},{4,2},{5,3},{6,4},{7,5},{8,6},{9,7},{10,... | collective-permute-start | bytes 688136 | tf_op jit(solution)/shard_map/ppermute | solution.py:19
  86.8 15.5 %collective-permute-start.18 = (bf16[16,7168]{1,0:T(8,128)(2,1)S(1)}, bf16[16,7168]{1,0:T(8,128)(2,1)S(1)}, u32[]{:S(2)}, u32[]{:S(2)}) collective-permute-start(bf16[16,7168]{1,0:T(8,128)(2,1)S(1)} %add_convert_fusion.1.refs_0_), channel_id=1, source_target_pairs={{0,2},{1,3},{2,4},{3,5},{4,6},{5,7},{6,8},{7,9},{8,10},{9,11},{10,... | collective-permute-start | bytes 688136 | tf_op jit(solution)/shard_map/ppermute | solution.py:19
  93.7 17.5 %collective-permute-start.23 = (bf16[16,7168]{1,0:T(8,128)(2,1)S(1)}, bf16[16,7168]{1,0:T(8,128)(2,1)S(1)}, u32[]{:S(2)}, u32[]{:S(2)}) collective-permute-start(bf16[16,7168]{1,0:T(8,128)(2,1)S(1)} %collective-permute-done.21.refs_4_), channel_id=1, source_target_pairs={{0,14},{1,15},{2,0},{3,1},{4,2},{5,3},{6,4},{7,5},{8,6},{9,7},{10,... | collective-permute-start | bytes 688136 | tf_op jit(solution)/shard_map/ppermute | solution.py:19
  97.4 13.8 %collective-permute-start.22 = (bf16[16,7168]{1,0:T(8,128)(2,1)S(1)}, bf16[16,7168]{1,0:T(8,128)(2,1)S(1)}, u32[]{:S(2)}, u32[]{:S(2)}) collective-permute-start(bf16[16,7168]{1,0:T(8,128)(2,1)S(1)} %collective-permute-done.20.refs_3_), channel_id=1, source_target_pairs={{0,2},{1,3},{2,4},{3,5},{4,6},{5,7},{6,8},{7,9},{8,10},{9,11},{10,... | collective-permute-start | bytes 688136 | tf_op jit(solution)/shard_map/ppermute | solution.py:19
  99.4 11.8 %collective-permute-start.24 = (bf16[16,3584]{1,0:T(8,128)(2,1)S(1)}, bf16[16,3584]{1,0:T(8,128)(2,1)S(1)}, u32[]{:S(2)}, u32[]{:S(2)}) collective-permute-start(bf16[16,3584]{1,0:T(8,128)(2,1)S(1)} %slice.18), channel_id=1, source_target_pairs={{0,4},{1,5},{2,6},{3,7},{4,8},{5,9},{6,10},{7,11},{8,12},{9,13},{1... | collective-permute-start | bytes 344072 | tf_op jit(solution)/shard_map/ppermute | solution.py:19
  117.5 10.3 %collective-permute-start.28 = (bf16[16,7168]{1,0:T(8,128)(2,1)S(1)}, bf16[16,7168]{1,0:T(8,128)(2,1)S(1)}, u32[]{:S(2)}, u32[]{:S(2)}) collective-permute-start(bf16[16,7168]{1,0:T(8,128)(2,1)S(1)} %get-tuple-element.64), channel_id=1, source_target_pairs={{0,14},{1,15},{2,0},{3,1},{4,2},{5,3},{6,4},{7,5},{8,6},{9,7},{10,... | collective-permute-start | bytes 688136 | tf_op jit(solution)/shard_map/ppermute | solution.py:19
  118.9 10.6 %collective-permute-start.29 = (bf16[16,7168]{1,0:T(8,128)(2,1)S(1)}, bf16[16,7168]{1,0:T(8,128)(2,1)S(1)}, u32[]{:S(2)}, u32[]{:S(2)}) collective-permute-start(bf16[16,7168]{1,0:T(8,128)(2,1)S(1)} %get-tuple-element.65), channel_id=1, source_target_pairs={{0,2},{1,3},{2,4},{3,5},{4,6},{5,7},{6,8},{7,9},{8,10},{9,11},{10,... | collective-permute-start | bytes 688136 | tf_op jit(solution)/shard_map/ppermute | solution.py:19
  123.9 12.1 %collective-permute-start.33 = (bf16[16,7168]{1,0:T(8,128)(2,1)S(1)}, bf16[16,7168]{1,0:T(8,128)(2,1)S(1)}, u32[]{:S(2)}, u32[]{:S(2)}) collective-permute-start(bf16[16,7168]{1,0:T(8,128)(2,1)S(1)} %get-tuple-element.70), channel_id=1, source_target_pairs={{0,2},{1,3},{2,4},{3,5},{4,6},{5,7},{6,8},{7,9},{8,10},{9,11},{10,... | collective-permute-start | bytes 688136 | tf_op jit(solution)/shard_map/ppermute | solution.py:19
  126.0 10.0 %collective-permute-start.32 = (bf16[16,7168]{1,0:T(8,128)(2,1)S(1)}, bf16[16,7168]{1,0:T(8,128)(2,1)S(1)}, u32[]{:S(2)}, u32[]{:S(2)}) collective-permute-start(bf16[16,7168]{1,0:T(8,128)(2,1)S(1)} %get-tuple-element.69), channel_id=1, source_target_pairs={{0,14},{1,15},{2,0},{3,1},{4,2},{5,3},{6,4},{7,5},{8,6},{9,7},{10,... | collective-permute-start | bytes 688136 | tf_op jit(solution)/shard_map/ppermute | solution.py:19
  129.6 14.5 %collective-permute-start.30 = (bf16[16,7168]{1,0:T(8,128)(2,1)S(1)}, bf16[16,7168]{1,0:T(8,128)(2,1)S(1)}, u32[]{:S(2)}, u32[]{:S(2)}) collective-permute-start(bf16[16,7168]{1,0:T(8,128)(2,1)S(1)} %get-tuple-element.66), channel_id=1, source_target_pairs={{0,28},{1,29},{2,30},{3,31},{4,16},{5,17},{6,18},{7,19},{8,20},{9,... | collective-permute-start | bytes 688136 | tf_op jit(solution)/shard_map/ppermute | solution.py:36
  129.7 16.1 %collective-permute-start.31 = (bf16[16,7168]{1,0:T(8,128)(2,1)S(1)}, bf16[16,7168]{1,0:T(8,128)(2,1)S(1)}, u32[]{:S(2)}, u32[]{:S(2)}) collective-permute-start(bf16[16,7168]{1,0:T(8,128)(2,1)S(1)} %get-tuple-element.67), channel_id=1, source_target_pairs={{0,20},{1,21},{2,22},{3,23},{4,24},{5,25},{6,26},{7,27},{8,28},{9,... | collective-permute-start | bytes 688136 | tf_op jit(solution)/shard_map/ppermute | solution.py:36
  136.1 14.4 %collective-permute-start.34 = (bf16[16,7168]{1,0:T(8,128)(2,1)S(1)}, bf16[16,7168]{1,0:T(8,128)(2,1)S(1)}, u32[]{:S(2)}, u32[]{:S(2)}) collective-permute-start(bf16[16,7168]{1,0:T(8,128)(2,1)S(1)} %join_near.3), channel_id=1, source_target_pairs={{0,16},{1,17},{2,18},{3,19},{4,20},{5,21},{6,22},{7,23},{8,24},{9,... | collective-permute-start | bytes 688136 | tf_op jit(solution)/shard_map/ppermute | solution.py:36
  (5 other events, 64.1 us)

commit v4 on v3

--- a/solution.py
+++ b/solution.py
@@ -40,20 +40,14 @@
     return width // LANES // 2 * LANES
 
 
-def gather_first(block):
-    far_back, far_ahead = along_z(block, 2), along_z(block, -2)
-    return [block, along_z(block, 1), along_z(block, -1), far_back, far_ahead]
-
-
-def gather_second(first):
-    far_back, far_ahead = first[3], first[4]
-    cut = cut_of(far_back.shape[1])
-    return first + [
-        along_z(far_back, 1),
-        along_z(far_ahead, -1),
-        along_z(far_back[:, :cut], 2),
-        along_z(far_ahead[:, cut:], -2),
-    ]
+def gather(rows):
+    back, ahead = rows, rows
+    blocks = [rows]
+    for _ in range(3):
+        back, ahead = along_z(back, 1), along_z(ahead, -1)
+        blocks += [back, ahead]
+    cut = cut_of(rows.shape[1])
+    return blocks + [along_z(back[:, :cut], 1), along_z(ahead[:, cut:], -1)]
 
 
 def sum_to_next(outs):
@@ -345,7 +339,7 @@
 
     held_table = None
     for tick in range(TICKS):
-        pieces = gather_second(gather_first(rows))
+        pieces = gather(rows)
         outs, held_table = experts_share(
             pieces, norm_gain, weights, held_table, tick * experts
         )

time: 154 us -> 148 us (0.961); the launches traced: 151 us -> 148 us
  starting transfers between devices: 56.2 us -> 51.8 us
    ppermute x28, starting transfers between devices: 47.3 us -> 42.8 us  [along_z(): lax.ppermute(shard, 'expert', [(i, (i + 2 * by) % length) for i in range(...]
    ppermute x28, waiting for transfers between devices: 54.9 us -> 58.3 us  [along_z(): lax.ppermute(shard, 'expert', [(i, (i + 2 * by) % length) for i in range(...]
    ppermute x6, waiting for transfers between devices: 25 us -> 22.5 us  [to_next_section(): return lax.ppermute(shard, ('section', 'expert'), pairs)]
  transfers between devices with their start and end apart: 35 -> 35, of which waited for: 23 -> 27; matrix products, arithmetic and copies ran while one was open for 0% -> 0% of each run, Pallas kernels for 0% -> 0%
where the time goes in v4:
time: 148 us
  waiting for transfers between devices  80.8 us (55%)
  starting transfers between devices  51.8 us (35%)
  Pallas kernels  13.5 us (9%)
    ppermute x28, waiting for transfers between devices, along_z(): lax.ppermute(shard, 'expert', [(i, (i + 2 * by) % length) for i in range(...  58.3 us
    ppermute x28, starting transfers between devices, along_z(): lax.ppermute(shard, 'expert', [(i, (i + 2 * by) % length) for i in range(...  42.8 us
    ppermute x6, waiting for transfers between devices, to_next_section(): return lax.ppermute(shard, ('section', 'expert'), pairs)  22.5 us
    ppermute x6, starting transfers between devices, to_next_section(): return lax.ppermute(shard, ('section', 'expert'), pairs)  8.97 us
    pallas_call x2, Pallas kernels, experts_share(): pl.pallas_call(kernel, in_specs=[vmem] * len(operands), out_specs=[vmem]...  6.75 us
    pallas_call x1, Pallas kernels, prepare(): pl.pallas_call(kernel, in_specs=[hbm, hbm, hbm, vmem] + [hbm] * len(array...  6.24 us
  transfers between devices with their start and end apart: 35, of which 27 were waited for; matrix products, arithmetic and copies ran while one was open for 0% of the time, Pallas kernels for 0%

profile of v4, /device:TPU:0, one launch (start us, length us, event | category | flops | bytes accessed | tf_op | source)
XLA Modules:
  0.0 147.8 jit_solution(7518470338364897366)
XLA Ops:
  0.7 6.2 %prepare.1 = (bf16[16,7296]{1,0:T(8,128)(2,1)S(1)}, bf16[21504,256]{1,0:T(8,128)(2,1)S(1)}) custom-call(s32[3,2,56]{2,1,0:T(2,128)} %bitcast.20, bf16[16,7168]{1,0:T(8,128)(2,1)} %bitcast.19, s32[2,2,16]{2,1,0:T(2,128)} %bitcast.21, bf16[2,2,16]{2,1,0:T(2,128)(2,1)S(1)} %bitcast.15, bf16[7168,256]{1,0:T(8,128)(2,1)} %bitcast.16, bf16[7168,256]{1,0:T(8,128)(2,1)} %bitcast.17, ...), custom_call_target="tpu_custom_call" | custom-call | flops 5505024 | bytes 22020096 | tf_op jit(solution)/shard_map/prepare/pallas_call | solution.py:211
  7.0 4.2 %collective-permute-start.1 = (bf16[16,7296]{1,0:T(8,128)(2,1)S(1)}, bf16[16,7296]{1,0:T(8,128)(2,1)S(1)}, u32[]{:S(2)}, u32[]{:S(2)}) collective-permute-start(bf16[16,7296]{1,0:T(8,128)(2,1)S(1)} %get-tuple-element.38.refs_0_), channel_id=1, source_target_pairs={{0,14},{1,15},{2,0},{3,1},{4,2},{5,3},{6,4},{7,5},{8,6},{9,7},{10,... | collective-permute-start | bytes 700424 | tf_op jit(solution)/shard_map/ppermute | solution.py:19
  11.2 5.5 %collective-permute-done.1.refs_2_ = bf16[16,7296]{1,0:T(8,128)(2,1)S(1)} collective-permute-done((bf16[16,7296]{1,0:T(8,128)(2,1)S(1)}, bf16[16,7296]{1,0:T(8,128)(2,1)S(1)}, u32[]{:S(2)}, u32[]{:S(2)}) %collective-permute-start.1) | collective-permute-done | bytes 233504 | tf_op jit(solution)/shard_map/ppermute | solution.py:19
  16.8 3.7 %collective-permute-start.3 = (bf16[16,7296]{1,0:T(8,128)(2,1)S(1)}, bf16[16,7296]{1,0:T(8,128)(2,1)S(1)}, u32[]{:S(2)}, u32[]{:S(2)}) collective-permute-start(bf16[16,7296]{1,0:T(8,128)(2,1)S(1)} %collective-permute-done.1.refs_2_), channel_id=1, source_target_pairs={{0,14},{1,15},{2,0},{3,1},{4,2},{5,3},{6,4},{7,5},{8,6},{9,7},{10,... | collective-permute-start | bytes 700424 | tf_op jit(solution)/shard_map/ppermute | solution.py:19
  20.5 4.8 %collective-permute-done.3.refs_4_ = bf16[16,7296]{1,0:T(8,128)(2,1)S(1)} collective-permute-done((bf16[16,7296]{1,0:T(8,128)(2,1)S(1)}, bf16[16,7296]{1,0:T(8,128)(2,1)S(1)}, u32[]{:S(2)}, u32[]{:S(2)}) %collective-permute-start.3) | collective-permute-done | bytes 233504 | tf_op jit(solution)/shard_map/ppermute | solution.py:19
  25.2 3.7 %collective-permute-start.5 = (bf16[16,7296]{1,0:T(8,128)(2,1)S(1)}, bf16[16,7296]{1,0:T(8,128)(2,1)S(1)}, u32[]{:S(2)}, u32[]{:S(2)}) collective-permute-start(bf16[16,7296]{1,0:T(8,128)(2,1)S(1)} %collective-permute-done.3.refs_4_), channel_id=1, source_target_pairs={{0,14},{1,15},{2,0},{3,1},{4,2},{5,3},{6,4},{7,5},{8,6},{9,7},{10,... | collective-permute-start | bytes 700424 | tf_op jit(solution)/shard_map/ppermute | solution.py:19
  28.9 3.9 %collective-permute-done.5.refs_6_ = bf16[16,7296]{1,0:T(8,128)(2,1)S(1)} collective-permute-done((bf16[16,7296]{1,0:T(8,128)(2,1)S(1)}, bf16[16,7296]{1,0:T(8,128)(2,1)S(1)}, u32[]{:S(2)}, u32[]{:S(2)}) %collective-permute-start.5) | collective-permute-done | bytes 233504 | tf_op jit(solution)/shard_map/ppermute | solution.py:19
  32.8 3.8 %collective-permute-start.7 = (bf16[16,3712]{1,0:T(8,128)(2,1)S(1)}, bf16[16,3712]{1,0:T(8,128)(2,1)S(1)}, u32[]{:S(2)}, u32[]{:S(2)}) collective-permute-start(bf16[16,3712]{1,0:T(8,128)(2,1)S(1)} %slice.17), channel_id=1, source_target_pairs={{0,14},{1,15},{2,0},{3,1},{4,2},{5,3},{6,4},{7,5},{8,6},{9,7},{10,... | collective-permute-start | bytes 356360 | tf_op jit(solution)/shard_map/ppermute | solution.py:19
  36.8 6.0 %collective-permute-done.6.refs_7_ = bf16[16,3584]{1,0:T(8,128)(2,1)S(1)} collective-permute-done((bf16[16,3584]{1,0:T(8,128)(2,1)S(1)}, bf16[16,3584]{1,0:T(8,128)(2,1)S(1)}, u32[]{:S(2)}, u32[]{:S(2)}) %collective-permute-start.6) | collective-permute-done | bytes 114720 | tf_op jit(solution)/shard_map/ppermute | solution.py:19
  42.9 3.4 %experts_share.2 = (bf16[16,7168]{1,0:T(8,128)(2,1)S(1)}, bf16[16,7168]{1,0:T(8,128)(2,1)S(1)}, bf16[16,7168]{1,0:T(8,128)(2,1)S(1)}, bf16[16,7168]{1,0:T(8,128)...) custom-call(bf16[16,7296]{1,0:T(8,128)(2,1)S(1)} %get-tuple-element., ...), custom_call_target="tpu_custom_call" | custom-call | flops 2818572288 | bytes 22020096 | tf_op jit(solution)/shard_map/experts_share/pallas_call | solution.py:304
  46.4 2.9 %collective-permute-start.10 = (bf16[16,3584]{1,0:T(8,128)(2,1)S(1)}, bf16[16,3584]{1,0:T(8,128)(2,1)S(1)}, u32[]{:S(2)}, u32[]{:S(2)}) collective-permute-start(bf16[16,3584]{1,0:T(8,128)(2,1)S(1)} %get-tuple-element.45), channel_id=1, source_target_pairs={{0,4},{1,5},{2,6},{3,7},{4,8},{5,9},{6,10},{7,11},{8,12},{9,13},{1... | collective-permute-start | bytes 344072 | tf_op jit(solution)/shard_map/ppermute | solution.py:19
  52.6 2.5 %collective-permute-done.10.right = bf16[16,3584]{1,0:T(8,128)(2,1)S(1)} collective-permute-done((bf16[16,3584]{1,0:T(8,128)(2,1)S(1)}, bf16[16,3584]{1,0:T(8,128)(2,1)S(1)}, u32[]{:S(2)}, u32[]{:S(2)}) %collective-permute-start.10) | collective-permute-done | bytes 114720 | tf_op jit(solution)/shard_map/ppermute | solution.py:19
  55.1 1.9 %collective-permute-start.16 = (bf16[16,7168]{1,0:T(8,128)(2,1)S(1)}, bf16[16,7168]{1,0:T(8,128)(2,1)S(1)}, u32[]{:S(2)}, u32[]{:S(2)}) collective-permute-start(bf16[16,7168]{1,0:T(8,128)(2,1)S(1)} %get-tuple-element.54), channel_id=1, source_target_pairs={{0,2},{1,3},{2,4},{3,5},{4,6},{5,7},{6,8},{7,9},{8,10},{9,11},{10,... | collective-permute-start | bytes 688136 | tf_op jit(solution)/shard_map/ppermute | solution.py:19
  61.0 3.9 %collective-permute-start.14 = (bf16[16,7168]{1,0:T(8,128)(2,1)S(1)}, bf16[16,7168]{1,0:T(8,128)(2,1)S(1)}, u32[]{:S(2)}, u32[]{:S(2)}) collective-permute-start(bf16[16,7168]{1,0:T(8,128)(2,1)S(1)} %get-tuple-element.51), channel_id=1, source_target_pairs={{0,20},{1,21},{2,22},{3,23},{4,24},{5,25},{6,26},{7,27},{8,28},{9,... | collective-permute-start | bytes 688136 | tf_op jit(solution)/shard_map/ppermute | solution.py:36
  65.9 2.0 %collective-permute-start.17 = (bf16[16,7168]{1,0:T(8,128)(2,1)S(1)}, bf16[16,7168]{1,0:T(8,128)(2,1)S(1)}, u32[]{:S(2)}, u32[]{:S(2)}) collective-permute-start(bf16[16,7168]{1,0:T(8,128)(2,1)S(1)} %join_near.2), channel_id=1, source_target_pairs={{0,16},{1,17},{2,18},{3,19},{4,20},{5,21},{6,22},{7,23},{8,24},{9,... | collective-permute-start | bytes 688136 | tf_op jit(solution)/shard_map/ppermute | solution.py:36
  67.9 7.3 %collective-permute-done.13 = bf16[16,7168]{1,0:T(8,128)(2,1)S(1)} collective-permute-done((bf16[16,7168]{1,0:T(8,128)(2,1)S(1)}, bf16[16,7168]{1,0:T(8,128)(2,1)S(1)}, u32[]{:S(2)}, u32[]{:S(2)}) %collective-permute-start.13) | collective-permute-done | bytes 229408 | tf_op jit(solution)/shard_map/ppermute | solution.py:36
  75.8 2.6 %collective-permute-done.17 = bf16[16,7168]{1,0:T(8,128)(2,1)S(1)} collective-permute-done((bf16[16,7168]{1,0:T(8,128)(2,1)S(1)}, bf16[16,7168]{1,0:T(8,128)(2,1)S(1)}, u32[]{:S(2)}, u32[]{:S(2)}) %collective-permute-start.17) | collective-permute-done | bytes 229408 | tf_op jit(solution)/shard_map/ppermute | solution.py:36
  80.5 4.6 %collective-permute-done.19.refs_2_ = bf16[16,7168]{1,0:T(8,128)(2,1)S(1)} collective-permute-done((bf16[16,7168]{1,0:T(8,128)(2,1)S(1)}, bf16[16,7168]{1,0:T(8,128)(2,1)S(1)}, u32[]{:S(2)}, u32[]{:S(2)}) %collective-permute-start.19) | collective-permute-done | bytes 229408 | tf_op jit(solution)/shard_map/ppermute | solution.py:19
  85.1 2.2 %collective-permute-start.21 = (bf16[16,7168]{1,0:T(8,128)(2,1)S(1)}, bf16[16,7168]{1,0:T(8,128)(2,1)S(1)}, u32[]{:S(2)}, u32[]{:S(2)}) collective-permute-start(bf16[16,7168]{1,0:T(8,128)(2,1)S(1)} %collective-permute-done.19.refs_2_), channel_id=1, source_target_pairs={{0,14},{1,15},{2,0},{3,1},{4,2},{5,3},{6,4},{7,5},{8,6},{9,7},{10,... | collective-permute-start | bytes 688136 | tf_op jit(solution)/shard_map/ppermute | solution.py:19
  88.1 6.4 %collective-permute-done.21.refs_4_ = bf16[16,7168]{1,0:T(8,128)(2,1)S(1)} collective-permute-done((bf16[16,7168]{1,0:T(8,128)(2,1)S(1)}, bf16[16,7168]{1,0:T(8,128)(2,1)S(1)}, u32[]{:S(2)}, u32[]{:S(2)}) %collective-permute-start.21) | collective-permute-done | bytes 229408 | tf_op jit(solution)/shard_map/ppermute | solution.py:19
  96.6 4.5 %collective-permute-done.23.refs_6_ = bf16[16,7168]{1,0:T(8,128)(2,1)S(1)} collective-permute-done((bf16[16,7168]{1,0:T(8,128)(2,1)S(1)}, bf16[16,7168]{1,0:T(8,128)(2,1)S(1)}, u32[]{:S(2)}, u32[]{:S(2)}) %collective-permute-start.23) | collective-permute-done | bytes 229408 | tf_op jit(solution)/shard_map/ppermute | solution.py:19
  101.0 3.5 %collective-permute-start.25 = (bf16[16,3584]{1,0:T(8,128)(2,1)S(1)}, bf16[16,3584]{1,0:T(8,128)(2,1)S(1)}, u32[]{:S(2)}, u32[]{:S(2)}) collective-permute-start(bf16[16,3584]{1,0:T(8,128)(2,1)S(1)} %slice.19), channel_id=1, source_target_pairs={{0,14},{1,15},{2,0},{3,1},{4,2},{5,3},{6,4},{7,5},{8,6},{9,7},{10,... | collective-permute-start | bytes 344072 | tf_op jit(solution)/shard_map/ppermute | solution.py:19
  104.8 2.2 %collective-permute-done.25.refs_8_ = bf16[16,3584]{1,0:T(8,128)(2,1)S(1)} collective-permute-done((bf16[16,3584]{1,0:T(8,128)(2,1)S(1)}, bf16[16,3584]{1,0:T(8,128)(2,1)S(1)}, u32[]{:S(2)}, u32[]{:S(2)}) %collective-permute-start.25) | collective-permute-done | bytes 114720 | tf_op jit(solution)/shard_map/ppermute | solution.py:19
  106.9 3.8 %collective-permute-done.24.refs_7_ = bf16[16,3584]{1,0:T(8,128)(2,1)S(1)} collective-permute-done((bf16[16,3584]{1,0:T(8,128)(2,1)S(1)}, bf16[16,3584]{1,0:T(8,128)(2,1)S(1)}, u32[]{:S(2)}, u32[]{:S(2)}) %collective-permute-start.24) | collective-permute-done | bytes 114720 | tf_op jit(solution)/shard_map/ppermute | solution.py:19
  110.7 3.3 %experts_share.3 = (bf16[16,7168]{1,0:T(8,128)(2,1)S(1)}, bf16[16,7168]{1,0:T(8,128)(2,1)S(1)}, bf16[16,7168]{1,0:T(8,128)(2,1)S(1)}, bf16[16,7168]{1,0:T(8,128)...) custom-call(bf16[16,7168]{1,0:T(8,128)(2,1)S(1)} %add_convert_fusion, ...), custom_call_target="tpu_custom_call" | custom-call | flops 2818572288 | bytes 22020096 | tf_op jit(solution)/shard_map/experts_share/pallas_call | solution.py:304
  114.2 2.9 %collective-permute-start.27 = (bf16[16,3584]{1,0:T(8,128)(2,1)S(1)}, bf16[16,3584]{1,0:T(8,128)(2,1)S(1)}, u32[]{:S(2)}, u32[]{:S(2)}) collective-permute-start(bf16[16,3584]{1,0:T(8,128)(2,1)S(1)} %get-tuple-element.61), channel_id=1, source_target_pairs={{0,4},{1,5},{2,6},{3,7},{4,8},{5,9},{6,10},{7,11},{8,12},{9,13},{1... | collective-permute-start | bytes 344072 | tf_op jit(solution)/shard_map/ppermute | solution.py:19
  119.1 2.4 %collective-permute-done.26.left = bf16[16,3584]{1,0:T(8,128)(2,1)S(1)} collective-permute-done((bf16[16,3584]{1,0:T(8,128)(2,1)S(1)}, bf16[16,3584]{1,0:T(8,128)(2,1)S(1)}, u32[]{:S(2)}, u32[]{:S(2)}) %collective-permute-start.26) | collective-permute-done | bytes 114720 | tf_op jit(solution)/shard_map/ppermute | solution.py:19
  121.5 1.8 %collective-permute-done.27.right = bf16[16,3584]{1,0:T(8,128)(2,1)S(1)} collective-permute-done((bf16[16,3584]{1,0:T(8,128)(2,1)S(1)}, bf16[16,3584]{1,0:T(8,128)(2,1)S(1)}, u32[]{:S(2)}, u32[]{:S(2)}) %collective-permute-start.27) | collective-permute-done | bytes 114720 | tf_op jit(solution)/shard_map/ppermute | solution.py:19
  123.3 3.8 %collective-permute-start.33 = (bf16[16,7168]{1,0:T(8,128)(2,1)S(1)}, bf16[16,7168]{1,0:T(8,128)(2,1)S(1)}, u32[]{:S(2)}, u32[]{:S(2)}) collective-permute-start(bf16[16,7168]{1,0:T(8,128)(2,1)S(1)} %get-tuple-element.70), channel_id=1, source_target_pairs={{0,2},{1,3},{2,4},{3,5},{4,6},{5,7},{6,8},{7,9},{8,10},{9,11},{10,... | collective-permute-start | bytes 688136 | tf_op jit(solution)/shard_map/ppermute | solution.py:19
  129.5 2.1 %collective-permute-done.33.ahead = bf16[16,7168]{1,0:T(8,128)(2,1)S(1)} collective-permute-done((bf16[16,7168]{1,0:T(8,128)(2,1)S(1)}, bf16[16,7168]{1,0:T(8,128)(2,1)S(1)}, u32[]{:S(2)}, u32[]{:S(2)}) %collective-permute-start.33) | collective-permute-done | bytes 229408 | tf_op jit(solution)/shard_map/ppermute | solution.py:19
  135.0 9.7 %collective-permute-done.30 = bf16[16,7168]{1,0:T(8,128)(2,1)S(1)} collective-permute-done((bf16[16,7168]{1,0:T(8,128)(2,1)S(1)}, bf16[16,7168]{1,0:T(8,128)(2,1)S(1)}, u32[]{:S(2)}, u32[]{:S(2)}) %collective-permute-start.30) | collective-permute-done | bytes 229408 | tf_op jit(solution)/shard_map/ppermute | solution.py:36
  144.7 2.4 %collective-permute-done.34 = bf16[16,7168]{1,0:T(8,128)(2,1)S(1)} collective-permute-done((bf16[16,7168]{1,0:T(8,128)(2,1)S(1)}, bf16[16,7168]{1,0:T(8,128)(2,1)S(1)}, u32[]{:S(2)}, u32[]{:S(2)}) %collective-permute-start.34) | collective-permute-done | bytes 229408 | tf_op jit(solution)/shard_map/ppermute | solution.py:36
  (55 shorter events, 24.0 us)
Async XLA Ops:
  6.9 35.9 %collective-permute-start.8 = (bf16[21504,256]{1,0:T(8,128)(2,1)S(1)}, bf16[21504,256]{1,0:T(8,128)(2,1)S(1)}, u32[]{:S(2)}, u32[]{:S(2)}) collective-permute-start(bf16[21504,256]{1,0:T(8,128)(2,1)S(1)} %get-tuple-element.39.refs_10_), channel_id=1, source_target_pairs={{0,1},{1,0},{2,3},{3,2},{4,5},{5,4},{6,7},{7,6},{8,9},{9,8},{10,11... | collective-permute-start | bytes 33030152 | tf_op jit(solution)/shard_map/ppermute | solution.py:26
  7.0 9.7 %collective-permute-start.1 = (bf16[16,7296]{1,0:T(8,128)(2,1)S(1)}, bf16[16,7296]{1,0:T(8,128)(2,1)S(1)}, u32[]{:S(2)}, u32[]{:S(2)}) collective-permute-start(bf16[16,7296]{1,0:T(8,128)(2,1)S(1)} %get-tuple-element.38.refs_0_), channel_id=1, source_target_pairs={{0,14},{1,15},{2,0},{3,1},{4,2},{5,3},{6,4},{7,5},{8,6},{9,7},{10,... | collective-permute-start | bytes 700424 | tf_op jit(solution)/shard_map/ppermute | solution.py:19
  11.2 9.2 %collective-permute-start = (bf16[16,7296]{1,0:T(8,128)(2,1)S(1)}, bf16[16,7296]{1,0:T(8,128)(2,1)S(1)}, u32[]{:S(2)}, u32[]{:S(2)}) collective-permute-start(bf16[16,7296]{1,0:T(8,128)(2,1)S(1)} %get-tuple-element.38.refs_0_), channel_id=1, source_target_pairs={{0,2},{1,3},{2,4},{3,5},{4,6},{5,7},{6,8},{7,9},{8,10},{9,11},{10,... | collective-permute-start | bytes 700424 | tf_op jit(solution)/shard_map/ppermute | solution.py:19
  16.8 8.5 %collective-permute-start.3 = (bf16[16,7296]{1,0:T(8,128)(2,1)S(1)}, bf16[16,7296]{1,0:T(8,128)(2,1)S(1)}, u32[]{:S(2)}, u32[]{:S(2)}) collective-permute-start(bf16[16,7296]{1,0:T(8,128)(2,1)S(1)} %collective-permute-done.1.refs_2_), channel_id=1, source_target_pairs={{0,14},{1,15},{2,0},{3,1},{4,2},{5,3},{6,4},{7,5},{8,6},{9,7},{10,... | collective-permute-start | bytes 700424 | tf_op jit(solution)/shard_map/ppermute | solution.py:19
  20.5 8.5 %collective-permute-start.2 = (bf16[16,7296]{1,0:T(8,128)(2,1)S(1)}, bf16[16,7296]{1,0:T(8,128)(2,1)S(1)}, u32[]{:S(2)}, u32[]{:S(2)}) collective-permute-start(bf16[16,7296]{1,0:T(8,128)(2,1)S(1)} %collective-permute-done.refs_1_), channel_id=1, source_target_pairs={{0,2},{1,3},{2,4},{3,5},{4,6},{5,7},{6,8},{7,9},{8,10},{9,11},{10,... | collective-permute-start | bytes 700424 | tf_op jit(solution)/shard_map/ppermute | solution.py:19
  25.2 7.6 %collective-permute-start.5 = (bf16[16,7296]{1,0:T(8,128)(2,1)S(1)}, bf16[16,7296]{1,0:T(8,128)(2,1)S(1)}, u32[]{:S(2)}, u32[]{:S(2)}) collective-permute-start(bf16[16,7296]{1,0:T(8,128)(2,1)S(1)} %collective-permute-done.3.refs_4_), channel_id=1, source_target_pairs={{0,14},{1,15},{2,0},{3,1},{4,2},{5,3},{6,4},{7,5},{8,6},{9,7},{10,... | collective-permute-start | bytes 700424 | tf_op jit(solution)/shard_map/ppermute | solution.py:19
  28.9 7.6 %collective-permute-start.4 = (bf16[16,7296]{1,0:T(8,128)(2,1)S(1)}, bf16[16,7296]{1,0:T(8,128)(2,1)S(1)}, u32[]{:S(2)}, u32[]{:S(2)}) collective-permute-start(bf16[16,7296]{1,0:T(8,128)(2,1)S(1)} %collective-permute-done.2.refs_3_), channel_id=1, source_target_pairs={{0,2},{1,3},{2,4},{3,5},{4,6},{5,7},{6,8},{7,9},{8,10},{9,11},{10,... | collective-permute-start | bytes 700424 | tf_op jit(solution)/shard_map/ppermute | solution.py:19
  32.8 10.0 %collective-permute-start.7 = (bf16[16,3712]{1,0:T(8,128)(2,1)S(1)}, bf16[16,3712]{1,0:T(8,128)(2,1)S(1)}, u32[]{:S(2)}, u32[]{:S(2)}) collective-permute-start(bf16[16,3712]{1,0:T(8,128)(2,1)S(1)} %slice.17), channel_id=1, source_target_pairs={{0,14},{1,15},{2,0},{3,1},{4,2},{5,3},{6,4},{7,5},{8,6},{9,7},{10,... | collective-permute-start | bytes 356360 | tf_op jit(solution)/shard_map/ppermute | solution.py:19
  36.6 6.3 %collective-permute-start.6 = (bf16[16,3584]{1,0:T(8,128)(2,1)S(1)}, bf16[16,3584]{1,0:T(8,128)(2,1)S(1)}, u32[]{:S(2)}, u32[]{:S(2)}) collective-permute-start(bf16[16,3584]{1,0:T(8,128)(2,1)S(1)} %slice.16), channel_id=1, source_target_pairs={{0,2},{1,3},{2,4},{3,5},{4,6},{5,7},{6,8},{7,9},{8,10},{9,11},{10,... | collective-permute-start | bytes 344072 | tf_op jit(solution)/shard_map/ppermute | solution.py:19
  46.3 6.4 %collective-permute-start.9 = (bf16[16,3584]{1,0:T(8,128)(2,1)S(1)}, bf16[16,3584]{1,0:T(8,128)(2,1)S(1)}, u32[]{:S(2)}, u32[]{:S(2)}) collective-permute-start(bf16[16,3584]{1,0:T(8,128)(2,1)S(1)} %get-tuple-element.42), channel_id=1, source_target_pairs={{0,12},{1,13},{2,14},{3,15},{4,0},{5,1},{6,2},{7,3},{8,4},{9,5},{1... | collective-permute-start | bytes 344072 | tf_op jit(solution)/shard_map/ppermute | solution.py:19
  46.4 8.8 %collective-permute-start.10 = (bf16[16,3584]{1,0:T(8,128)(2,1)S(1)}, bf16[16,3584]{1,0:T(8,128)(2,1)S(1)}, u32[]{:S(2)}, u32[]{:S(2)}) collective-permute-start(bf16[16,3584]{1,0:T(8,128)(2,1)S(1)} %get-tuple-element.45), channel_id=1, source_target_pairs={{0,4},{1,5},{2,6},{3,7},{4,8},{5,9},{6,10},{7,11},{8,12},{9,13},{1... | collective-permute-start | bytes 344072 | tf_op jit(solution)/shard_map/ppermute | solution.py:19
  49.3 9.1 %collective-permute-start.11 = (bf16[16,7168]{1,0:T(8,128)(2,1)S(1)}, bf16[16,7168]{1,0:T(8,128)(2,1)S(1)}, u32[]{:S(2)}, u32[]{:S(2)}) collective-permute-start(bf16[16,7168]{1,0:T(8,128)(2,1)S(1)} %get-tuple-element.48), channel_id=1, source_target_pairs={{0,14},{1,15},{2,0},{3,1},{4,2},{5,3},{6,4},{7,5},{8,6},{9,7},{10,... | collective-permute-start | bytes 688136 | tf_op jit(solution)/shard_map/ppermute | solution.py:19
  50.3 9.5 %collective-permute-start.12 = (bf16[16,7168]{1,0:T(8,128)(2,1)S(1)}, bf16[16,7168]{1,0:T(8,128)(2,1)S(1)}, u32[]{:S(2)}, u32[]{:S(2)}) collective-permute-start(bf16[16,7168]{1,0:T(8,128)(2,1)S(1)} %get-tuple-element.49), channel_id=1, source_target_pairs={{0,2},{1,3},{2,4},{3,5},{4,6},{5,7},{6,8},{7,9},{8,10},{9,11},{10,... | collective-permute-start | bytes 688136 | tf_op jit(solution)/shard_map/ppermute | solution.py:19
  55.1 9.8 %collective-permute-start.16 = (bf16[16,7168]{1,0:T(8,128)(2,1)S(1)}, bf16[16,7168]{1,0:T(8,128)(2,1)S(1)}, u32[]{:S(2)}, u32[]{:S(2)}) collective-permute-start(bf16[16,7168]{1,0:T(8,128)(2,1)S(1)} %get-tuple-element.54), channel_id=1, source_target_pairs={{0,2},{1,3},{2,4},{3,5},{4,6},{5,7},{6,8},{7,9},{8,10},{9,11},{10,... | collective-permute-start | bytes 688136 | tf_op jit(solution)/shard_map/ppermute | solution.py:19
  57.0 8.8 %collective-permute-start.15 = (bf16[16,7168]{1,0:T(8,128)(2,1)S(1)}, bf16[16,7168]{1,0:T(8,128)(2,1)S(1)}, u32[]{:S(2)}, u32[]{:S(2)}) collective-permute-start(bf16[16,7168]{1,0:T(8,128)(2,1)S(1)} %get-tuple-element.53), channel_id=1, source_target_pairs={{0,14},{1,15},{2,0},{3,1},{4,2},{5,3},{6,4},{7,5},{8,6},{9,7},{10,... | collective-permute-start | bytes 688136 | tf_op jit(solution)/shard_map/ppermute | solution.py:19
  59.9 15.3 %collective-permute-start.13 = (bf16[16,7168]{1,0:T(8,128)(2,1)S(1)}, bf16[16,7168]{1,0:T(8,128)(2,1)S(1)}, u32[]{:S(2)}, u32[]{:S(2)}) collective-permute-start(bf16[16,7168]{1,0:T(8,128)(2,1)S(1)} %get-tuple-element.50), channel_id=1, source_target_pairs={{0,28},{1,29},{2,30},{3,31},{4,16},{5,17},{6,18},{7,19},{8,20},{9,... | collective-permute-start | bytes 688136 | tf_op jit(solution)/shard_map/ppermute | solution.py:36
  61.0 14.7 %collective-permute-start.14 = (bf16[16,7168]{1,0:T(8,128)(2,1)S(1)}, bf16[16,7168]{1,0:T(8,128)(2,1)S(1)}, u32[]{:S(2)}, u32[]{:S(2)}) collective-permute-start(bf16[16,7168]{1,0:T(8,128)(2,1)S(1)} %get-tuple-element.51), channel_id=1, source_target_pairs={{0,20},{1,21},{2,22},{3,23},{4,24},{5,25},{6,26},{7,27},{8,28},{9,... | collective-permute-start | bytes 688136 | tf_op jit(solution)/shard_map/ppermute | solution.py:36
  65.9 12.4 %collective-permute-start.17 = (bf16[16,7168]{1,0:T(8,128)(2,1)S(1)}, bf16[16,7168]{1,0:T(8,128)(2,1)S(1)}, u32[]{:S(2)}, u32[]{:S(2)}) collective-permute-start(bf16[16,7168]{1,0:T(8,128)(2,1)S(1)} %join_near.2), channel_id=1, source_target_pairs={{0,16},{1,17},{2,18},{3,19},{4,20},{5,21},{6,22},{7,23},{8,24},{9,... | collective-permute-start | bytes 688136 | tf_op jit(solution)/shard_map/ppermute | solution.py:36
  78.4 6.7 %collective-permute-start.19 = (bf16[16,7168]{1,0:T(8,128)(2,1)S(1)}, bf16[16,7168]{1,0:T(8,128)(2,1)S(1)}, u32[]{:S(2)}, u32[]{:S(2)}) collective-permute-start(bf16[16,7168]{1,0:T(8,128)(2,1)S(1)} %add_convert_fusion.1.refs_0_), channel_id=1, source_target_pairs={{0,14},{1,15},{2,0},{3,1},{4,2},{5,3},{6,4},{7,5},{8,6},{9,7},{10,... | collective-permute-start | bytes 688136 | tf_op jit(solution)/shard_map/ppermute | solution.py:19
  79.8 7.8 %collective-permute-start.18 = (bf16[16,7168]{1,0:T(8,128)(2,1)S(1)}, bf16[16,7168]{1,0:T(8,128)(2,1)S(1)}, u32[]{:S(2)}, u32[]{:S(2)}) collective-permute-start(bf16[16,7168]{1,0:T(8,128)(2,1)S(1)} %add_convert_fusion.1.refs_0_), channel_id=1, source_target_pairs={{0,2},{1,3},{2,4},{3,5},{4,6},{5,7},{6,8},{7,9},{8,10},{9,11},{10,... | collective-permute-start | bytes 688136 | tf_op jit(solution)/shard_map/ppermute | solution.py:19
  85.1 9.3 %collective-permute-start.21 = (bf16[16,7168]{1,0:T(8,128)(2,1)S(1)}, bf16[16,7168]{1,0:T(8,128)(2,1)S(1)}, u32[]{:S(2)}, u32[]{:S(2)}) collective-permute-start(bf16[16,7168]{1,0:T(8,128)(2,1)S(1)} %collective-permute-done.19.refs_2_), channel_id=1, source_target_pairs={{0,14},{1,15},{2,0},{3,1},{4,2},{5,3},{6,4},{7,5},{8,6},{9,7},{10,... | collective-permute-start | bytes 688136 | tf_op jit(solution)/shard_map/ppermute | solution.py:19
  87.6 9.0 %collective-permute-start.20 = (bf16[16,7168]{1,0:T(8,128)(2,1)S(1)}, bf16[16,7168]{1,0:T(8,128)(2,1)S(1)}, u32[]{:S(2)}, u32[]{:S(2)}) collective-permute-start(bf16[16,7168]{1,0:T(8,128)(2,1)S(1)} %collective-permute-done.18.refs_1_), channel_id=1, source_target_pairs={{0,2},{1,3},{2,4},{3,5},{4,6},{5,7},{6,8},{7,9},{8,10},{9,11},{10,... | collective-permute-start | bytes 688136 | tf_op jit(solution)/shard_map/ppermute | solution.py:19
  94.5 6.6 %collective-permute-start.23 = (bf16[16,7168]{1,0:T(8,128)(2,1)S(1)}, bf16[16,7168]{1,0:T(8,128)(2,1)S(1)}, u32[]{:S(2)}, u32[]{:S(2)}) collective-permute-start(bf16[16,7168]{1,0:T(8,128)(2,1)S(1)} %collective-permute-done.21.refs_4_), channel_id=1, source_target_pairs={{0,14},{1,15},{2,0},{3,1},{4,2},{5,3},{6,4},{7,5},{8,6},{9,7},{10,... | collective-permute-start | bytes 688136 | tf_op jit(solution)/shard_map/ppermute | solution.py:19
  96.6 8.1 %collective-permute-start.22 = (bf16[16,7168]{1,0:T(8,128)(2,1)S(1)}, bf16[16,7168]{1,0:T(8,128)(2,1)S(1)}, u32[]{:S(2)}, u32[]{:S(2)}) collective-permute-start(bf16[16,7168]{1,0:T(8,128)(2,1)S(1)} %collective-permute-done.20.refs_3_), channel_id=1, source_target_pairs={{0,2},{1,3},{2,4},{3,5},{4,6},{5,7},{6,8},{7,9},{8,10},{9,11},{10,... | collective-permute-start | bytes 688136 | tf_op jit(solution)/shard_map/ppermute | solution.py:19
  114.1 7.5 %collective-permute-start.26 = (bf16[16,3584]{1,0:T(8,128)(2,1)S(1)}, bf16[16,3584]{1,0:T(8,128)(2,1)S(1)}, u32[]{:S(2)}, u32[]{:S(2)}) collective-permute-start(bf16[16,3584]{1,0:T(8,128)(2,1)S(1)} %get-tuple-element.58), channel_id=1, source_target_pairs={{0,12},{1,13},{2,14},{3,15},{4,0},{5,1},{6,2},{7,3},{8,4},{9,5},{1... | collective-permute-start | bytes 344072 | tf_op jit(solution)/shard_map/ppermute | solution.py:19
  114.2 9.2 %collective-permute-start.27 = (bf16[16,3584]{1,0:T(8,128)(2,1)S(1)}, bf16[16,3584]{1,0:T(8,128)(2,1)S(1)}, u32[]{:S(2)}, u32[]{:S(2)}) collective-permute-start(bf16[16,3584]{1,0:T(8,128)(2,1)S(1)} %get-tuple-element.61), channel_id=1, source_target_pairs={{0,4},{1,5},{2,6},{3,7},{4,8},{5,9},{6,10},{7,11},{8,12},{9,13},{1... | collective-permute-start | bytes 344072 | tf_op jit(solution)/shard_map/ppermute | solution.py:19
  117.1 10.7 %collective-permute-start.28 = (bf16[16,7168]{1,0:T(8,128)(2,1)S(1)}, bf16[16,7168]{1,0:T(8,128)(2,1)S(1)}, u32[]{:S(2)}, u32[]{:S(2)}) collective-permute-start(bf16[16,7168]{1,0:T(8,128)(2,1)S(1)} %get-tuple-element.64), channel_id=1, source_target_pairs={{0,14},{1,15},{2,0},{3,1},{4,2},{5,3},{6,4},{7,5},{8,6},{9,7},{10,... | collective-permute-start | bytes 688136 | tf_op jit(solution)/shard_map/ppermute | solution.py:19
  118.1 11.0 %collective-permute-start.29 = (bf16[16,7168]{1,0:T(8,128)(2,1)S(1)}, bf16[16,7168]{1,0:T(8,128)(2,1)S(1)}, u32[]{:S(2)}, u32[]{:S(2)}) collective-permute-start(bf16[16,7168]{1,0:T(8,128)(2,1)S(1)} %get-tuple-element.65), channel_id=1, source_target_pairs={{0,2},{1,3},{2,4},{3,5},{4,6},{5,7},{6,8},{7,9},{8,10},{9,11},{10,... | collective-permute-start | bytes 688136 | tf_op jit(solution)/shard_map/ppermute | solution.py:19
  123.3 8.3 %collective-permute-start.33 = (bf16[16,7168]{1,0:T(8,128)(2,1)S(1)}, bf16[16,7168]{1,0:T(8,128)(2,1)S(1)}, u32[]{:S(2)}, u32[]{:S(2)}) collective-permute-start(bf16[16,7168]{1,0:T(8,128)(2,1)S(1)} %get-tuple-element.70), channel_id=1, source_target_pairs={{0,2},{1,3},{2,4},{3,5},{4,6},{5,7},{6,8},{7,9},{8,10},{9,11},{10,... | collective-permute-start | bytes 688136 | tf_op jit(solution)/shard_map/ppermute | solution.py:19
  129.3 15.4 %collective-permute-start.30 = (bf16[16,7168]{1,0:T(8,128)(2,1)S(1)}, bf16[16,7168]{1,0:T(8,128)(2,1)S(1)}, u32[]{:S(2)}, u32[]{:S(2)}) collective-permute-start(bf16[16,7168]{1,0:T(8,128)(2,1)S(1)} %get-tuple-element.66), channel_id=1, source_target_pairs={{0,28},{1,29},{2,30},{3,31},{4,16},{5,17},{6,18},{7,19},{8,20},{9,... | collective-permute-start | bytes 688136 | tf_op jit(solution)/shard_map/ppermute | solution.py:36
  129.4 15.3 %collective-permute-start.31 = (bf16[16,7168]{1,0:T(8,128)(2,1)S(1)}, bf16[16,7168]{1,0:T(8,128)(2,1)S(1)}, u32[]{:S(2)}, u32[]{:S(2)}) collective-permute-start(bf16[16,7168]{1,0:T(8,128)(2,1)S(1)} %get-tuple-element.67), channel_id=1, source_target_pairs={{0,20},{1,21},{2,22},{3,23},{4,24},{5,25},{6,26},{7,27},{8,28},{9,... | collective-permute-start | bytes 688136 | tf_op jit(solution)/shard_map/ppermute | solution.py:36
  133.2 13.8 %collective-permute-start.34 = (bf16[16,7168]{1,0:T(8,128)(2,1)S(1)}, bf16[16,7168]{1,0:T(8,128)(2,1)S(1)}, u32[]{:S(2)}, u32[]{:S(2)}) collective-permute-start(bf16[16,7168]{1,0:T(8,128)(2,1)S(1)} %join_near.3), channel_id=1, source_target_pairs={{0,16},{1,17},{2,18},{3,19},{4,20},{5,21},{6,22},{7,23},{8,24},{9,... | collective-permute-start | bytes 688136 | tf_op jit(solution)/shard_map/ppermute | solution.py:36
  (5 other events, 60.8 us)

commit v5 on v4

--- a/solution.py
+++ b/solution.py
@@ -14,10 +14,14 @@
 BF16 = jnp.bfloat16
 
 
+def z_places(place, by):
+    return 2 * by if place % 2 == 0 else -2 * by
+
+
 def along_z(shard, by):
     length = lax.axis_size("expert")
     return lax.ppermute(
-        shard, "expert", [(i, (i + 2 * by) % length) for i in range(length)]
+        shard, "expert", [(i, (i + z_places(i, by)) % length) for i in range(length)]
     )
 
 
@@ -29,7 +33,7 @@
 def to_next_section(shard, by):
     sections, length = lax.axis_size("section"), lax.axis_size("expert")
     pairs = [
-        (s * length + e, (s + 1) % sections * length + (e + 2 * by) % length)
+        (s * length + e, (s + 1) % sections * length + (e + z_places(e, by)) % length)
         for s in range(sections)
         for e in range(length)
     ]

time: 148 us -> 152 us (1.027)
  waiting for transfers between devices: 80.8 us -> 92.5 us
  starting transfers between devices: 51.8 us -> 44 us
    ppermute x28, waiting for transfers between devices: 58.3 us -> 67.9 us  [along_z(): lax.ppermute(shard, 'expert', [(i, (i + z_places(i, by)) % length) for i...]
    ppermute x28, starting transfers between devices: 42.8 us -> 35.2 us  [along_z(): lax.ppermute(shard, 'expert', [(i, (i + z_places(i, by)) % length) for i...]
    ppermute x6, waiting for transfers between devices: 22.5 us -> 24.6 us  [to_next_section(): return lax.ppermute(shard, ('section', 'expert'), pairs)]
where the time goes in v5:
time: 152 us
  waiting for transfers between devices  92.5 us (61%)
  starting transfers between devices  44 us (29%)
  Pallas kernels  13.5 us (9%)
    ppermute x28, waiting for transfers between devices, along_z(): lax.ppermute(shard, 'expert', [(i, (i + z_places(i, by)) % length) for i...  67.9 us
    ppermute x28, starting transfers between devices, along_z(): lax.ppermute(shard, 'expert', [(i, (i + z_places(i, by)) % length) for i...  35.2 us
    ppermute x6, waiting for transfers between devices, to_next_section(): return lax.ppermute(shard, ('section', 'expert'), pairs)  24.6 us
    ppermute x6, starting transfers between devices, to_next_section(): return lax.ppermute(shard, ('section', 'expert'), pairs)  8.72 us
    pallas_call x2, Pallas kernels, experts_share(): pl.pallas_call(kernel, in_specs=[vmem] * len(operands), out_specs=[vmem]...  6.77 us
    pallas_call x1, Pallas kernels, prepare(): pl.pallas_call(kernel, in_specs=[hbm, hbm, hbm, vmem] + [hbm] * len(array...  6.24 us
  transfers between devices with their start and end apart: 35, of which 27 were waited for; matrix products, arithmetic and copies ran while one was open for 0% of the time, Pallas kernels for 0%

profile of v5, /device:TPU:0, one launch (start us, length us, event | category | flops | bytes accessed | tf_op | source)
XLA Modules:
  0.0 151.7 jit_solution(6167455710819228749)
XLA Ops:
  0.7 6.2 %prepare.1 = (bf16[16,7296]{1,0:T(8,128)(2,1)S(1)}, bf16[21504,256]{1,0:T(8,128)(2,1)S(1)}) custom-call(s32[3,2,56]{2,1,0:T(2,128)} %bitcast.20, bf16[16,7168]{1,0:T(8,128)(2,1)} %bitcast.19, s32[2,2,16]{2,1,0:T(2,128)} %bitcast.21, bf16[2,2,16]{2,1,0:T(2,128)(2,1)S(1)} %bitcast.15, bf16[7168,256]{1,0:T(8,128)(2,1)} %bitcast.16, bf16[7168,256]{1,0:T(8,128)(2,1)} %bitcast.17, ...), custom_call_target="tpu_custom_call" | custom-call | flops 5505024 | bytes 22020096 | tf_op jit(solution)/shard_map/prepare/pallas_call | solution.py:215
  7.0 4.2 %collective-permute-start.1 = (bf16[16,7296]{1,0:T(8,128)(2,1)S(1)}, bf16[16,7296]{1,0:T(8,128)(2,1)S(1)}, u32[]{:S(2)}, u32[]{:S(2)}) collective-permute-start(bf16[16,7296]{1,0:T(8,128)(2,1)S(1)} %get-tuple-element.38.refs_0_), channel_id=1, source_target_pairs={{0,14},{1,3},{2,0},{3,5},{4,2},{5,7},{6,4},{7,9},{8,6},{9,11},{10,... | collective-permute-start | bytes 700424 | tf_op jit(solution)/shard_map/ppermute | solution.py:23
  11.2 5.5 %collective-permute-done.1.refs_2_ = bf16[16,7296]{1,0:T(8,128)(2,1)S(1)} collective-permute-done((bf16[16,7296]{1,0:T(8,128)(2,1)S(1)}, bf16[16,7296]{1,0:T(8,128)(2,1)S(1)}, u32[]{:S(2)}, u32[]{:S(2)}) %collective-permute-start.1) | collective-permute-done | bytes 233504 | tf_op jit(solution)/shard_map/ppermute | solution.py:23
  16.8 3.7 %collective-permute-start.3 = (bf16[16,7296]{1,0:T(8,128)(2,1)S(1)}, bf16[16,7296]{1,0:T(8,128)(2,1)S(1)}, u32[]{:S(2)}, u32[]{:S(2)}) collective-permute-start(bf16[16,7296]{1,0:T(8,128)(2,1)S(1)} %collective-permute-done.1.refs_2_), channel_id=1, source_target_pairs={{0,14},{1,3},{2,0},{3,5},{4,2},{5,7},{6,4},{7,9},{8,6},{9,11},{10,... | collective-permute-start | bytes 700424 | tf_op jit(solution)/shard_map/ppermute | solution.py:23
  20.5 4.8 %collective-permute-done.3.refs_4_ = bf16[16,7296]{1,0:T(8,128)(2,1)S(1)} collective-permute-done((bf16[16,7296]{1,0:T(8,128)(2,1)S(1)}, bf16[16,7296]{1,0:T(8,128)(2,1)S(1)}, u32[]{:S(2)}, u32[]{:S(2)}) %collective-permute-start.3) | collective-permute-done | bytes 233504 | tf_op jit(solution)/shard_map/ppermute | solution.py:23
  25.2 3.7 %collective-permute-start.5 = (bf16[16,7296]{1,0:T(8,128)(2,1)S(1)}, bf16[16,7296]{1,0:T(8,128)(2,1)S(1)}, u32[]{:S(2)}, u32[]{:S(2)}) collective-permute-start(bf16[16,7296]{1,0:T(8,128)(2,1)S(1)} %collective-permute-done.3.refs_4_), channel_id=1, source_target_pairs={{0,14},{1,3},{2,0},{3,5},{4,2},{5,7},{6,4},{7,9},{8,6},{9,11},{10,... | collective-permute-start | bytes 700424 | tf_op jit(solution)/shard_map/ppermute | solution.py:23
  29.8 3.0 %collective-permute-done.5.refs_6_ = bf16[16,7296]{1,0:T(8,128)(2,1)S(1)} collective-permute-done((bf16[16,7296]{1,0:T(8,128)(2,1)S(1)}, bf16[16,7296]{1,0:T(8,128)(2,1)S(1)}, u32[]{:S(2)}, u32[]{:S(2)}) %collective-permute-start.5) | collective-permute-done | bytes 233504 | tf_op jit(solution)/shard_map/ppermute | solution.py:23
  32.8 3.8 %collective-permute-start.7 = (bf16[16,3712]{1,0:T(8,128)(2,1)S(1)}, bf16[16,3712]{1,0:T(8,128)(2,1)S(1)}, u32[]{:S(2)}, u32[]{:S(2)}) collective-permute-start(bf16[16,3712]{1,0:T(8,128)(2,1)S(1)} %slice.17), channel_id=1, source_target_pairs={{0,14},{1,3},{2,0},{3,5},{4,2},{5,7},{6,4},{7,9},{8,6},{9,11},{10,... | collective-permute-start | bytes 356360 | tf_op jit(solution)/shard_map/ppermute | solution.py:23
  37.4 6.0 %collective-permute-done.6.refs_7_ = bf16[16,3584]{1,0:T(8,128)(2,1)S(1)} collective-permute-done((bf16[16,3584]{1,0:T(8,128)(2,1)S(1)}, bf16[16,3584]{1,0:T(8,128)(2,1)S(1)}, u32[]{:S(2)}, u32[]{:S(2)}) %collective-permute-start.6) | collective-permute-done | bytes 114720 | tf_op jit(solution)/shard_map/ppermute | solution.py:23
  43.4 3.4 %experts_share.2 = (bf16[16,7168]{1,0:T(8,128)(2,1)S(1)}, bf16[16,7168]{1,0:T(8,128)(2,1)S(1)}, bf16[16,7168]{1,0:T(8,128)(2,1)S(1)}, bf16[16,7168]{1,0:T(8,128)...) custom-call(bf16[16,7296]{1,0:T(8,128)(2,1)S(1)} %get-tuple-element., ...), custom_call_target="tpu_custom_call" | custom-call | flops 2818572288 | bytes 22020096 | tf_op jit(solution)/shard_map/experts_share/pallas_call | solution.py:308
  46.9 2.9 %collective-permute-start.10 = (bf16[16,3584]{1,0:T(8,128)(2,1)S(1)}, bf16[16,3584]{1,0:T(8,128)(2,1)S(1)}, u32[]{:S(2)}, u32[]{:S(2)}) collective-permute-start(bf16[16,3584]{1,0:T(8,128)(2,1)S(1)} %get-tuple-element.45), channel_id=1, source_target_pairs={{0,4},{1,13},{2,6},{3,15},{4,8},{5,1},{6,10},{7,3},{8,12},{9,5},{1... | collective-permute-start | bytes 344072 | tf_op jit(solution)/shard_map/ppermute | solution.py:23
  51.9 2.5 %collective-permute-done.9.left = bf16[16,3584]{1,0:T(8,128)(2,1)S(1)} collective-permute-done((bf16[16,3584]{1,0:T(8,128)(2,1)S(1)}, bf16[16,3584]{1,0:T(8,128)(2,1)S(1)}, u32[]{:S(2)}, u32[]{:S(2)}) %collective-permute-start.9) | collective-permute-done | bytes 114720 | tf_op jit(solution)/shard_map/ppermute | solution.py:23
  55.9 2.3 %collective-permute-start.15 = (bf16[16,7168]{1,0:T(8,128)(2,1)S(1)}, bf16[16,7168]{1,0:T(8,128)(2,1)S(1)}, u32[]{:S(2)}, u32[]{:S(2)}) collective-permute-start(bf16[16,7168]{1,0:T(8,128)(2,1)S(1)} %get-tuple-element.53), channel_id=1, source_target_pairs={{0,14},{1,3},{2,0},{3,5},{4,2},{5,7},{6,4},{7,9},{8,6},{9,11},{10,... | collective-permute-start | bytes 688136 | tf_op jit(solution)/shard_map/ppermute | solution.py:23
  58.3 4.0 %collective-permute-done.12.a3 = bf16[16,7168]{1,0:T(8,128)(2,1)S(1)} collective-permute-done((bf16[16,7168]{1,0:T(8,128)(2,1)S(1)}, bf16[16,7168]{1,0:T(8,128)(2,1)S(1)}, u32[]{:S(2)}, u32[]{:S(2)}) %collective-permute-start.12) | collective-permute-done | bytes 229408 | tf_op jit(solution)/shard_map/ppermute | solution.py:23
  62.5 4.8 %collective-permute-start.14 = (bf16[16,7168]{1,0:T(8,128)(2,1)S(1)}, bf16[16,7168]{1,0:T(8,128)(2,1)S(1)}, u32[]{:S(2)}, u32[]{:S(2)}) collective-permute-start(bf16[16,7168]{1,0:T(8,128)(2,1)S(1)} %get-tuple-element.51), channel_id=1, source_target_pairs={{0,20},{1,29},{2,22},{3,31},{4,24},{5,17},{6,26},{7,19},{8,28},{9,... | collective-permute-start | bytes 688136 | tf_op jit(solution)/shard_map/ppermute | solution.py:40
  70.6 8.8 %collective-permute-done.13 = bf16[16,7168]{1,0:T(8,128)(2,1)S(1)} collective-permute-done((bf16[16,7168]{1,0:T(8,128)(2,1)S(1)}, bf16[16,7168]{1,0:T(8,128)(2,1)S(1)}, u32[]{:S(2)}, u32[]{:S(2)}) %collective-permute-start.13) | collective-permute-done | bytes 229408 | tf_op jit(solution)/shard_map/ppermute | solution.py:40
  79.4 2.5 %collective-permute-done.17 = bf16[16,7168]{1,0:T(8,128)(2,1)S(1)} collective-permute-done((bf16[16,7168]{1,0:T(8,128)(2,1)S(1)}, bf16[16,7168]{1,0:T(8,128)(2,1)S(1)}, u32[]{:S(2)}, u32[]{:S(2)}) %collective-permute-start.17) | collective-permute-done | bytes 229408 | tf_op jit(solution)/shard_map/ppermute | solution.py:40
  82.2 1.9 %collective-permute-start.18 = (bf16[16,7168]{1,0:T(8,128)(2,1)S(1)}, bf16[16,7168]{1,0:T(8,128)(2,1)S(1)}, u32[]{:S(2)}, u32[]{:S(2)}) collective-permute-start(bf16[16,7168]{1,0:T(8,128)(2,1)S(1)} %add_convert_fusion.1.refs_0_), channel_id=1, source_target_pairs={{0,2},{1,15},{2,4},{3,1},{4,6},{5,3},{6,8},{7,5},{8,10},{9,7},{10,... | collective-permute-start | bytes 688136 | tf_op jit(solution)/shard_map/ppermute | solution.py:23
  84.1 5.3 %collective-permute-done.19.refs_2_ = bf16[16,7168]{1,0:T(8,128)(2,1)S(1)} collective-permute-done((bf16[16,7168]{1,0:T(8,128)(2,1)S(1)}, bf16[16,7168]{1,0:T(8,128)(2,1)S(1)}, u32[]{:S(2)}, u32[]{:S(2)}) %collective-permute-start.19) | collective-permute-done | bytes 229408 | tf_op jit(solution)/shard_map/ppermute | solution.py:23
  91.4 6.2 %collective-permute-done.21.refs_4_ = bf16[16,7168]{1,0:T(8,128)(2,1)S(1)} collective-permute-done((bf16[16,7168]{1,0:T(8,128)(2,1)S(1)}, bf16[16,7168]{1,0:T(8,128)(2,1)S(1)}, u32[]{:S(2)}, u32[]{:S(2)}) %collective-permute-start.21) | collective-permute-done | bytes 229408 | tf_op jit(solution)/shard_map/ppermute | solution.py:23
  97.6 1.9 %collective-permute-done.20.refs_3_ = bf16[16,7168]{1,0:T(8,128)(2,1)S(1)} collective-permute-done((bf16[16,7168]{1,0:T(8,128)(2,1)S(1)}, bf16[16,7168]{1,0:T(8,128)(2,1)S(1)}, u32[]{:S(2)}, u32[]{:S(2)}) %collective-permute-start.20) | collective-permute-done | bytes 229408 | tf_op jit(solution)/shard_map/ppermute | solution.py:23
  99.6 4.9 %collective-permute-done.23.refs_6_ = bf16[16,7168]{1,0:T(8,128)(2,1)S(1)} collective-permute-done((bf16[16,7168]{1,0:T(8,128)(2,1)S(1)}, bf16[16,7168]{1,0:T(8,128)(2,1)S(1)}, u32[]{:S(2)}, u32[]{:S(2)}) %collective-permute-start.23) | collective-permute-done | bytes 229408 | tf_op jit(solution)/shard_map/ppermute | solution.py:23
  104.9 1.8 %collective-permute-done.22.refs_5_ = bf16[16,7168]{1,0:T(8,128)(2,1)S(1)} collective-permute-done((bf16[16,7168]{1,0:T(8,128)(2,1)S(1)}, bf16[16,7168]{1,0:T(8,128)(2,1)S(1)}, u32[]{:S(2)}, u32[]{:S(2)}) %collective-permute-start.22) | collective-permute-done | bytes 229408 | tf_op jit(solution)/shard_map/ppermute | solution.py:23
  106.8 2.6 %collective-permute-done.25.refs_8_ = bf16[16,3584]{1,0:T(8,128)(2,1)S(1)} collective-permute-done((bf16[16,3584]{1,0:T(8,128)(2,1)S(1)}, bf16[16,3584]{1,0:T(8,128)(2,1)S(1)}, u32[]{:S(2)}, u32[]{:S(2)}) %collective-permute-start.25) | collective-permute-done | bytes 114720 | tf_op jit(solution)/shard_map/ppermute | solution.py:23
  109.4 5.6 %collective-permute-done.24.refs_7_ = bf16[16,3584]{1,0:T(8,128)(2,1)S(1)} collective-permute-done((bf16[16,3584]{1,0:T(8,128)(2,1)S(1)}, bf16[16,3584]{1,0:T(8,128)(2,1)S(1)}, u32[]{:S(2)}, u32[]{:S(2)}) %collective-permute-start.24) | collective-permute-done | bytes 114720 | tf_op jit(solution)/shard_map/ppermute | solution.py:23
  115.0 3.3 %experts_share.3 = (bf16[16,7168]{1,0:T(8,128)(2,1)S(1)}, bf16[16,7168]{1,0:T(8,128)(2,1)S(1)}, bf16[16,7168]{1,0:T(8,128)(2,1)S(1)}, bf16[16,7168]{1,0:T(8,128)...) custom-call(bf16[16,7168]{1,0:T(8,128)(2,1)S(1)} %add_convert_fusion, ...), custom_call_target="tpu_custom_call" | custom-call | flops 2818572288 | bytes 22020096 | tf_op jit(solution)/shard_map/experts_share/pallas_call | solution.py:308
  118.4 2.9 %collective-permute-start.27 = (bf16[16,3584]{1,0:T(8,128)(2,1)S(1)}, bf16[16,3584]{1,0:T(8,128)(2,1)S(1)}, u32[]{:S(2)}, u32[]{:S(2)}) collective-permute-start(bf16[16,3584]{1,0:T(8,128)(2,1)S(1)} %get-tuple-element.61), channel_id=1, source_target_pairs={{0,4},{1,13},{2,6},{3,15},{4,8},{5,1},{6,10},{7,3},{8,12},{9,5},{1... | collective-permute-start | bytes 344072 | tf_op jit(solution)/shard_map/ppermute | solution.py:23
  123.3 3.4 %collective-permute-done.26.left = bf16[16,3584]{1,0:T(8,128)(2,1)S(1)} collective-permute-done((bf16[16,3584]{1,0:T(8,128)(2,1)S(1)}, bf16[16,3584]{1,0:T(8,128)(2,1)S(1)}, u32[]{:S(2)}, u32[]{:S(2)}) %collective-permute-start.26) | collective-permute-done | bytes 114720 | tf_op jit(solution)/shard_map/ppermute | solution.py:23
  128.1 2.0 %collective-permute-start.33 = (bf16[16,7168]{1,0:T(8,128)(2,1)S(1)}, bf16[16,7168]{1,0:T(8,128)(2,1)S(1)}, u32[]{:S(2)}, u32[]{:S(2)}) collective-permute-start(bf16[16,7168]{1,0:T(8,128)(2,1)S(1)} %get-tuple-element.70), channel_id=1, source_target_pairs={{0,2},{1,15},{2,4},{3,1},{4,6},{5,3},{6,8},{7,5},{8,10},{9,7},{10,... | collective-permute-start | bytes 688136 | tf_op jit(solution)/shard_map/ppermute | solution.py:23
  131.4 2.8 %collective-permute-done.29.a3 = bf16[16,7168]{1,0:T(8,128)(2,1)S(1)} collective-permute-done((bf16[16,7168]{1,0:T(8,128)(2,1)S(1)}, bf16[16,7168]{1,0:T(8,128)(2,1)S(1)}, u32[]{:S(2)}, u32[]{:S(2)}) %collective-permute-start.29) | collective-permute-done | bytes 229408 | tf_op jit(solution)/shard_map/ppermute | solution.py:23
  137.6 9.7 %collective-permute-done.30 = bf16[16,7168]{1,0:T(8,128)(2,1)S(1)} collective-permute-done((bf16[16,7168]{1,0:T(8,128)(2,1)S(1)}, bf16[16,7168]{1,0:T(8,128)(2,1)S(1)}, u32[]{:S(2)}, u32[]{:S(2)}) %collective-permute-start.30) | collective-permute-done | bytes 229408 | tf_op jit(solution)/shard_map/ppermute | solution.py:40
  147.3 2.0 %collective-permute-done.31 = bf16[16,7168]{1,0:T(8,128)(2,1)S(1)} collective-permute-done((bf16[16,7168]{1,0:T(8,128)(2,1)S(1)}, bf16[16,7168]{1,0:T(8,128)(2,1)S(1)}, u32[]{:S(2)}, u32[]{:S(2)}) %collective-permute-start.31) | collective-permute-done | bytes 229408 | tf_op jit(solution)/shard_map/ppermute | solution.py:40
  (55 shorter events, 23.3 us)
Async XLA Ops:
  6.9 36.5 %collective-permute-start.8 = (bf16[21504,256]{1,0:T(8,128)(2,1)S(1)}, bf16[21504,256]{1,0:T(8,128)(2,1)S(1)}, u32[]{:S(2)}, u32[]{:S(2)}) collective-permute-start(bf16[21504,256]{1,0:T(8,128)(2,1)S(1)} %get-tuple-element.39.refs_10_), channel_id=1, source_target_pairs={{0,1},{1,0},{2,3},{3,2},{4,5},{5,4},{6,7},{7,6},{8,9},{9,8},{10,11... | collective-permute-start | bytes 33030152 | tf_op jit(solution)/shard_map/ppermute | solution.py:30
  7.0 9.8 %collective-permute-start.1 = (bf16[16,7296]{1,0:T(8,128)(2,1)S(1)}, bf16[16,7296]{1,0:T(8,128)(2,1)S(1)}, u32[]{:S(2)}, u32[]{:S(2)}) collective-permute-start(bf16[16,7296]{1,0:T(8,128)(2,1)S(1)} %get-tuple-element.38.refs_0_), channel_id=1, source_target_pairs={{0,14},{1,3},{2,0},{3,5},{4,2},{5,7},{6,4},{7,9},{8,6},{9,11},{10,... | collective-permute-start | bytes 700424 | tf_op jit(solution)/shard_map/ppermute | solution.py:23
  11.2 9.2 %collective-permute-start = (bf16[16,7296]{1,0:T(8,128)(2,1)S(1)}, bf16[16,7296]{1,0:T(8,128)(2,1)S(1)}, u32[]{:S(2)}, u32[]{:S(2)}) collective-permute-start(bf16[16,7296]{1,0:T(8,128)(2,1)S(1)} %get-tuple-element.38.refs_0_), channel_id=1, source_target_pairs={{0,2},{1,15},{2,4},{3,1},{4,6},{5,3},{6,8},{7,5},{8,10},{9,7},{10,... | collective-permute-start | bytes 700424 | tf_op jit(solution)/shard_map/ppermute | solution.py:23
  16.8 8.5 %collective-permute-start.3 = (bf16[16,7296]{1,0:T(8,128)(2,1)S(1)}, bf16[16,7296]{1,0:T(8,128)(2,1)S(1)}, u32[]{:S(2)}, u32[]{:S(2)}) collective-permute-start(bf16[16,7296]{1,0:T(8,128)(2,1)S(1)} %collective-permute-done.1.refs_2_), channel_id=1, source_target_pairs={{0,14},{1,3},{2,0},{3,5},{4,2},{5,7},{6,4},{7,9},{8,6},{9,11},{10,... | collective-permute-start | bytes 700424 | tf_op jit(solution)/shard_map/ppermute | solution.py:23
  20.5 9.3 %collective-permute-start.2 = (bf16[16,7296]{1,0:T(8,128)(2,1)S(1)}, bf16[16,7296]{1,0:T(8,128)(2,1)S(1)}, u32[]{:S(2)}, u32[]{:S(2)}) collective-permute-start(bf16[16,7296]{1,0:T(8,128)(2,1)S(1)} %collective-permute-done.refs_1_), channel_id=1, source_target_pairs={{0,2},{1,15},{2,4},{3,1},{4,6},{5,3},{6,8},{7,5},{8,10},{9,7},{10,... | collective-permute-start | bytes 700424 | tf_op jit(solution)/shard_map/ppermute | solution.py:23
  25.2 7.6 %collective-permute-start.5 = (bf16[16,7296]{1,0:T(8,128)(2,1)S(1)}, bf16[16,7296]{1,0:T(8,128)(2,1)S(1)}, u32[]{:S(2)}, u32[]{:S(2)}) collective-permute-start(bf16[16,7296]{1,0:T(8,128)(2,1)S(1)} %collective-permute-done.3.refs_4_), channel_id=1, source_target_pairs={{0,14},{1,3},{2,0},{3,5},{4,2},{5,7},{6,4},{7,9},{8,6},{9,11},{10,... | collective-permute-start | bytes 700424 | tf_op jit(solution)/shard_map/ppermute | solution.py:23
  29.8 7.4 %collective-permute-start.4 = (bf16[16,7296]{1,0:T(8,128)(2,1)S(1)}, bf16[16,7296]{1,0:T(8,128)(2,1)S(1)}, u32[]{:S(2)}, u32[]{:S(2)}) collective-permute-start(bf16[16,7296]{1,0:T(8,128)(2,1)S(1)} %collective-permute-done.2.refs_3_), channel_id=1, source_target_pairs={{0,2},{1,15},{2,4},{3,1},{4,6},{5,3},{6,8},{7,5},{8,10},{9,7},{10,... | collective-permute-start | bytes 700424 | tf_op jit(solution)/shard_map/ppermute | solution.py:23
  32.8 10.6 %collective-permute-start.7 = (bf16[16,3712]{1,0:T(8,128)(2,1)S(1)}, bf16[16,3712]{1,0:T(8,128)(2,1)S(1)}, u32[]{:S(2)}, u32[]{:S(2)}) collective-permute-start(bf16[16,3712]{1,0:T(8,128)(2,1)S(1)} %slice.17), channel_id=1, source_target_pairs={{0,14},{1,3},{2,0},{3,5},{4,2},{5,7},{6,4},{7,9},{8,6},{9,11},{10,... | collective-permute-start | bytes 356360 | tf_op jit(solution)/shard_map/ppermute | solution.py:23
  46.8 7.5 %collective-permute-start.9 = (bf16[16,3584]{1,0:T(8,128)(2,1)S(1)}, bf16[16,3584]{1,0:T(8,128)(2,1)S(1)}, u32[]{:S(2)}, u32[]{:S(2)}) collective-permute-start(bf16[16,3584]{1,0:T(8,128)(2,1)S(1)} %get-tuple-element.42), channel_id=1, source_target_pairs={{0,12},{1,5},{2,14},{3,7},{4,0},{5,9},{6,2},{7,11},{8,4},{9,13},{1... | collective-permute-start | bytes 344072 | tf_op jit(solution)/shard_map/ppermute | solution.py:23
  46.9 8.1 %collective-permute-start.10 = (bf16[16,3584]{1,0:T(8,128)(2,1)S(1)}, bf16[16,3584]{1,0:T(8,128)(2,1)S(1)}, u32[]{:S(2)}, u32[]{:S(2)}) collective-permute-start(bf16[16,3584]{1,0:T(8,128)(2,1)S(1)} %get-tuple-element.45), channel_id=1, source_target_pairs={{0,4},{1,13},{2,6},{3,15},{4,8},{5,1},{6,10},{7,3},{8,12},{9,5},{1... | collective-permute-start | bytes 344072 | tf_op jit(solution)/shard_map/ppermute | solution.py:23
  49.8 8.4 %collective-permute-start.11 = (bf16[16,7168]{1,0:T(8,128)(2,1)S(1)}, bf16[16,7168]{1,0:T(8,128)(2,1)S(1)}, u32[]{:S(2)}, u32[]{:S(2)}) collective-permute-start(bf16[16,7168]{1,0:T(8,128)(2,1)S(1)} %get-tuple-element.48), channel_id=1, source_target_pairs={{0,14},{1,3},{2,0},{3,5},{4,2},{5,7},{6,4},{7,9},{8,6},{9,11},{10,... | collective-permute-start | bytes 688136 | tf_op jit(solution)/shard_map/ppermute | solution.py:23
  50.7 11.6 %collective-permute-start.12 = (bf16[16,7168]{1,0:T(8,128)(2,1)S(1)}, bf16[16,7168]{1,0:T(8,128)(2,1)S(1)}, u32[]{:S(2)}, u32[]{:S(2)}) collective-permute-start(bf16[16,7168]{1,0:T(8,128)(2,1)S(1)} %get-tuple-element.49), channel_id=1, source_target_pairs={{0,2},{1,15},{2,4},{3,1},{4,6},{5,3},{6,8},{7,5},{8,10},{9,7},{10,... | collective-permute-start | bytes 688136 | tf_op jit(solution)/shard_map/ppermute | solution.py:23
  55.0 12.3 %collective-permute-start.16 = (bf16[16,7168]{1,0:T(8,128)(2,1)S(1)}, bf16[16,7168]{1,0:T(8,128)(2,1)S(1)}, u32[]{:S(2)}, u32[]{:S(2)}) collective-permute-start(bf16[16,7168]{1,0:T(8,128)(2,1)S(1)} %get-tuple-element.54), channel_id=1, source_target_pairs={{0,2},{1,15},{2,4},{3,1},{4,6},{5,3},{6,8},{7,5},{8,10},{9,7},{10,... | collective-permute-start | bytes 688136 | tf_op jit(solution)/shard_map/ppermute | solution.py:23
  55.9 12.9 %collective-permute-start.15 = (bf16[16,7168]{1,0:T(8,128)(2,1)S(1)}, bf16[16,7168]{1,0:T(8,128)(2,1)S(1)}, u32[]{:S(2)}, u32[]{:S(2)}) collective-permute-start(bf16[16,7168]{1,0:T(8,128)(2,1)S(1)} %get-tuple-element.53), channel_id=1, source_target_pairs={{0,14},{1,3},{2,0},{3,5},{4,2},{5,7},{6,4},{7,9},{8,6},{9,11},{10,... | collective-permute-start | bytes 688136 | tf_op jit(solution)/shard_map/ppermute | solution.py:23
  62.4 17.0 %collective-permute-start.13 = (bf16[16,7168]{1,0:T(8,128)(2,1)S(1)}, bf16[16,7168]{1,0:T(8,128)(2,1)S(1)}, u32[]{:S(2)}, u32[]{:S(2)}) collective-permute-start(bf16[16,7168]{1,0:T(8,128)(2,1)S(1)} %get-tuple-element.50), channel_id=1, source_target_pairs={{0,28},{1,21},{2,30},{3,23},{4,16},{5,25},{6,18},{7,27},{8,20},{9,... | collective-permute-start | bytes 688136 | tf_op jit(solution)/shard_map/ppermute | solution.py:40
  62.5 16.9 %collective-permute-start.14 = (bf16[16,7168]{1,0:T(8,128)(2,1)S(1)}, bf16[16,7168]{1,0:T(8,128)(2,1)S(1)}, u32[]{:S(2)}, u32[]{:S(2)}) collective-permute-start(bf16[16,7168]{1,0:T(8,128)(2,1)S(1)} %get-tuple-element.51), channel_id=1, source_target_pairs={{0,20},{1,29},{2,22},{3,31},{4,24},{5,17},{6,26},{7,19},{8,28},{9,... | collective-permute-start | bytes 688136 | tf_op jit(solution)/shard_map/ppermute | solution.py:40
  68.9 12.9 %collective-permute-start.17 = (bf16[16,7168]{1,0:T(8,128)(2,1)S(1)}, bf16[16,7168]{1,0:T(8,128)(2,1)S(1)}, u32[]{:S(2)}, u32[]{:S(2)}) collective-permute-start(bf16[16,7168]{1,0:T(8,128)(2,1)S(1)} %join_near.2), channel_id=1, source_target_pairs={{0,16},{1,17},{2,18},{3,19},{4,20},{5,21},{6,22},{7,23},{8,24},{9,... | collective-permute-start | bytes 688136 | tf_op jit(solution)/shard_map/ppermute | solution.py:40
  82.0 7.4 %collective-permute-start.19 = (bf16[16,7168]{1,0:T(8,128)(2,1)S(1)}, bf16[16,7168]{1,0:T(8,128)(2,1)S(1)}, u32[]{:S(2)}, u32[]{:S(2)}) collective-permute-start(bf16[16,7168]{1,0:T(8,128)(2,1)S(1)} %add_convert_fusion.1.refs_0_), channel_id=1, source_target_pairs={{0,14},{1,3},{2,0},{3,5},{4,2},{5,7},{6,4},{7,9},{8,6},{9,11},{10,... | collective-permute-start | bytes 688136 | tf_op jit(solution)/shard_map/ppermute | solution.py:23
  82.2 9.0 %collective-permute-start.18 = (bf16[16,7168]{1,0:T(8,128)(2,1)S(1)}, bf16[16,7168]{1,0:T(8,128)(2,1)S(1)}, u32[]{:S(2)}, u32[]{:S(2)}) collective-permute-start(bf16[16,7168]{1,0:T(8,128)(2,1)S(1)} %add_convert_fusion.1.refs_0_), channel_id=1, source_target_pairs={{0,2},{1,15},{2,4},{3,1},{4,6},{5,3},{6,8},{7,5},{8,10},{9,7},{10,... | collective-permute-start | bytes 688136 | tf_op jit(solution)/shard_map/ppermute | solution.py:23
  89.4 8.2 %collective-permute-start.21 = (bf16[16,7168]{1,0:T(8,128)(2,1)S(1)}, bf16[16,7168]{1,0:T(8,128)(2,1)S(1)}, u32[]{:S(2)}, u32[]{:S(2)}) collective-permute-start(bf16[16,7168]{1,0:T(8,128)(2,1)S(1)} %collective-permute-done.19.refs_2_), channel_id=1, source_target_pairs={{0,14},{1,3},{2,0},{3,5},{4,2},{5,7},{6,4},{7,9},{8,6},{9,11},{10,... | collective-permute-start | bytes 688136 | tf_op jit(solution)/shard_map/ppermute | solution.py:23
  91.2 8.2 %collective-permute-start.20 = (bf16[16,7168]{1,0:T(8,128)(2,1)S(1)}, bf16[16,7168]{1,0:T(8,128)(2,1)S(1)}, u32[]{:S(2)}, u32[]{:S(2)}) collective-permute-start(bf16[16,7168]{1,0:T(8,128)(2,1)S(1)} %collective-permute-done.18.refs_1_), channel_id=1, source_target_pairs={{0,2},{1,15},{2,4},{3,1},{4,6},{5,3},{6,8},{7,5},{8,10},{9,7},{10,... | collective-permute-start | bytes 688136 | tf_op jit(solution)/shard_map/ppermute | solution.py:23
  97.6 6.9 %collective-permute-start.23 = (bf16[16,7168]{1,0:T(8,128)(2,1)S(1)}, bf16[16,7168]{1,0:T(8,128)(2,1)S(1)}, u32[]{:S(2)}, u32[]{:S(2)}) collective-permute-start(bf16[16,7168]{1,0:T(8,128)(2,1)S(1)} %collective-permute-done.21.refs_4_), channel_id=1, source_target_pairs={{0,14},{1,3},{2,0},{3,5},{4,2},{5,7},{6,4},{7,9},{8,6},{9,11},{10,... | collective-permute-start | bytes 688136 | tf_op jit(solution)/shard_map/ppermute | solution.py:23
  99.4 7.2 %collective-permute-start.22 = (bf16[16,7168]{1,0:T(8,128)(2,1)S(1)}, bf16[16,7168]{1,0:T(8,128)(2,1)S(1)}, u32[]{:S(2)}, u32[]{:S(2)}) collective-permute-start(bf16[16,7168]{1,0:T(8,128)(2,1)S(1)} %collective-permute-done.20.refs_3_), channel_id=1, source_target_pairs={{0,2},{1,15},{2,4},{3,1},{4,6},{5,3},{6,8},{7,5},{8,10},{9,7},{10,... | collective-permute-start | bytes 688136 | tf_op jit(solution)/shard_map/ppermute | solution.py:23
  106.7 8.3 %collective-permute-start.24 = (bf16[16,3584]{1,0:T(8,128)(2,1)S(1)}, bf16[16,3584]{1,0:T(8,128)(2,1)S(1)}, u32[]{:S(2)}, u32[]{:S(2)}) collective-permute-start(bf16[16,3584]{1,0:T(8,128)(2,1)S(1)} %slice.18), channel_id=1, source_target_pairs={{0,2},{1,15},{2,4},{3,1},{4,6},{5,3},{6,8},{7,5},{8,10},{9,7},{10,... | collective-permute-start | bytes 344072 | tf_op jit(solution)/shard_map/ppermute | solution.py:23
  118.3 8.4 %collective-permute-start.26 = (bf16[16,3584]{1,0:T(8,128)(2,1)S(1)}, bf16[16,3584]{1,0:T(8,128)(2,1)S(1)}, u32[]{:S(2)}, u32[]{:S(2)}) collective-permute-start(bf16[16,3584]{1,0:T(8,128)(2,1)S(1)} %get-tuple-element.58), channel_id=1, source_target_pairs={{0,12},{1,5},{2,14},{3,7},{4,0},{5,9},{6,2},{7,11},{8,4},{9,13},{1... | collective-permute-start | bytes 344072 | tf_op jit(solution)/shard_map/ppermute | solution.py:23
  118.4 9.7 %collective-permute-start.27 = (bf16[16,3584]{1,0:T(8,128)(2,1)S(1)}, bf16[16,3584]{1,0:T(8,128)(2,1)S(1)}, u32[]{:S(2)}, u32[]{:S(2)}) collective-permute-start(bf16[16,3584]{1,0:T(8,128)(2,1)S(1)} %get-tuple-element.61), channel_id=1, source_target_pairs={{0,4},{1,13},{2,6},{3,15},{4,8},{5,1},{6,10},{7,3},{8,12},{9,5},{1... | collective-permute-start | bytes 344072 | tf_op jit(solution)/shard_map/ppermute | solution.py:23
  121.3 10.1 %collective-permute-start.28 = (bf16[16,7168]{1,0:T(8,128)(2,1)S(1)}, bf16[16,7168]{1,0:T(8,128)(2,1)S(1)}, u32[]{:S(2)}, u32[]{:S(2)}) collective-permute-start(bf16[16,7168]{1,0:T(8,128)(2,1)S(1)} %get-tuple-element.64), channel_id=1, source_target_pairs={{0,14},{1,3},{2,0},{3,5},{4,2},{5,7},{6,4},{7,9},{8,6},{9,11},{10,... | collective-permute-start | bytes 688136 | tf_op jit(solution)/shard_map/ppermute | solution.py:23
  121.9 12.2 %collective-permute-start.29 = (bf16[16,7168]{1,0:T(8,128)(2,1)S(1)}, bf16[16,7168]{1,0:T(8,128)(2,1)S(1)}, u32[]{:S(2)}, u32[]{:S(2)}) collective-permute-start(bf16[16,7168]{1,0:T(8,128)(2,1)S(1)} %get-tuple-element.65), channel_id=1, source_target_pairs={{0,2},{1,15},{2,4},{3,1},{4,6},{5,3},{6,8},{7,5},{8,10},{9,7},{10,... | collective-permute-start | bytes 688136 | tf_op jit(solution)/shard_map/ppermute | solution.py:23
  128.1 8.6 %collective-permute-start.33 = (bf16[16,7168]{1,0:T(8,128)(2,1)S(1)}, bf16[16,7168]{1,0:T(8,128)(2,1)S(1)}, u32[]{:S(2)}, u32[]{:S(2)}) collective-permute-start(bf16[16,7168]{1,0:T(8,128)(2,1)S(1)} %get-tuple-element.70), channel_id=1, source_target_pairs={{0,2},{1,15},{2,4},{3,1},{4,6},{5,3},{6,8},{7,5},{8,10},{9,7},{10,... | collective-permute-start | bytes 688136 | tf_op jit(solution)/shard_map/ppermute | solution.py:23
  134.3 13.0 %collective-permute-start.30 = (bf16[16,7168]{1,0:T(8,128)(2,1)S(1)}, bf16[16,7168]{1,0:T(8,128)(2,1)S(1)}, u32[]{:S(2)}, u32[]{:S(2)}) collective-permute-start(bf16[16,7168]{1,0:T(8,128)(2,1)S(1)} %get-tuple-element.66), channel_id=1, source_target_pairs={{0,28},{1,21},{2,30},{3,23},{4,16},{5,25},{6,18},{7,27},{8,20},{9,... | collective-permute-start | bytes 688136 | tf_op jit(solution)/shard_map/ppermute | solution.py:40
  134.4 14.9 %collective-permute-start.31 = (bf16[16,7168]{1,0:T(8,128)(2,1)S(1)}, bf16[16,7168]{1,0:T(8,128)(2,1)S(1)}, u32[]{:S(2)}, u32[]{:S(2)}) collective-permute-start(bf16[16,7168]{1,0:T(8,128)(2,1)S(1)} %get-tuple-element.67), channel_id=1, source_target_pairs={{0,20},{1,29},{2,22},{3,31},{4,24},{5,17},{6,26},{7,19},{8,28},{9,... | collective-permute-start | bytes 688136 | tf_op jit(solution)/shard_map/ppermute | solution.py:40
  136.8 14.1 %collective-permute-start.34 = (bf16[16,7168]{1,0:T(8,128)(2,1)S(1)}, bf16[16,7168]{1,0:T(8,128)(2,1)S(1)}, u32[]{:S(2)}, u32[]{:S(2)}) collective-permute-start(bf16[16,7168]{1,0:T(8,128)(2,1)S(1)} %join_near.3), channel_id=1, source_target_pairs={{0,16},{1,17},{2,18},{3,19},{4,20},{5,21},{6,22},{7,23},{8,24},{9,... | collective-permute-start | bytes 688136 | tf_op jit(solution)/shard_map/ppermute | solution.py:40
  (5 other events, 61.1 us)
